TPU v7x, 256 devices: a whole 4x4x8 slice. The times are simulated.
256 devices in a mesh: wide: 16 (over z, x_hi), narrow: 16 (over x_lo, y, core).
Axes of the slice: x: 4 (x_hi: 2, x_lo: 2; x = x_hi * 2 + x_lo), y: 4, z: 8, core: 2. Of those that a mesh axis runs over, the one named last changes fastest.
Arguments:
- activations: bfloat16 [1536, 4096], P('narrow', 'wide'), may hold values from -6 to 6
- grad_outputs: bfloat16 [1536, 14336], P('wide', 'narrow'), may hold values from -0.75 to 0.75
- act_basis: bfloat16 [4096, 4096], P('wide', 'narrow'), may hold values from -0.09375 to 0.09375
- grad_basis: bfloat16 [14336, 14336], P('narrow', 'wide'), may hold values from -0.046875 to 0.046875
Outputs:
- eigenvalues: float32 [4096, 14336], P('narrow', 'wide')
All inputs are finite; a program needn't handle non-finite values.
Results may differ from a plain program's by a relative error of at most 0.0034.
Values may be sent and summed in bfloat16 or wider, within the bound.
No kernel may reach another device: no remote copies, remote signals or barrier semaphores. Data moves between devices by JAX's collectives and lax.ppermute only.
A program may use at most 64 MiB of HBM per device.

v0:
```python
import jax
import jax.numpy as jnp
from jax import lax
from jax.sharding import PartitionSpec as P

SEQS = 4


def per_device(activations, grad_outputs, act_basis, grad_basis):
    act_terms = jnp.dot(
        lax.all_gather(activations, "narrow", axis=0, tiled=True),
        act_basis,
        preferred_element_type=jnp.float32,
    )
    act_rot = lax.psum(act_terms, "wide").astype(jnp.bfloat16)
    grad_terms = jnp.dot(
        lax.all_gather(grad_outputs, "wide", axis=0, tiled=True),
        grad_basis,
        preferred_element_type=jnp.float32,
    )
    grad_rot = lax.psum(grad_terms, "narrow").astype(jnp.bfloat16)
    act_seqs = act_rot.reshape(SEQS, -1, act_rot.shape[1])
    grad_seqs = grad_rot.reshape(SEQS, -1, grad_rot.shape[1])
    coeffs = jnp.einsum("sli,slj->sij", act_seqs, grad_seqs, preferred_element_type=jnp.float32)
    return jnp.sum(coeffs * coeffs, axis=0) / SEQS


def solution(mesh):
    return jax.shard_map(
        per_device,
        mesh=mesh,
        in_specs=(
            P("narrow", "wide"),
            P("wide", "narrow"),
            P("wide", "narrow"),
            P("narrow", "wide"),
        ),
        out_specs=P("narrow", "wide"),
        check_vma=False,
    )
```

profile of v0, /device:TPU:0, one launch (start us, length us, event | category | flops | bytes accessed | tf_op | source)
XLA Modules:
  0.0 242.2 jit_solution(7635053997404210031)
XLA Ops:
  6.5 0.0 copy-start
  6.5 0.0 all-gather.2.cloned.1.call-start
  6.5 0.7 all-gather.2.cloned.1.call-update
  7.3 20.5 %all_gather.6 = bf16[1536,256]{1,0:T(8,128)(2,1)S(1)} all-gather(bf16[96,256]{1,0:T(8,128)(2,1)} %param.4), channel_id=1, replica_groups=mesh['wide'=16,'narrow'=16] {'narrow'}, dimensions={0}, use_global_device_ids=true | all-gather | bytes 835584 | tf_op jit(solution)/shard_map/all_gather | solution.py:11
  27.8 1.3 fusion
  29.0 112.2 %all-reduce.3 = bf16[1536,256]{1,0:T(8,128)(2,1)} all-reduce(f32[1536,256]{1,0:T(8,128)S(1)} %fusion), channel_id=1, replica_groups=mesh['wide'=16,'narrow'=16] {'wide'}, use_global_device_ids=true, to_apply=%region_0.0 | all-reduce | flops 393216 | bytes 2359296 | tf_op jit(solution)/shard_map/psum | solution.py:15
  141.3 0.0 all-gather.2.cloned.1.call-done
  141.3 0.0 copy-done
  141.3 6.9 %fusion.1 = f32[1536,896]{1,0:T(8,128)} fusion(bf16[1536,896]{1,0:T(8,128)(2,1)} %all-gather.2.cloned.1.call-done, bf16[896,896]{1,0:T(8,128)(2,1)S(1)} %copy-done), kind=kOutput, calls=%fused_computation.3 | convolution fusion | flops 2466250752 | bytes 9863168 | tf_op jit(solution)/shard_map/dot_general | solution.py:16
  148.2 0.0 copy-start.1
  148.2 83.1 %all-reduce.2 = bf16[1536,896]{1,0:T(8,128)(2,1)} all-reduce(f32[1536,896]{1,0:T(8,128)} %fusion.1), channel_id=1, replica_groups=mesh['wide'=16,'narrow'=16] {'narrow'}, use_global_device_ids=true, to_apply=%region_1.0 | all-reduce | flops 1376256 | bytes 8257536 | tf_op jit(solution)/shard_map/psum | solution.py:21
  231.3 0.0 copy-done.1
  231.3 3.1 %multiply_reduce_fusion = f32[256,896]{1,0:T(8,128)S(1)} fusion(bf16[4,384,256]{2,1,0:T(8,128)(2,1)S(1)} %bitcast.9, bf16[4,384,896]{2,1,0:T(8,128)(2,1)} %bitcast.8), kind=kOutput, calls=%fused_computation | convolution fusion | flops 706248704 | bytes 4456448 | tf_op jit(solution)/shard_map/sli,slj->sij/dot_general | solution.py:24
  234.4 1.0 broadcast_multiply_fusion
Async XLA Ops:
  6.5 134.7 %copy-start = (bf16[896,896]{1,0:T(8,128)(2,1)S(1)}, bf16[896,896]{1,0:T(8,128)(2,1)}, u32[]{:S(2)}) copy-start(bf16[896,896]{1,0:T(8,128)(2,1)} %param.7) | copy-start | bytes 4816900
  6.5 134.7 %all-gather.2.cloned.1.call-start = ((), (), s32[]{:S(2)}) async-start(), calls=%async_computation | async-start | bytes 2924544 | tf_op jit(solution)/shard_map/all_gather | solution.py:17
  148.2 83.1 %copy-start.1 = (bf16[1536,256]{1,0:T(8,128)(2,1)S(1)}, bf16[1536,256]{1,0:T(8,128)(2,1)}, u32[]{:S(2)}) copy-start(bf16[1536,256]{1,0:T(8,128)(2,1)} %all-reduce.3) | copy-start | bytes 2359300
Sparse Core Ops, SparseCore 0:
  9.9 113.3 all-gather.1
where the time goes:
time: 242 us
  blocking collectives  216 us (89%)
  between operations  13.4 us (6%)
  matrix products  11.3 us (5%)
    psum x1, blocking collectives, per_device(): act_rot = lax.psum(act_terms, 'wide').astype(jnp.bfloat16)  112 us
    psum x1, blocking collectives, per_device(): grad_rot = lax.psum(grad_terms, 'narrow').astype(jnp.bfloat16)  83.1 us
    all_gather x1, blocking collectives, per_device(): lax.all_gather(activations, 'narrow', axis=0, tiled=True)  20.5 us
    dot_general x1, matrix products, per_device(): jnp.dot(lax.all_gather(grad_outputs, 'wide', axis=0, tiled=True), grad_ba...  6.94 us
  transfers between devices with their start and end apart: 1, of which 0 were waited for; matrix products, arithmetic and copies ran while one was open for 1% of the time, Pallas kernels for 0%

commit v1 on v0

v1 whole, which is shorter than its diff:
```python
import jax
import jax.numpy as jnp
from jax import lax
from jax.experimental import pallas as pl
from jax.experimental.pallas import tpu as pltpu
from jax.sharding import Mesh, PartitionSpec as P

SEQS = 4
NZ = 8
CHIPS = ("xl", "y")


def shift(x, axis, by, size):
    return lax.ppermute(x, axis, [(i, (i + by) % size) for i in range(size)])


def swap(x, axis):
    return lax.ppermute(x, axis, [(0, 1), (1, 0)])


def dot(x, y):
    return jnp.dot(x, y, preferred_element_type=jnp.float32)


def spread(x, axis, size):
    copies = jnp.broadcast_to(x[None], (size,) + x.shape).reshape((size * x.shape[0],) + x.shape[1:])
    return lax.all_to_all(copies, axis, 0, 0, tiled=True)


def ring(block, half):
    out = [None] * NZ
    out[0] = up = down = block
    for step in range(1, NZ // 2):
        up = shift(up, "z", 1, NZ)
        down = shift(down, "z", -1, NZ)
        out[NZ - step], out[step] = up, down
    last = (shift(up[:, :half], "z", 1, NZ), shift(down[:, half:], "z", -1, NZ))
    out[NZ // 2] = jnp.concatenate(last, axis=1)
    return out


def coeffs_kernel(where, act, mine, other, out):
    z, d = where[0], where[1]
    total = None
    for seq in range(SEQS):
        left, right = [], []
        for block in (2 * seq, 2 * seq + 1):
            rel = lax.rem(block - z + NZ, NZ)
            left += [act[rel, d, d], act[rel, d, 1 - d], act[rel, 1 - d, d], act[rel, 1 - d, 1 - d]]
            right += [mine[rel], other[rel]]
        coeffs = lax.dot_general(
            jnp.concatenate(left, axis=0),
            jnp.concatenate(right, axis=0),
            (((0,), (0,)), ((), ())),
            preferred_element_type=jnp.float32,
        )
        square = coeffs * coeffs
        total = square if total is None else total + square
    out[...] = total * (1.0 / SEQS)


def per_device(activations, grad_outputs, act_basis, grad_basis):
    z, xh, c = lax.axis_index("z"), lax.axis_index("xh"), lax.axis_index("c")
    rows, half = grad_outputs.shape[0], grad_outputs.shape[0] // 2

    basis = jnp.concatenate([grad_basis, swap(grad_basis, "c")], axis=0)
    both = jnp.concatenate([grad_outputs, swap(grad_outputs, "c")], axis=1)
    block = lax.dynamic_slice(both, (c * half, 0), (half, both.shape[1]))
    mine = ring(block, grad_outputs.shape[1])
    theirs = ring(swap(block, "xh"), grad_outputs.shape[1])

    act_basis2 = jnp.concatenate([act_basis, swap(act_basis, "xh")], axis=0)
    act_both = jnp.concatenate([activations, swap(activations, "xh")], axis=1)
    act_block = lax.dynamic_slice(act_both, (xh * half, 0), (half, act_both.shape[1]))
    act_own = spread(act_block, CHIPS, 8)
    act_oth = swap(act_own, "c")
    act_rows = jnp.stack([act_own.reshape(8, half, -1), act_oth.reshape(8, half, -1)], axis=1)
    act_terms = dot(act_rows.reshape(8 * rows, -1), act_basis2)
    act_sum = lax.psum_scatter(act_terms, "z", scatter_dimension=0, tiled=True).astype(jnp.bfloat16)
    act_pair = jnp.concatenate([act_sum, swap(act_sum, "xh")], axis=0)
    act_all = jnp.stack(ring(act_pair, 128)).reshape(NZ, 2, 2, half, -1)

    terms = [None] * NZ
    for first, second in ((7, 1), (6, 2), (5, 3), (0, 4)):
        x = jnp.concatenate([mine[first], theirs[first], mine[second], theirs[second]], axis=0)
        term = dot(x, basis).astype(jnp.bfloat16)
        terms[first], terms[second] = term[:rows], term[rows:]
    parts = lax.all_to_all(jnp.concatenate(terms, axis=0), CHIPS, 0, 0, tiled=True)
    grad_sum = jnp.sum(parts.reshape(8, rows, -1).astype(jnp.float32), axis=0).astype(jnp.bfloat16)
    grad_own = spread(grad_sum, CHIPS, 8)
    grad_oth = swap(grad_own, "c")

    where = jnp.stack([z, jnp.bitwise_xor(xh, c)]).astype(jnp.int32)
    width = grad_outputs.shape[1]
    return pl.pallas_call(
        coeffs_kernel,
        out_shape=jax.ShapeDtypeStruct((act_basis.shape[1], width), jnp.float32),
        in_specs=[pl.BlockSpec(memory_space=pltpu.SMEM)] + [pl.BlockSpec(memory_space=pltpu.VMEM)] * 3,
        out_specs=pl.BlockSpec(memory_space=pltpu.VMEM),
        compiler_params=pltpu.CompilerParams(vmem_limit_bytes=48 * 1024 * 1024),
        cost_estimate=pl.CostEstimate(flops=703 * 10**6, bytes_accessed=5 * 10**6, transcendentals=0),
    )(where, act_all, grad_own.reshape(NZ, rows, width), grad_oth.reshape(NZ, rows, width))


def solution(mesh):
    fine = Mesh(mesh.devices.reshape(8, 2, 2, 4, 2), ("z", "xh", "xl", "y", "c"))
    wide, narrow = ("z", "xh"), ("xl", "y", "c")
    return jax.shard_map(
        per_device,
        mesh=fine,
        in_specs=(P(narrow, wide), P(wide, narrow), P(wide, narrow), P(narrow, wide)),
        out_specs=P(narrow, wide),
        check_vma=False,
    )
```

time: 242 us -> 172 us (0.71)
  the two profiles are of different devices: /device:TPU:0 before, /device:TPU:4 now
where the time goes in v1:
time: 172 us
  starting transfers between devices  59.8 us (35%)
  waiting for transfers between devices  55.6 us (32%)
  blocking collectives  19.5 us (11%)
  between operations  13.7 us (8%)
  local copies, waits for them, and re-layouts  10.6 us (6%)
  matrix products  7.93 us (5%)
  Pallas kernels  2.72 us (2%)
  other arithmetic  2.18 us (1%)
    ppermute x24, starting transfers between devices, shift(): return lax.ppermute(x, axis, [(i, (i + by) % size) for i in range(size)])  43.2 us
    ppermute x8, waiting for transfers between devices, swap(): return lax.ppermute(x, axis, [(0, 1), (1, 0)])  20.1 us
    ppermute x24, waiting for transfers between devices, shift(): return lax.ppermute(x, axis, [(i, (i + by) % size) for i in range(size)])  19.9 us
    all_to_all x1, blocking collectives, spread(): return lax.all_to_all(copies, axis, 0, 0, tiled=True)  19.5 us
    reduce_scatter x1, waiting for transfers between devices, per_device(): lax.psum_scatter(act_terms, 'z', scatter_dimension=0, tiled=True)  15.5 us
    dot_general x5, matrix products, dot(): return jnp.dot(x, y, preferred_element_type=jnp.float32)  7.93 us
    unnamed x25, local copies, waits for them, and re-layouts  7.64 us
    all_to_all x1, starting transfers between devices, per_device(): lax.all_to_all(jnp.concatenate(terms, axis=0), CHIPS, 0, 0, tiled=True)  5.83 us
  transfers between devices with their start and end apart: 35, of which 17 were waited for; matrix products, arithmetic and copies ran while one was open for 12% of the time, Pallas kernels for 0%

profile of v1, /device:TPU:4, one launch (start us, length us, event | category | flops | bytes accessed | tf_op | source)
XLA Modules:
  0.0 171.9 jit_solution(11862239678056734713)
XLA Ops:
  7.0 3.4 %collective-permute-done.12 = bf16[96,896]{1,0:T(8,128)(2,1)S(1)} collective-permute-done((bf16[96,896]{1,0:T(8,128)(2,1)}, bf16[96,896]{1,0:T(8,128)(2,1)S(1)}, u32[]{:S(2)}, u32[]{:S(2)}) %collective-permute-start.12) | collective-permute-done | bytes 172064 | tf_op jit(solution)/shard_map/ppermute | solution.py:18
  15.0 5.9 %collective-permute-start.18 = (bf16[48,1792]{1,0:T(8,128)(2,1)S(1)}, bf16[48,1792]{1,0:T(8,128)(2,1)S(1)}, u32[]{:S(2)}, u32[]{:S(2)}) collective-permute-start(bf16[48,1792]{1,0:T(8,128)(2,1)S(1)} %fusion.36), channel_id=1, source_target_pairs={{0,224},{32,0},{64,32},{96,64},{128,96},{160,128},{192,160},{224,1... | collective-permute-start | bytes 516104 | tf_op jit(solution)/shard_map/ppermute | solution.py:14
  20.9 4.9 %collective-permute-start.26 = (bf16[48,1792]{1,0:T(8,128)(2,1)S(1)}, bf16[48,1792]{1,0:T(8,128)(2,1)S(1)}, u32[]{:S(2)}, u32[]{:S(2)}) collective-permute-start(bf16[48,1792]{1,0:T(8,128)(2,1)S(1)} %collective-permute-done.13), channel_id=1, source_target_pairs={{0,224},{32,0},{64,32},{96,64},{128,96},{160,128},{192,160},{224,1... | collective-permute-start | bytes 516104 | tf_op jit(solution)/shard_map/ppermute | solution.py:14
  25.8 3.2 %collective-permute-start.19 = (bf16[48,1792]{1,0:T(8,128)(2,1)S(1)}, bf16[48,1792]{1,0:T(8,128)(2,1)}, u32[]{:S(2)}, u32[]{:S(2)}) collective-permute-start(bf16[48,1792]{1,0:T(8,128)(2,1)S(1)} %collective-permute-done.18), channel_id=1, source_target_pairs={{0,224},{32,0},{64,32},{96,64},{128,96},{160,128},{192,160},{224,1... | collective-permute-start | bytes 516104 | tf_op jit(solution)/shard_map/ppermute | solution.py:14
  30.1 3.7 %collective-permute-start.27 = (bf16[48,1792]{1,0:T(8,128)(2,1)S(1)}, bf16[48,1792]{1,0:T(8,128)(2,1)}, u32[]{:S(2)}, u32[]{:S(2)}) collective-permute-start(bf16[48,1792]{1,0:T(8,128)(2,1)S(1)} %collective-permute-done.26), channel_id=1, source_target_pairs={{0,224},{32,0},{64,32},{96,64},{128,96},{160,128},{192,160},{224,1... | collective-permute-start | bytes 516104 | tf_op jit(solution)/shard_map/ppermute | solution.py:14
  34.0 3.6 %collective-permute-start.20 = (bf16[48,1792]{1,0:T(8,128)(2,1)}, bf16[48,1792]{1,0:T(8,128)(2,1)S(1)}, u32[]{:S(2)}, u32[]{:S(2)}) collective-permute-start(bf16[48,1792]{1,0:T(8,128)(2,1)} %collective-permute-done.19), channel_id=1, source_target_pairs={{0,224},{32,0},{64,32},{96,64},{128,96},{160,128},{192,160},{224,1... | collective-permute-start | bytes 516104 | tf_op jit(solution)/shard_map/ppermute | solution.py:14
  38.3 3.8 %collective-permute-start.28 = (bf16[48,1792]{1,0:T(8,128)(2,1)}, bf16[48,1792]{1,0:T(8,128)(2,1)S(1)}, u32[]{:S(2)}, u32[]{:S(2)}) collective-permute-start(bf16[48,1792]{1,0:T(8,128)(2,1)} %collective-permute-done.27), channel_id=1, source_target_pairs={{0,224},{32,0},{64,32},{96,64},{128,96},{160,128},{192,160},{224,1... | collective-permute-start | bytes 516104 | tf_op jit(solution)/shard_map/ppermute | solution.py:14
  42.6 2.7 %constant_dynamic-update-slice_fusion.9 = bf16[1792,896]{1,0:T(8,128)(2,1)} fusion(bf16[896,896]{1,0:T(8,128)(2,1)} %param.7), kind=kLoop, calls=%fused_computation.66 | loop fusion | bytes 3211264
  46.1 5.1 %all-to-all-start = ((bf16[8,48,512]{2,1,0:T(8,128)(2,1)}), bf16[8,48,512]{2,1,0:T(8,128)(2,1)S(1)}, u32[]{:S(2)}, u32[]{:S(2)}) async-start(bf16[8,48,512]{2,1,0:T(8,128)(2,1)} %broadcast_in_dim.4), calls=%async_computation | async-start | bytes 786432 | tf_op jit(solution)/shard_map/all_to_all | solution.py:27
  51.2 3.5 %collective-permute-start.21 = (bf16[48,896]{1,0:T(8,128)(2,1)S(1)}, bf16[48,896]{1,0:T(8,128)(2,1)S(1)}, u32[]{:S(2)}, u32[]{:S(2)}) collective-permute-start(bf16[48,896]{1,0:T(8,128)(2,1)S(1)} %slice.59), channel_id=1, source_target_pairs={{0,224},{32,0},{64,32},{96,64},{128,96},{160,128},{192,160},{224,1... | collective-permute-start | bytes 258056 | tf_op jit(solution)/shard_map/ppermute | solution.py:14
  54.9 3.3 %collective-permute-start.29 = (bf16[48,896]{1,0:T(8,128)(2,1)S(1)}, bf16[48,896]{1,0:T(8,128)(2,1)S(1)}, u32[]{:S(2)}, u32[]{:S(2)}) collective-permute-start(bf16[48,896]{1,0:T(8,128)(2,1)S(1)} %slice.61), channel_id=1, source_target_pairs={{0,224},{32,0},{64,32},{96,64},{128,96},{160,128},{192,160},{224,1... | collective-permute-start | bytes 258056 | tf_op jit(solution)/shard_map/ppermute | solution.py:14
  60.5 3.4 %collective-permute-done.25 = bf16[48,896]{1,0:T(8,128)(2,1)S(1)} collective-permute-done((bf16[48,896]{1,0:T(8,128)(2,1)S(1)}, bf16[48,896]{1,0:T(8,128)(2,1)S(1)}, u32[]{:S(2)}, u32[]{:S(2)}) %collective-permute-start.25) | collective-permute-done | bytes 86048 | tf_op jit(solution)/shard_map/ppermute | solution.py:14
  63.9 2.8 %convolution_convert_fusion.3 = bf16[192,896]{1,0:T(8,128)(2,1)S(1)} fusion(bf16[1792,896]{1,0:T(8,128)(2,1)} %constant_dynamic-update-slice_fusion.8, bf16[48,896]{1,0:T(8,128)(2,1)S(1)} %collective-permute-done.29, bf16[48,896]{1,0:T(8,128)(2,1)S(1)} %collective-permute-done.25, bf16[48,896]{1,0:T(8,128)(2,1)S(1)} %collective-permute-done.21, ...), kind=kOutput, calls=%fused_computation.3 | convolution fusion | flops 620863488 | bytes 4243456 | tf_op jit(solution)/shard_map/dot_general | solution.py:22
  76.2 5.8 %all-to-all-start.1 = ((bf16[8,96,896]{2,1,0:T(8,128)(2,1)}), bf16[8,96,896]{2,1,0:T(8,128)(2,1)S(1)}, u32[]{:S(2)}, u32[]{:S(2)}) async-start(bf16[8,96,896]{2,1,0:T(8,128)(2,1)} %bitcast.14), calls=%async_computation.2 | async-start | bytes 2752512 | tf_op jit(solution)/shard_map/all_to_all | solution.py:88
  83.9 10.9 %collective-permute-done.2 = bf16[256,256]{1,0:T(8,128)(2,1)S(1)} collective-permute-done((bf16[256,256]{1,0:T(8,128)(2,1)S(1)}, bf16[256,256]{1,0:T(8,128)(2,1)S(1)}, u32[]{:S(2)}, u32[]{:S(2)}) %collective-permute-start.2) | collective-permute-done | bytes 131104 | tf_op jit(solution)/shard_map/ppermute | solution.py:18
  96.4 19.5 %all_to_all.27.mine = bf16[8,96,896]{2,1,0:T(8,128)(2,1)S(1)} all-to-all(bf16[8,96,896]{2,1,0:T(8,128)(2,1)S(1)} %broadcast_in_dim.5), channel_id=1, replica_groups=mesh['z'=8,'xh'=2,'xl'=2,'y'=4,'c'=2] {'xl','y'}, dimensions={0} | all-to-all | bytes 2752512 | tf_op jit(solution)/shard_map/all_to_all | solution.py:27
  115.9 15.5 %reduce-scatter.2.cloned.1.call-done = f32[96,256]{1,0:T(8,128)} async-done(((f32[768,256]{1,0:T(8,128)}), f32[96,256]{1,0:T(8,128)}) %reduce-scatter.2.cloned.1.call-update) | async-done | bytes 98320 | tf_op jit(solution)/shard_map/reduce_scatter | solution.py:79
  132.9 5.0 %collective-permute-done.3 = bf16[96,256]{1,0:T(8,128)(2,1)S(1)} collective-permute-done((bf16[96,256]{1,0:T(8,128)(2,1)S(1)}, bf16[96,256]{1,0:T(8,128)(2,1)S(1)}, u32[]{:S(2)}, u32[]{:S(2)}) %collective-permute-start.3) | collective-permute-done | bytes 49184 | tf_op jit(solution)/shard_map/ppermute | solution.py:18
  140.0 2.8 %collective-permute-done.4 = bf16[192,256]{1,0:T(8,128)(2,1)S(1)} collective-permute-done((bf16[192,256]{1,0:T(8,128)(2,1)S(1)}, bf16[192,256]{1,0:T(8,128)(2,1)S(1)}, u32[]{:S(2)}, u32[]{:S(2)}) %collective-permute-start.4) | collective-permute-done | bytes 98336 | tf_op jit(solution)/shard_map/ppermute | solution.py:14
  145.2 2.7 %collective-permute-done.5 = bf16[192,256]{1,0:T(8,128)(2,1)S(1)} collective-permute-done((bf16[192,256]{1,0:T(8,128)(2,1)S(1)}, bf16[192,256]{1,0:T(8,128)(2,1)S(1)}, u32[]{:S(2)}, u32[]{:S(2)}) %collective-permute-start.5) | collective-permute-done | bytes 98336 | tf_op jit(solution)/shard_map/ppermute | solution.py:14
  148.0 3.1 %collective-permute-start.6 = (bf16[192,256]{1,0:T(8,128)(2,1)S(1)}, bf16[192,256]{1,0:T(8,128)(2,1)S(1)}, u32[]{:S(2)}, u32[]{:S(2)}) collective-permute-start(bf16[192,256]{1,0:T(8,128)(2,1)S(1)} %collective-permute-done.5), channel_id=1, source_target_pairs={{0,224},{32,0},{64,32},{96,64},{128,96},{160,128},{192,160},{224,1... | collective-permute-start | bytes 294920 | tf_op jit(solution)/shard_map/ppermute | solution.py:14
  153.3 3.6 %collective-permute-start.11 = (bf16[192,128]{1,0:T(8,128)(2,1)S(1)}, bf16[192,128]{1,0:T(8,128)(2,1)S(1)}, u32[]{:S(2)}, u32[]{:S(2)}) collective-permute-start(bf16[192,128]{1,0:T(8,128)(2,1)S(1)} %slice.57), channel_id=1, source_target_pairs={{0,224},{32,0},{64,32},{96,64},{128,96},{160,128},{192,160},{224,1... | collective-permute-start | bytes 147464 | tf_op jit(solution)/shard_map/ppermute | solution.py:14
  158.6 3.6 %collective-permute-done.10 = bf16[192,128]{1,0:T(8,128)(2,1)S(1)} collective-permute-done((bf16[192,128]{1,0:T(8,128)(2,1)S(1)}, bf16[192,128]{1,0:T(8,128)(2,1)S(1)}, u32[]{:S(2)}, u32[]{:S(2)}) %collective-permute-start.10) | collective-permute-done | bytes 49184 | tf_op jit(solution)/shard_map/ppermute | solution.py:14
  162.3 2.7 %shard_map.46 = f32[256,896]{1,0:T(8,128)} custom-call(s32[2]{0:T(128)S(1)} %pad_add_fusion.where, bf16[8,2,2,48,256]{4,3,2,1,0:T(8,128)(2,1)S(1)} %constant_dynamic-update-slice_fusion.act, bf16[8,96,896]{2,1,0:T(8,128)(2,1)S(1)} %all_to_all.27.mine, bf16[8,96,896]{2,1,0:T(8,128)(2,1)S(1)} %bitcast.23), custom_call_target="tpu_custom_call" | custom-call | flops 703000000 | bytes 5000000 | tf_op jit(solution)/shard_map/pallas_call | solution.py:95
  (98 shorter events, 33.7 us)
Async XLA Ops:
  6.5 51.7 %collective-permute-start.30 = (bf16[896,896]{1,0:T(8,128)(2,1)}, bf16[896,896]{1,0:T(8,128)(2,1)S(1)}, u32[]{:S(2)}, u32[]{:S(2)}) collective-permute-start(bf16[896,896]{1,0:T(8,128)(2,1)} %param.7), channel_id=1, source_target_pairs={{0,1},{1,0},{2,3},{3,2},{4,5},{5,4},{6,7},{7,6},{8,9},{9,8},{10,11... | collective-permute-start | bytes 4816904 | tf_op jit(solution)/shard_map/ppermute | solution.py:18
  11.4 9.5 %collective-permute-start.13 = (bf16[48,1792]{1,0:T(8,128)(2,1)S(1)}, bf16[48,1792]{1,0:T(8,128)(2,1)S(1)}, u32[]{:S(2)}, u32[]{:S(2)}) collective-permute-start(bf16[48,1792]{1,0:T(8,128)(2,1)S(1)} %fusion.36), channel_id=1, source_target_pairs={{0,16},{16,0},{1,17},{17,1},{2,18},{18,2},{3,19},{19,3},{4,20},{20... | collective-permute-start | bytes 516104 | tf_op jit(solution)/shard_map/ppermute | solution.py:18
  13.7 12.1 %collective-permute-start = (bf16[96,256]{1,0:T(8,128)(2,1)}, bf16[96,256]{1,0:T(8,128)(2,1)S(1)}, u32[]{:S(2)}, u32[]{:S(2)}) collective-permute-start(bf16[96,256]{1,0:T(8,128)(2,1)} %param.4), channel_id=1, source_target_pairs={{0,16},{16,0},{1,17},{17,1},{2,18},{18,2},{3,19},{19,3},{4,20},{20... | collective-permute-start | bytes 147464 | tf_op jit(solution)/shard_map/ppermute | solution.py:18
  15.0 10.8 %collective-permute-start.18 = (bf16[48,1792]{1,0:T(8,128)(2,1)S(1)}, bf16[48,1792]{1,0:T(8,128)(2,1)S(1)}, u32[]{:S(2)}, u32[]{:S(2)}) collective-permute-start(bf16[48,1792]{1,0:T(8,128)(2,1)S(1)} %fusion.36), channel_id=1, source_target_pairs={{0,224},{32,0},{64,32},{96,64},{128,96},{160,128},{192,160},{224,1... | collective-permute-start | bytes 516104 | tf_op jit(solution)/shard_map/ppermute | solution.py:14
  20.9 8.2 %collective-permute-start.14 = (bf16[48,1792]{1,0:T(8,128)(2,1)S(1)}, bf16[48,1792]{1,0:T(8,128)(2,1)S(1)}, u32[]{:S(2)}, u32[]{:S(2)}) collective-permute-start(bf16[48,1792]{1,0:T(8,128)(2,1)S(1)} %fusion.36), channel_id=1, source_target_pairs={{0,32},{32,64},{64,96},{96,128},{128,160},{160,192},{192,224},{224... | collective-permute-start | bytes 516104 | tf_op jit(solution)/shard_map/ppermute | solution.py:14
  20.9 9.3 %collective-permute-start.26 = (bf16[48,1792]{1,0:T(8,128)(2,1)S(1)}, bf16[48,1792]{1,0:T(8,128)(2,1)S(1)}, u32[]{:S(2)}, u32[]{:S(2)}) collective-permute-start(bf16[48,1792]{1,0:T(8,128)(2,1)S(1)} %collective-permute-done.13), channel_id=1, source_target_pairs={{0,224},{32,0},{64,32},{96,64},{128,96},{160,128},{192,160},{224,1... | collective-permute-start | bytes 516104 | tf_op jit(solution)/shard_map/ppermute | solution.py:14
  25.8 8.3 %collective-permute-start.22 = (bf16[48,1792]{1,0:T(8,128)(2,1)S(1)}, bf16[48,1792]{1,0:T(8,128)(2,1)S(1)}, u32[]{:S(2)}, u32[]{:S(2)}) collective-permute-start(bf16[48,1792]{1,0:T(8,128)(2,1)S(1)} %collective-permute-done.13), channel_id=1, source_target_pairs={{0,32},{32,64},{64,96},{96,128},{128,160},{160,192},{192,224},{224... | collective-permute-start | bytes 516104 | tf_op jit(solution)/shard_map/ppermute | solution.py:14
  25.8 8.3 %collective-permute-start.19 = (bf16[48,1792]{1,0:T(8,128)(2,1)S(1)}, bf16[48,1792]{1,0:T(8,128)(2,1)}, u32[]{:S(2)}, u32[]{:S(2)}) collective-permute-start(bf16[48,1792]{1,0:T(8,128)(2,1)S(1)} %collective-permute-done.18), channel_id=1, source_target_pairs={{0,224},{32,0},{64,32},{96,64},{128,96},{160,128},{192,160},{224,1... | collective-permute-start | bytes 516104 | tf_op jit(solution)/shard_map/ppermute | solution.py:14
  29.0 8.8 %collective-permute-start.15 = (bf16[48,1792]{1,0:T(8,128)(2,1)S(1)}, bf16[48,1792]{1,0:T(8,128)(2,1)}, u32[]{:S(2)}, u32[]{:S(2)}) collective-permute-start(bf16[48,1792]{1,0:T(8,128)(2,1)S(1)} %collective-permute-done.14), channel_id=1, source_target_pairs={{0,32},{32,64},{64,96},{96,128},{128,160},{160,192},{192,224},{224... | collective-permute-start | bytes 516104 | tf_op jit(solution)/shard_map/ppermute | solution.py:14
  30.1 8.2 %collective-permute-start.27 = (bf16[48,1792]{1,0:T(8,128)(2,1)S(1)}, bf16[48,1792]{1,0:T(8,128)(2,1)}, u32[]{:S(2)}, u32[]{:S(2)}) collective-permute-start(bf16[48,1792]{1,0:T(8,128)(2,1)S(1)} %collective-permute-done.26), channel_id=1, source_target_pairs={{0,224},{32,0},{64,32},{96,64},{128,96},{160,128},{192,160},{224,1... | collective-permute-start | bytes 516104 | tf_op jit(solution)/shard_map/ppermute | solution.py:14
  34.0 8.6 %collective-permute-start.23 = (bf16[48,1792]{1,0:T(8,128)(2,1)S(1)}, bf16[48,1792]{1,0:T(8,128)(2,1)}, u32[]{:S(2)}, u32[]{:S(2)}) collective-permute-start(bf16[48,1792]{1,0:T(8,128)(2,1)S(1)} %collective-permute-done.22), channel_id=1, source_target_pairs={{0,32},{32,64},{64,96},{96,128},{128,160},{160,192},{192,224},{224... | collective-permute-start | bytes 516104 | tf_op jit(solution)/shard_map/ppermute | solution.py:14
  34.0 17.2 %collective-permute-start.20 = (bf16[48,1792]{1,0:T(8,128)(2,1)}, bf16[48,1792]{1,0:T(8,128)(2,1)S(1)}, u32[]{:S(2)}, u32[]{:S(2)}) collective-permute-start(bf16[48,1792]{1,0:T(8,128)(2,1)} %collective-permute-done.19), channel_id=1, source_target_pairs={{0,224},{32,0},{64,32},{96,64},{128,96},{160,128},{192,160},{224,1... | collective-permute-start | bytes 516104 | tf_op jit(solution)/shard_map/ppermute | solution.py:14
  37.8 16.9 %collective-permute-start.16 = (bf16[48,1792]{1,0:T(8,128)(2,1)}, bf16[48,1792]{1,0:T(8,128)(2,1)S(1)}, u32[]{:S(2)}, u32[]{:S(2)}) collective-permute-start(bf16[48,1792]{1,0:T(8,128)(2,1)} %collective-permute-done.15), channel_id=1, source_target_pairs={{0,32},{32,64},{64,96},{96,128},{128,160},{160,192},{192,224},{224... | collective-permute-start | bytes 516104 | tf_op jit(solution)/shard_map/ppermute | solution.py:14
  38.3 16.5 %collective-permute-start.28 = (bf16[48,1792]{1,0:T(8,128)(2,1)}, bf16[48,1792]{1,0:T(8,128)(2,1)S(1)}, u32[]{:S(2)}, u32[]{:S(2)}) collective-permute-start(bf16[48,1792]{1,0:T(8,128)(2,1)} %collective-permute-done.27), channel_id=1, source_target_pairs={{0,224},{32,0},{64,32},{96,64},{128,96},{160,128},{192,160},{224,1... | collective-permute-start | bytes 516104 | tf_op jit(solution)/shard_map/ppermute | solution.py:14
  42.6 15.6 %collective-permute-start.24 = (bf16[48,1792]{1,0:T(8,128)(2,1)}, bf16[48,1792]{1,0:T(8,128)(2,1)S(1)}, u32[]{:S(2)}, u32[]{:S(2)}) collective-permute-start(bf16[48,1792]{1,0:T(8,128)(2,1)} %collective-permute-done.23), channel_id=1, source_target_pairs={{0,32},{32,64},{64,96},{96,128},{128,160},{160,192},{192,224},{224... | collective-permute-start | bytes 516104 | tf_op jit(solution)/shard_map/ppermute | solution.py:14
  46.1 30.0 %all-to-all-start = ((bf16[8,48,512]{2,1,0:T(8,128)(2,1)}), bf16[8,48,512]{2,1,0:T(8,128)(2,1)S(1)}, u32[]{:S(2)}, u32[]{:S(2)}) async-start(bf16[8,48,512]{2,1,0:T(8,128)(2,1)} %broadcast_in_dim.4), calls=%async_computation | async-start | bytes 786432 | tf_op jit(solution)/shard_map/all_to_all | solution.py:27
  51.2 8.3 %collective-permute-start.21 = (bf16[48,896]{1,0:T(8,128)(2,1)S(1)}, bf16[48,896]{1,0:T(8,128)(2,1)S(1)}, u32[]{:S(2)}, u32[]{:S(2)}) collective-permute-start(bf16[48,896]{1,0:T(8,128)(2,1)S(1)} %slice.59), channel_id=1, source_target_pairs={{0,224},{32,0},{64,32},{96,64},{128,96},{160,128},{192,160},{224,1... | collective-permute-start | bytes 258056 | tf_op jit(solution)/shard_map/ppermute | solution.py:14
  76.2 19.9 %all-to-all-start.1 = ((bf16[8,96,896]{2,1,0:T(8,128)(2,1)}), bf16[8,96,896]{2,1,0:T(8,128)(2,1)S(1)}, u32[]{:S(2)}, u32[]{:S(2)}) async-start(bf16[8,96,896]{2,1,0:T(8,128)(2,1)} %bitcast.14), calls=%async_computation.2 | async-start | bytes 2752512 | tf_op jit(solution)/shard_map/all_to_all | solution.py:88
  82.0 49.4 %reduce-scatter.2.cloned.1.call-start = ((), (), s32[]{:S(2)}) async-start(), calls=%async_computation.4 | async-start | bytes 884736 | tf_op jit(solution)/shard_map/reduce_scatter | solution.py:79
  82.1 12.7 %collective-permute-start.2 = (bf16[256,256]{1,0:T(8,128)(2,1)S(1)}, bf16[256,256]{1,0:T(8,128)(2,1)S(1)}, u32[]{:S(2)}, u32[]{:S(2)}) collective-permute-start(bf16[256,256]{1,0:T(8,128)(2,1)S(1)} %copy-done.1), channel_id=1, source_target_pairs={{0,16},{16,0},{1,17},{17,1},{2,18},{18,2},{3,19},{19,3},{4,20},{20... | collective-permute-start | bytes 393224 | tf_op jit(solution)/shard_map/ppermute | solution.py:18
  115.9 46.4 %collective-permute-start.31 = (bf16[768,896]{1,0:T(8,128)(2,1)S(1)}, bf16[768,896]{1,0:T(8,128)(2,1)S(1)}, u32[]{:S(2)}, u32[]{:S(2)}) collective-permute-start(bf16[768,896]{1,0:T(8,128)(2,1)S(1)} %bitcast.22), channel_id=1, source_target_pairs={{0,1},{1,0},{2,3},{3,2},{4,5},{5,4},{6,7},{7,6},{8,9},{9,8},{10,11... | collective-permute-start | bytes 4128776 | tf_op jit(solution)/shard_map/ppermute | solution.py:18
  139.4 5.8 %collective-permute-start.7 = (bf16[192,256]{1,0:T(8,128)(2,1)S(1)}, bf16[192,256]{1,0:T(8,128)(2,1)S(1)}, u32[]{:S(2)}, u32[]{:S(2)}) collective-permute-start(bf16[192,256]{1,0:T(8,128)(2,1)S(1)} %pad_maximum_fusion.1), channel_id=1, source_target_pairs={{0,32},{32,64},{64,96},{96,128},{128,160},{160,192},{192,224},{224... | collective-permute-start | bytes 294920 | tf_op jit(solution)/shard_map/ppermute | solution.py:14
  145.2 5.8 %collective-permute-start.8 = (bf16[192,256]{1,0:T(8,128)(2,1)S(1)}, bf16[192,256]{1,0:T(8,128)(2,1)S(1)}, u32[]{:S(2)}, u32[]{:S(2)}) collective-permute-start(bf16[192,256]{1,0:T(8,128)(2,1)S(1)} %collective-permute-done.7), channel_id=1, source_target_pairs={{0,32},{32,64},{64,96},{96,128},{128,160},{160,192},{192,224},{224... | collective-permute-start | bytes 294920 | tf_op jit(solution)/shard_map/ppermute | solution.py:14
  151.0 5.8 %collective-permute-start.9 = (bf16[192,256]{1,0:T(8,128)(2,1)S(1)}, bf16[192,256]{1,0:T(8,128)(2,1)S(1)}, u32[]{:S(2)}, u32[]{:S(2)}) collective-permute-start(bf16[192,256]{1,0:T(8,128)(2,1)S(1)} %collective-permute-done.8), channel_id=1, source_target_pairs={{0,32},{32,64},{64,96},{96,128},{128,160},{160,192},{192,224},{224... | collective-permute-start | bytes 294920 | tf_op jit(solution)/shard_map/ppermute | solution.py:14
  (16 other events, 118.3 us)
Sparse Core Ops, SparseCore 0:
  96.2 35.1 reduce-scatter.1

commit v2 on v0

v2 whole, which is shorter than its diff:
```python
import jax
import jax.numpy as jnp
from jax import lax
from jax.experimental import pallas as pl
from jax.experimental.pallas import tpu as pltpu
from jax.sharding import Mesh, PartitionSpec as P

SEQS = 4
NZ = 8
CHIPS, NARROW, WIDE = ("xl", "y"), ("xl", "y", "c"), ("z", "xh")


def shift(x, axis, by, size):
    return lax.ppermute(x, axis, [(i, (i + by) % size) for i in range(size)])


def swap(x, axis):
    return lax.ppermute(x, axis, [(0, 1), (1, 0)])


def dot(x, y):
    return jnp.dot(x, y, preferred_element_type=jnp.float32)


VMEM = pl.BlockSpec(memory_space=pltpu.VMEM)
ANY = pl.BlockSpec(memory_space=pl.ANY)
SMEM = pl.BlockSpec(memory_space=pltpu.SMEM)


def call(body, out, ins, specs, after=(), flops=10**6, moved=10**6, **more):
    def kernel(*refs):
        body(*refs[: len(ins)], *refs[len(ins) + len(after) :])

    return pl.pallas_call(
        kernel,
        out_shape=out,
        in_specs=list(specs) + [ANY] * len(after),
        compiler_params=pltpu.CompilerParams(vmem_limit_bytes=16 * 1024 * 1024),
        cost_estimate=pl.CostEstimate(flops=flops, bytes_accessed=moved, transcendentals=0),
        **more,
    )(*ins, *after)


def gate(live, after=()):
    live = list(live)
    return call(
        lambda *refs: None,
        [jax.ShapeDtypeStruct(x.shape, x.dtype) for x in live],
        live,
        [VMEM] * len(live),
        after,
        out_specs=[VMEM] * len(live),
        input_output_aliases={k: k for k in range(len(live))},
    )


def hop(up, down):
    return shift(up, "z", 1, NZ), shift(down, "z", -1, NZ)


def lap(x):
    steps = [(z, c, (z + 1 - 2 * c) % NZ) for z in range(NZ) for c in (0, 1)]
    return lax.ppermute(x, ("z", "c"), [(2 * z + c, 2 * to + c) for z, c, to in steps])


def pick(where, pairs, after=()):
    def body(where, *refs):
        ins, outs = refs[: 2 * len(pairs)], refs[2 * len(pairs) :]
        for k, out in enumerate(outs):

            @pl.when(where[1] == 0)
            def _():
                out[...] = ins[2 * k][...]

            @pl.when(where[1] != 0)
            def _():
                out[...] = ins[2 * k + 1][...]

    out = [jax.ShapeDtypeStruct(x.shape, x.dtype) for x, _ in pairs]
    ins = [where] + [x for pair in pairs for x in pair]
    return call(body, out, ins, [SMEM] + [VMEM] * (len(ins) - 1), after, out_specs=[VMEM] * len(pairs))


def rotate(blocks, bases, done=(), after=()):
    rows, width = blocks[0][0].shape[0], bases[0].shape[1]
    before = sum(x.shape[0] for x in done)
    parts = [block[0] for block in blocks] + [block[1] for block in blocks]

    def body(*refs):
        refs, (first, second, *done, out) = refs[: len(parts)], refs[len(parts) :]
        left = jnp.concatenate([ref[...] for ref in refs[: len(blocks)]], axis=0)
        right = jnp.concatenate([ref[...] for ref in refs[len(blocks) :]], axis=0)
        out[before:] = (dot(left, first[...]) + dot(right, second[...])).astype(out.dtype)
        for x in done:
            out[:before] = x[...]

    out = jax.ShapeDtypeStruct((before + rows * len(blocks), width), jnp.bfloat16)
    flops = 4 * rows * len(blocks) * width * width
    ins = parts + list(bases) + list(done)
    return call(body, out, ins, [VMEM] * len(ins), after, flops, 6 * 10**6, out_specs=VMEM)


def summed(parts, count, copies, after=()):
    rows, width = parts.shape[0] // count, parts.shape[1]

    def body(x, out):
        total = x[:rows].astype(jnp.float32)
        for k in range(1, count):
            total = total + x[k * rows : (k + 1) * rows].astype(jnp.float32)
        total = total.astype(out.dtype)
        for k in range(copies):
            out[k * rows : (k + 1) * rows] = total

    out = jax.ShapeDtypeStruct((copies * rows, width), jnp.bfloat16)
    return call(body, out, [parts], [VMEM], after, out_specs=VMEM)


def rotate_act(own, other, bases, after=()):
    rows = own.shape[0] // 8
    depth, width = bases[0].shape

    def body(mine, theirs, first, second, out):
        for k, ref in enumerate((mine, theirs)):
            total = dot(ref[:, :depth], first[...]) + dot(ref[:, depth:], second[...])
            for chip in range(8):
                out[chip, k] = total[chip * rows : (chip + 1) * rows]

    out = jax.ShapeDtypeStruct((8, 2, rows, width), jnp.float32)
    return call(body, out, [own, other, *bases], [VMEM] * 4, after, 2 * 10**8, 2 * 10**6, out_specs=VMEM)


def act_halves(where, mine, theirs, after=()):
    half, depth = mine.shape[0] // 2, mine.shape[1]

    def body(where, mine, theirs, out):
        start = pl.multiple_of(where[0] * half, half)
        for k in range(8):
            out[k * half : (k + 1) * half, :depth] = mine[pl.ds(start, half)]
            out[k * half : (k + 1) * half, depth:] = theirs[pl.ds(start, half)]

    out = jax.ShapeDtypeStruct((8 * half, 2 * depth), mine.dtype)
    return call(body, out, [where, mine, theirs], [SMEM, VMEM, VMEM], after, out_specs=VMEM)


def spread(x, axis):
    return lax.all_to_all(x, axis, 0, 0, tiled=True)


def coeffs_kernel(where, *refs):
    sources, (out, grads, act, sems) = refs[:11], refs[11:]
    width = act.shape[-1] // 2
    copies = []
    for k, src in enumerate(sources[:7]):
        copies.append(pltpu.make_async_copy(src, act.at[k + (k >= 4)], sems.at[k]))
    for k, src in enumerate(sources[7:9]):
        copies.append(pltpu.make_async_copy(src, act.at[NZ // 2, :, :, :, pl.ds(k * width, width)], sems.at[7 + k]))
    for k, src in enumerate(sources[9:]):
        copies.append(pltpu.make_async_copy(src, grads.at[k], sems.at[9 + k]))
    for copy in copies:
        copy.start()
    for copy in copies:
        copy.wait()
    xh, c, z = where[0], where[1], where[2]
    total = None
    for seq in range(SEQS):
        left, right = [], []
        for block in (2 * seq, 2 * seq + 1):
            rel = lax.rem(block - z + NZ, NZ)
            for side in (0, 1):
                halved = lax.rem(rel, NZ // 2) == 0
                up = rel > NZ // 2
                core = jnp.where(halved, side, jnp.where(up, 0, 1))
                place = jnp.where(up, 2 * (NZ - rel) - 1 + side, 2 * rel - 1 + side)
                place = jnp.where(halved, 7 * (rel // (NZ // 2)), place)
                parity = jnp.bitwise_xor(jnp.bitwise_xor(xh, side), c)
                left += [act[rel, xh, parity], act[rel, 1 - xh, parity]]
                right.append(grads[jnp.bitwise_xor(core, c), place])
        coeffs = lax.dot_general(
            jnp.concatenate(left, axis=0),
            jnp.concatenate(right, axis=0),
            (((0,), (0,)), ((), ())),
            preferred_element_type=jnp.float32,
        )
        square = coeffs * coeffs
        total = square if total is None else total + square
    out[...] = total * (1.0 / SEQS)


def per_device(activations, grad_outputs, act_basis, grad_basis):
    z, xh, c = lax.axis_index("z"), lax.axis_index("xh"), lax.axis_index("c")
    where = jnp.stack([xh, c, z]).astype(jnp.int32)
    rows, half, width = grad_outputs.shape[0], grad_outputs.shape[0] // 2, grad_outputs.shape[1]
    cols = act_basis.shape[1]

    theirs = swap(grad_outputs, "xh")
    laps = [((grad_outputs, swap(grad_outputs, "c")), (theirs, swap(theirs, "c")))]
    for _ in range(3):
        laps.append(tuple(tuple(lap(x) for x in side) for side in laps[-1]))
    basis2 = swap(grad_basis, "c")

    act_x, act_basis2 = swap(activations, "xh"), swap(act_basis, "xh")
    act_copies = act_halves(where, activations, act_x, (laps[0][0][1],))
    (act_own,) = gate([spread(act_copies, CHIPS)], (*laps[2][0], act_basis2))
    act_oth = swap(act_own, "c")
    act_terms = rotate_act(act_own, act_oth, (act_basis, act_basis2))
    act_sum = lax.psum_scatter(act_terms.reshape(8 * rows, cols), "z", scatter_dimension=0, tiled=True)
    bases = grad_basis, basis2
    near = pick(where, list(zip(*laps[0])))
    early = rotate([near, laps[1][0], laps[1][1], laps[2][0], laps[2][1]], bases)
    far = [lap(x) for x in pick(where, list(zip(*laps[3])), (act_terms,))]
    terms = rotate([laps[3][0], laps[3][1], far], bases, (early,))

    parts = spread(terms, CHIPS)
    act_pair = summed(act_sum, 1, 1, (terms,))
    act_pair = jnp.concatenate([act_pair, swap(act_pair, "xh")], axis=0)
    one = hop(act_pair, act_pair)
    own = spread(summed(parts, 8, 8, one), CHIPS)
    two = hop(*one)
    three = hop(*two)
    four = hop(three[0][:, : cols // 2], three[1][:, cols // 2 :])
    (own,) = gate([own], four)
    other = swap(own, "c")

    acts = [x.reshape(2, 2, half, cols) for x in (act_pair, one[1], two[1], three[1], three[0], two[0], one[0])]
    acts += [x.reshape(2, 2, half, cols // 2) for x in four]
    return call(
        coeffs_kernel,
        jax.ShapeDtypeStruct((cols, width), jnp.float32),
        [where] + acts + [x.reshape(8, rows, width) for x in (own, other)],
        [SMEM] + [ANY] * 11,
        flops=703 * 10**6,
        moved=5 * 10**6,
        out_specs=VMEM,
        scratch_shapes=[
            pltpu.VMEM((2, 8, rows, width), jnp.bfloat16),
            pltpu.VMEM((NZ, 2, 2, half, cols), jnp.bfloat16),
            pltpu.SemaphoreType.DMA((11,)),
        ],
    )


def solution(mesh):
    fine = Mesh(mesh.devices.reshape(8, 2, 2, 4, 2), ("z", "xh", "xl", "y", "c"))
    return jax.shard_map(
        per_device,
        mesh=fine,
        in_specs=(P(NARROW, WIDE), P(WIDE, NARROW), P(WIDE, NARROW), P(NARROW, WIDE)),
        out_specs=P(NARROW, WIDE),
        check_vma=False,
    )
```

time: 242 us -> 144 us (0.60)
  the two profiles are of different devices: /device:TPU:0 before, /device:TPU:7 now
where the time goes in v2:
time: 144 us
  starting transfers between devices  72 us (50%)
  waiting for transfers between devices  39.6 us (28%)
  Pallas kernels  15.3 us (11%)
  between operations  13.6 us (9%)
  local copies, waits for them, and re-layouts  3.27 us (2%)
    ppermute x14, starting transfers between devices, lap(): lax.ppermute(x, ('z', 'c'), [(2 * z + c, 2 * to + c) for z, c, to in steps])  26.6 us
    ppermute x9, waiting for transfers between devices, swap(): return lax.ppermute(x, axis, [(0, 1), (1, 0)])  18.7 us
    ppermute x8, starting transfers between devices, shift(): return lax.ppermute(x, axis, [(i, (i + by) % size) for i in range(size)])  16.1 us
    all_to_all x3, starting transfers between devices, spread(): return lax.all_to_all(x, axis, 0, 0, tiled=True)  15.3 us
    pallas_call x11, Pallas kernels, call(): pl.pallas_call(kernel, out_shape=out, in_specs=list(specs) + [ANY] * len(...  15.3 us
    ppermute x9, starting transfers between devices, swap(): return lax.ppermute(x, axis, [(0, 1), (1, 0)])  14 us
    ppermute x8, waiting for transfers between devices, shift(): return lax.ppermute(x, axis, [(i, (i + by) % size) for i in range(size)])  8.79 us
    ppermute x14, waiting for transfers between devices, lap(): lax.ppermute(x, ('z', 'c'), [(2 * z + c, 2 * to + c) for z, c, to in steps])  8.19 us
  transfers between devices with their start and end apart: 35, of which 15 were waited for; matrix products, arithmetic and copies ran while one was open for 0% of the time, Pallas kernels for 7%

profile of v2, /device:TPU:7, one launch (start us, length us, event | category | flops | bytes accessed | tf_op | source)
XLA Modules:
  0.0 143.8 jit_solution(10731832206088833317)
XLA Ops:
  7.2 5.6 %collective-permute-start.2 = (bf16[96,896]{1,0:T(8,128)(2,1)}, bf16[96,896]{1,0:T(8,128)(2,1)S(1)}, u32[]{:S(2)}, u32[]{:S(2)}) collective-permute-start(bf16[96,896]{1,0:T(8,128)(2,1)} %refs_1_.3), channel_id=1, source_target_pairs={{0,32},{1,225},{32,64},{33,1},{64,96},{65,33},{96,128},{97,65},{12... | collective-permute-start | bytes 516104 | tf_op jit(solution)/shard_map/ppermute | solution.py:63
  14.0 2.3 %collective-permute-start.4 = (bf16[96,896]{1,0:T(8,128)(2,1)S(1)}, bf16[96,896]{1,0:T(8,128)(2,1)S(1)}, u32[]{:S(2)}, u32[]{:S(2)}) collective-permute-start(bf16[96,896]{1,0:T(8,128)(2,1)S(1)} %collective-permute-done.1.refs_3_), channel_id=1, source_target_pairs={{0,32},{1,225},{32,64},{33,1},{64,96},{65,33},{96,128},{97,65},{12... | collective-permute-start | bytes 516104 | tf_op jit(solution)/shard_map/ppermute | solution.py:63
  19.6 5.4 %all-to-all-start = ((bf16[8,48,512]{2,1,0:T(8,128)(2,1)}), bf16[8,48,512]{2,1,0:T(8,128)(2,1)S(1)}, u32[]{:S(2)}, u32[]{:S(2)}) async-start(bf16[8,48,512]{2,1,0:T(8,128)(2,1)} %bitcast.3), calls=%async_computation | async-start | bytes 786432 | tf_op jit(solution)/shard_map/all_to_all | solution.py:146
  29.5 2.3 %collective-permute-done.6.refs_3_ = bf16[256,256]{1,0:T(8,128)(2,1)S(1)} collective-permute-done((bf16[256,256]{1,0:T(8,128)(2,1)S(1)}, bf16[256,256]{1,0:T(8,128)(2,1)S(1)}, u32[]{:S(2)}, u32[]{:S(2)}) %collective-permute-start.6) | collective-permute-done | bytes 131104 | tf_op jit(solution)/shard_map/ppermute | solution.py:18
  31.9 3.6 %collective-permute-start.7 = (bf16[384,512]{1,0:T(8,128)(2,1)S(1)}, bf16[384,512]{1,0:T(8,128)(2,1)S(1)}, u32[]{:S(2)}, u32[]{:S(2)}) collective-permute-start(bf16[384,512]{1,0:T(8,128)(2,1)S(1)} %shard_map.47.refs_0_), channel_id=1, source_target_pairs={{0,1},{1,0},{2,3},{3,2},{4,5},{5,4},{6,7},{7,6},{8,9},{9,8},{10,11... | collective-permute-start | bytes 1179656 | tf_op jit(solution)/shard_map/ppermute | solution.py:18
  42.8 3.1 %collective-permute-start.11 = (bf16[96,896]{1,0:T(8,128)(2,1)}, bf16[96,896]{1,0:T(8,128)(2,1)S(1)}, u32[]{:S(2)}, u32[]{:S(2)}) collective-permute-start(bf16[96,896]{1,0:T(8,128)(2,1)} %collective-permute-done.10.refs_2_), channel_id=1, source_target_pairs={{0,32},{1,225},{32,64},{33,1},{64,96},{65,33},{96,128},{97,65},{12... | collective-permute-start | bytes 516104 | tf_op jit(solution)/shard_map/ppermute | solution.py:63
  48.5 3.0 %collective-permute-start.12 = (bf16[96,896]{1,0:T(8,128)(2,1)S(1)}, bf16[96,896]{1,0:T(8,128)(2,1)S(1)}, u32[]{:S(2)}, u32[]{:S(2)}) collective-permute-start(bf16[96,896]{1,0:T(8,128)(2,1)S(1)} %collective-permute-done.11.refs_4_), channel_id=1, source_target_pairs={{0,32},{1,225},{32,64},{33,1},{64,96},{65,33},{96,128},{97,65},{12... | collective-permute-start | bytes 516104 | tf_op jit(solution)/shard_map/ppermute | solution.py:63
  55.4 2.6 %collective-permute-done.12.refs_2_.refs_1_ = bf16[96,896]{1,0:T(8,128)(2,1)S(1)} collective-permute-done((bf16[96,896]{1,0:T(8,128)(2,1)S(1)}, bf16[96,896]{1,0:T(8,128)(2,1)S(1)}, u32[]{:S(2)}, u32[]{:S(2)}) %collective-permute-start.12) | collective-permute-done | bytes 172064 | tf_op jit(solution)/shard_map/ppermute | solution.py:63
  61.4 3.5 %collective-permute-start.18 = (bf16[96,896]{1,0:T(8,128)(2,1)S(1)}, bf16[96,896]{1,0:T(8,128)(2,1)S(1)}, u32[]{:S(2)}, u32[]{:S(2)}) collective-permute-start(bf16[96,896]{1,0:T(8,128)(2,1)S(1)} %get-tuple-element.9), channel_id=1, source_target_pairs={{0,32},{1,225},{32,64},{33,1},{64,96},{65,33},{96,128},{97,65},{12... | collective-permute-start | bytes 516104 | tf_op jit(solution)/shard_map/ppermute | solution.py:63
  67.1 3.1 %shard_map.51.refs_8_ = bf16[480,896]{1,0:T(8,128)(2,1)S(1)} custom-call(bf16[96,896]{1,0:T(8,128)(2,1)S(1)} %get-tuple-element.11.refs_0_, bf16[96,896]{1,0:T(8,128)(2,1)S(1)} %copy-done.4, bf16[96,896]{1,0:T(8,128)(2,1)} %collective-permute-done.10.refs_2_, bf16[96,896]{1,0:T(8,128)(2,1)S(1)} %collective-permute-done.3.refs_1_.refs_3_, ...), custom_call_target="tpu_custom_call" | custom-call | flops 1541406720 | bytes 6000000 | tf_op jit(solution)/shard_map/pallas_call | solution.py:34
  70.8 2.5 %shard_map.52.refs_1_ = bf16[768,896]{1,0:T(8,128)(2,1)} custom-call(bf16[96,896]{1,0:T(8,128)(2,1)S(1)} %collective-permute-done.8.refs_1_.refs_0_, bf16[96,896]{1,0:T(8,128)(2,1)S(1)} %collective-permute-done.12.refs_2_.refs_1_, bf16[96,896]{1,0:T(8,128)(2,1)S(1)} %collective-permute-done.18.refs_2_, bf16[96,896]{1,0:T(8,128)(2,1)S(1)} %collective-permute-done.13.refs_3_, ...), custom_call_target="tpu_custom_call" | custom-call | flops 924844032 | bytes 6000000 | tf_op jit(solution)/shard_map/pallas_call | solution.py:34
  73.3 4.7 %all-to-all-start.1 = ((bf16[8,96,896]{2,1,0:T(8,128)(2,1)}), bf16[8,96,896]{2,1,0:T(8,128)(2,1)S(1)}, u32[]{:S(2)}, u32[]{:S(2)}) async-start(bf16[8,96,896]{2,1,0:T(8,128)(2,1)} %bitcast.15), calls=%async_computation.2 | async-start | bytes 2752512 | tf_op jit(solution)/shard_map/all_to_all | solution.py:146
  78.9 2.9 %collective-permute-start.21 = (bf16[96,256]{1,0:T(8,128)(2,1)S(1)}, bf16[96,256]{1,0:T(8,128)(2,1)S(1)}, u32[]{:S(2)}, u32[]{:S(2)}) collective-permute-start(bf16[96,256]{1,0:T(8,128)(2,1)S(1)} %shard_map.53), channel_id=1, source_target_pairs={{0,16},{16,0},{1,17},{17,1},{2,18},{18,2},{3,19},{19,3},{4,20},{20... | collective-permute-start | bytes 147464 | tf_op jit(solution)/shard_map/ppermute | solution.py:18
  81.8 12.1 %collective-permute-done.21 = bf16[96,256]{1,0:T(8,128)(2,1)S(1)} collective-permute-done((bf16[96,256]{1,0:T(8,128)(2,1)S(1)}, bf16[96,256]{1,0:T(8,128)(2,1)S(1)}, u32[]{:S(2)}, u32[]{:S(2)}) %collective-permute-start.21) | collective-permute-done | bytes 49184 | tf_op jit(solution)/shard_map/ppermute | solution.py:18
  93.9 2.5 %collective-permute-start.25 = (bf16[192,256]{1,0:T(8,128)(2,1)S(1)}, bf16[192,256]{1,0:T(8,128)(2,1)S(1)}, u32[]{:S(2)}, u32[]{:S(2)}) collective-permute-start(bf16[192,256]{1,0:T(8,128)(2,1)S(1)} %pad_maximum_fusion), channel_id=1, source_target_pairs={{0,32},{32,64},{64,96},{96,128},{128,160},{160,192},{192,224},{224... | collective-permute-start | bytes 294920 | tf_op jit(solution)/shard_map/ppermute | solution.py:14
  96.4 5.5 %collective-permute-start.22 = (bf16[192,256]{1,0:T(8,128)(2,1)S(1)}, bf16[192,256]{1,0:T(8,128)(2,1)S(1)}, u32[]{:S(2)}, u32[]{:S(2)}) collective-permute-start(bf16[192,256]{1,0:T(8,128)(2,1)S(1)} %pad_maximum_fusion), channel_id=1, source_target_pairs={{0,224},{32,0},{64,32},{96,64},{128,96},{160,128},{192,160},{224,1... | collective-permute-start | bytes 294920 | tf_op jit(solution)/shard_map/ppermute | solution.py:14
  101.9 2.7 %collective-permute-done.25.refs_1_ = bf16[192,256]{1,0:T(8,128)(2,1)S(1)} collective-permute-done((bf16[192,256]{1,0:T(8,128)(2,1)S(1)}, bf16[192,256]{1,0:T(8,128)(2,1)S(1)}, u32[]{:S(2)}, u32[]{:S(2)}) %collective-permute-start.25) | collective-permute-done | bytes 98336 | tf_op jit(solution)/shard_map/ppermute | solution.py:14
  105.9 5.2 %all-to-all-start.2 = ((bf16[8,96,896]{2,1,0:T(8,128)(2,1)}), bf16[8,96,896]{2,1,0:T(8,128)(2,1)S(1)}, u32[]{:S(2)}, u32[]{:S(2)}) async-start(bf16[8,96,896]{2,1,0:T(8,128)(2,1)} %bitcast.17), calls=%async_computation.3 | async-start | bytes 2752512 | tf_op jit(solution)/shard_map/all_to_all | solution.py:146
  111.1 2.7 %collective-permute-start.23 = (bf16[192,256]{1,0:T(8,128)(2,1)S(1)}, bf16[192,256]{1,0:T(8,128)(2,1)S(1)}, u32[]{:S(2)}, u32[]{:S(2)}) collective-permute-start(bf16[192,256]{1,0:T(8,128)(2,1)S(1)} %collective-permute-done.22.refs_2_), channel_id=1, source_target_pairs={{0,224},{32,0},{64,32},{96,64},{128,96},{160,128},{192,160},{224,1... | collective-permute-start | bytes 294920 | tf_op jit(solution)/shard_map/ppermute | solution.py:14
  115.9 2.7 %collective-permute-start.24 = (bf16[192,256]{1,0:T(8,128)(2,1)S(1)}, bf16[192,256]{1,0:T(8,128)(2,1)S(1)}, u32[]{:S(2)}, u32[]{:S(2)}) collective-permute-start(bf16[192,256]{1,0:T(8,128)(2,1)S(1)} %collective-permute-done.23), channel_id=1, source_target_pairs={{0,224},{32,0},{64,32},{96,64},{128,96},{160,128},{192,160},{224,1... | collective-permute-start | bytes 294920 | tf_op jit(solution)/shard_map/ppermute | solution.py:14
  120.9 2.7 %collective-permute-start.29 = (bf16[192,128]{1,0:T(8,128)(2,1)S(1)}, bf16[192,128]{1,0:T(8,128)(2,1)S(1)}, u32[]{:S(2)}, u32[]{:S(2)}) collective-permute-start(bf16[192,128]{1,0:T(8,128)(2,1)S(1)} %slice.9), channel_id=1, source_target_pairs={{0,224},{32,0},{64,32},{96,64},{128,96},{160,128},{192,160},{224,1... | collective-permute-start | bytes 147464 | tf_op jit(solution)/shard_map/ppermute | solution.py:14
  125.3 3.9 %all-to-all-done.2 = bf16[8,96,896]{2,1,0:T(8,128)(2,1)S(1)} async-done(((bf16[8,96,896]{2,1,0:T(8,128)(2,1)}), bf16[8,96,896]{2,1,0:T(8,128)(2,1)S(1)}, u32[]{:S(2)}, u32[]{:S(2)}) %all-to-all-start.2) | async-done | bytes 1376288 | tf_op jit(solution)/shard_map/all_to_all | solution.py:146
  130.1 2.8 %collective-permute-done.30 = bf16[768,896]{1,0:T(8,128)(2,1)S(1)} collective-permute-done((bf16[768,896]{1,0:T(8,128)(2,1)S(1)}, bf16[768,896]{1,0:T(8,128)(2,1)S(1)}, u32[]{:S(2)}, u32[]{:S(2)}) %collective-permute-start.30) | collective-permute-done | bytes 1376288 | tf_op jit(solution)/shard_map/ppermute | solution.py:18
  132.8 4.1 %shard_map.56 = f32[256,896]{1,0:T(8,128)} custom-call(s32[3]{0:T(128)S(1)} %copy-done.14, bf16[2,2,48,256]{3,2,1,0:T(8,128)(2,1)S(1)} %bitcast.28, bf16[2,2,48,256]{3,2,1,0:T(8,128)(2,1)S(1)} %bitcast.27, bf16[2,2,48,256]{3,2,1,0:T(8,128)(2,1)S(1)} %bitcast.34, bf16[2,2,48,256]{3,2,1,0:T(8,128)(2,1)S(1)} %bitcast.30, bf16[2,2,48,256]{3,2,1,0:T(8,128)(2,1)S(1)} %bitcast.29, ...), custom_call_target="tpu_custom_call" | custom-call | flops 703000000 | bytes 5000000 | tf_op jit(solution)/shard_map/pallas_call | solution.py:34
  (92 shorter events, 38.6 us)
Async XLA Ops:
  6.5 60.5 %collective-permute-start.20 = (bf16[896,896]{1,0:T(8,128)(2,1)}, bf16[896,896]{1,0:T(8,128)(2,1)S(1)}, u32[]{:S(2)}, u32[]{:S(2)}) collective-permute-start(bf16[896,896]{1,0:T(8,128)(2,1)} %refs_6_.1), channel_id=1, source_target_pairs={{0,1},{1,0},{2,3},{3,2},{4,5},{5,4},{6,7},{7,6},{8,9},{9,8},{10,11... | collective-permute-start | bytes 4816904 | tf_op jit(solution)/shard_map/ppermute | solution.py:18
  7.2 6.8 %collective-permute-start.1 = (bf16[96,896]{1,0:T(8,128)(2,1)}, bf16[96,896]{1,0:T(8,128)(2,1)S(1)}, u32[]{:S(2)}, u32[]{:S(2)}) collective-permute-start(bf16[96,896]{1,0:T(8,128)(2,1)} %refs_1_.3), channel_id=1, source_target_pairs={{0,1},{1,0},{2,3},{3,2},{4,5},{5,4},{6,7},{7,6},{8,9},{9,8},{10,11... | collective-permute-start | bytes 516104 | tf_op jit(solution)/shard_map/ppermute | solution.py:18
  7.2 17.7 %collective-permute-start.2 = (bf16[96,896]{1,0:T(8,128)(2,1)}, bf16[96,896]{1,0:T(8,128)(2,1)S(1)}, u32[]{:S(2)}, u32[]{:S(2)}) collective-permute-start(bf16[96,896]{1,0:T(8,128)(2,1)} %refs_1_.3), channel_id=1, source_target_pairs={{0,32},{1,225},{32,64},{33,1},{64,96},{65,33},{96,128},{97,65},{12... | collective-permute-start | bytes 516104 | tf_op jit(solution)/shard_map/ppermute | solution.py:63
  14.0 12.3 %collective-permute-start.4 = (bf16[96,896]{1,0:T(8,128)(2,1)S(1)}, bf16[96,896]{1,0:T(8,128)(2,1)S(1)}, u32[]{:S(2)}, u32[]{:S(2)}) collective-permute-start(bf16[96,896]{1,0:T(8,128)(2,1)S(1)} %collective-permute-done.1.refs_3_), channel_id=1, source_target_pairs={{0,32},{1,225},{32,64},{33,1},{64,96},{65,33},{96,128},{97,65},{12... | collective-permute-start | bytes 516104 | tf_op jit(solution)/shard_map/ppermute | solution.py:63
  19.6 12.3 %all-to-all-start = ((bf16[8,48,512]{2,1,0:T(8,128)(2,1)}), bf16[8,48,512]{2,1,0:T(8,128)(2,1)S(1)}, u32[]{:S(2)}, u32[]{:S(2)}) async-start(bf16[8,48,512]{2,1,0:T(8,128)(2,1)} %bitcast.3), calls=%async_computation | async-start | bytes 786432 | tf_op jit(solution)/shard_map/all_to_all | solution.py:146
  25.0 53.0 %reduce-scatter.2.cloned.1.call-start = ((), (), s32[]{:S(2)}) async-start(), calls=%async_computation.4 | async-start | bytes 884736 | tf_op jit(solution)/shard_map/reduce_scatter | solution.py:206
  25.0 6.9 %collective-permute-start.3 = (bf16[96,896]{1,0:T(8,128)(2,1)S(1)}, bf16[96,896]{1,0:T(8,128)(2,1)S(1)}, u32[]{:S(2)}, u32[]{:S(2)}) collective-permute-start(bf16[96,896]{1,0:T(8,128)(2,1)S(1)} %collective-permute-done.2.refs_1_), channel_id=1, source_target_pairs={{0,32},{1,225},{32,64},{33,1},{64,96},{65,33},{96,128},{97,65},{12... | collective-permute-start | bytes 516104 | tf_op jit(solution)/shard_map/ppermute | solution.py:63
  26.4 5.5 %collective-permute-start.5 = (bf16[96,896]{1,0:T(8,128)(2,1)S(1)}, bf16[96,896]{1,0:T(8,128)(2,1)S(1)}, u32[]{:S(2)}, u32[]{:S(2)}) collective-permute-start(bf16[96,896]{1,0:T(8,128)(2,1)S(1)} %collective-permute-done.4.refs_6_), channel_id=1, source_target_pairs={{0,32},{1,225},{32,64},{33,1},{64,96},{65,33},{96,128},{97,65},{12... | collective-permute-start | bytes 516104 | tf_op jit(solution)/shard_map/ppermute | solution.py:63
  27.6 8.2 %collective-permute-start.9 = (bf16[96,896]{1,0:T(8,128)(2,1)S(1)}, bf16[96,896]{1,0:T(8,128)(2,1)}, u32[]{:S(2)}, u32[]{:S(2)}) collective-permute-start(bf16[96,896]{1,0:T(8,128)(2,1)S(1)} %copy-done.7), channel_id=1, source_target_pairs={{0,16},{16,0},{1,17},{17,1},{2,18},{18,2},{3,19},{19,3},{4,20},{20... | collective-permute-start | bytes 516104 | tf_op jit(solution)/shard_map/ppermute | solution.py:18
  31.9 9.6 %collective-permute-start.7 = (bf16[384,512]{1,0:T(8,128)(2,1)S(1)}, bf16[384,512]{1,0:T(8,128)(2,1)S(1)}, u32[]{:S(2)}, u32[]{:S(2)}) collective-permute-start(bf16[384,512]{1,0:T(8,128)(2,1)S(1)} %shard_map.47.refs_0_), channel_id=1, source_target_pairs={{0,1},{1,0},{2,3},{3,2},{4,5},{5,4},{6,7},{7,6},{8,9},{9,8},{10,11... | collective-permute-start | bytes 1179656 | tf_op jit(solution)/shard_map/ppermute | solution.py:18
  40.0 5.8 %collective-permute-start.15 = (bf16[96,896]{1,0:T(8,128)(2,1)}, bf16[96,896]{1,0:T(8,128)(2,1)}, u32[]{:S(2)}, u32[]{:S(2)}) collective-permute-start(bf16[96,896]{1,0:T(8,128)(2,1)} %collective-permute-done.14.refs_4_), channel_id=1, source_target_pairs={{0,32},{1,225},{32,64},{33,1},{64,96},{65,33},{96,128},{97,65},{12... | collective-permute-start | bytes 516104 | tf_op jit(solution)/shard_map/ppermute | solution.py:63
  42.8 5.7 %collective-permute-start.11 = (bf16[96,896]{1,0:T(8,128)(2,1)}, bf16[96,896]{1,0:T(8,128)(2,1)S(1)}, u32[]{:S(2)}, u32[]{:S(2)}) collective-permute-start(bf16[96,896]{1,0:T(8,128)(2,1)} %collective-permute-done.10.refs_2_), channel_id=1, source_target_pairs={{0,32},{1,225},{32,64},{33,1},{64,96},{65,33},{96,128},{97,65},{12... | collective-permute-start | bytes 516104 | tf_op jit(solution)/shard_map/ppermute | solution.py:63
  45.8 5.7 %collective-permute-start.16 = (bf16[96,896]{1,0:T(8,128)(2,1)}, bf16[96,896]{1,0:T(8,128)(2,1)S(1)}, u32[]{:S(2)}, u32[]{:S(2)}) collective-permute-start(bf16[96,896]{1,0:T(8,128)(2,1)} %collective-permute-done.15.refs_7_), channel_id=1, source_target_pairs={{0,32},{1,225},{32,64},{33,1},{64,96},{65,33},{96,128},{97,65},{12... | collective-permute-start | bytes 516104 | tf_op jit(solution)/shard_map/ppermute | solution.py:63
  47.7 5.7 %collective-permute-start.8 = (bf16[96,896]{1,0:T(8,128)(2,1)S(1)}, bf16[96,896]{1,0:T(8,128)(2,1)S(1)}, u32[]{:S(2)}, u32[]{:S(2)}) collective-permute-start(bf16[96,896]{1,0:T(8,128)(2,1)S(1)} %collective-permute-done.3.refs_1_.refs_3_), channel_id=1, source_target_pairs={{0,32},{1,225},{32,64},{33,1},{64,96},{65,33},{96,128},{97,65},{12... | collective-permute-start | bytes 516104 | tf_op jit(solution)/shard_map/ppermute | solution.py:63
  47.7 7.7 %collective-permute-start.13 = (bf16[96,896]{1,0:T(8,128)(2,1)S(1)}, bf16[96,896]{1,0:T(8,128)(2,1)S(1)}, u32[]{:S(2)}, u32[]{:S(2)}) collective-permute-start(bf16[96,896]{1,0:T(8,128)(2,1)S(1)} %collective-permute-done.5.refs_2_.refs_8_), channel_id=1, source_target_pairs={{0,32},{1,225},{32,64},{33,1},{64,96},{65,33},{96,128},{97,65},{12... | collective-permute-start | bytes 516104 | tf_op jit(solution)/shard_map/ppermute | solution.py:63
  48.5 9.6 %collective-permute-start.12 = (bf16[96,896]{1,0:T(8,128)(2,1)S(1)}, bf16[96,896]{1,0:T(8,128)(2,1)S(1)}, u32[]{:S(2)}, u32[]{:S(2)}) collective-permute-start(bf16[96,896]{1,0:T(8,128)(2,1)S(1)} %collective-permute-done.11.refs_4_), channel_id=1, source_target_pairs={{0,32},{1,225},{32,64},{33,1},{64,96},{65,33},{96,128},{97,65},{12... | collective-permute-start | bytes 516104 | tf_op jit(solution)/shard_map/ppermute | solution.py:63
  51.5 8.7 %collective-permute-start.17 = (bf16[96,896]{1,0:T(8,128)(2,1)S(1)}, bf16[96,896]{1,0:T(8,128)(2,1)S(1)}, u32[]{:S(2)}, u32[]{:S(2)}) collective-permute-start(bf16[96,896]{1,0:T(8,128)(2,1)S(1)} %collective-permute-done.16.refs_9_), channel_id=1, source_target_pairs={{0,32},{1,225},{32,64},{33,1},{64,96},{65,33},{96,128},{97,65},{12... | collective-permute-start | bytes 516104 | tf_op jit(solution)/shard_map/ppermute | solution.py:63
  61.4 8.8 %collective-permute-start.18 = (bf16[96,896]{1,0:T(8,128)(2,1)S(1)}, bf16[96,896]{1,0:T(8,128)(2,1)S(1)}, u32[]{:S(2)}, u32[]{:S(2)}) collective-permute-start(bf16[96,896]{1,0:T(8,128)(2,1)S(1)} %get-tuple-element.9), channel_id=1, source_target_pairs={{0,32},{1,225},{32,64},{33,1},{64,96},{65,33},{96,128},{97,65},{12... | collective-permute-start | bytes 516104 | tf_op jit(solution)/shard_map/ppermute | solution.py:63
  65.0 5.8 %collective-permute-start.19 = (bf16[96,896]{1,0:T(8,128)(2,1)S(1)}, bf16[96,896]{1,0:T(8,128)(2,1)S(1)}, u32[]{:S(2)}, u32[]{:S(2)}) collective-permute-start(bf16[96,896]{1,0:T(8,128)(2,1)S(1)} %get-tuple-element.10), channel_id=1, source_target_pairs={{0,32},{1,225},{32,64},{33,1},{64,96},{65,33},{96,128},{97,65},{12... | collective-permute-start | bytes 516104 | tf_op jit(solution)/shard_map/ppermute | solution.py:63
  73.3 31.3 %all-to-all-start.1 = ((bf16[8,96,896]{2,1,0:T(8,128)(2,1)}), bf16[8,96,896]{2,1,0:T(8,128)(2,1)S(1)}, u32[]{:S(2)}, u32[]{:S(2)}) async-start(bf16[8,96,896]{2,1,0:T(8,128)(2,1)} %bitcast.15), calls=%async_computation.2 | async-start | bytes 2752512 | tf_op jit(solution)/shard_map/all_to_all | solution.py:146
  78.9 15.0 %collective-permute-start.21 = (bf16[96,256]{1,0:T(8,128)(2,1)S(1)}, bf16[96,256]{1,0:T(8,128)(2,1)S(1)}, u32[]{:S(2)}, u32[]{:S(2)}) collective-permute-start(bf16[96,256]{1,0:T(8,128)(2,1)S(1)} %shard_map.53), channel_id=1, source_target_pairs={{0,16},{16,0},{1,17},{17,1},{2,18},{18,2},{3,19},{19,3},{4,20},{20... | collective-permute-start | bytes 147464 | tf_op jit(solution)/shard_map/ppermute | solution.py:18
  93.9 10.7 %collective-permute-start.25 = (bf16[192,256]{1,0:T(8,128)(2,1)S(1)}, bf16[192,256]{1,0:T(8,128)(2,1)S(1)}, u32[]{:S(2)}, u32[]{:S(2)}) collective-permute-start(bf16[192,256]{1,0:T(8,128)(2,1)S(1)} %pad_maximum_fusion), channel_id=1, source_target_pairs={{0,32},{32,64},{64,96},{96,128},{128,160},{160,192},{192,224},{224... | collective-permute-start | bytes 294920 | tf_op jit(solution)/shard_map/ppermute | solution.py:14
  96.4 8.2 %collective-permute-start.22 = (bf16[192,256]{1,0:T(8,128)(2,1)S(1)}, bf16[192,256]{1,0:T(8,128)(2,1)S(1)}, u32[]{:S(2)}, u32[]{:S(2)}) collective-permute-start(bf16[192,256]{1,0:T(8,128)(2,1)S(1)} %pad_maximum_fusion), channel_id=1, source_target_pairs={{0,224},{32,0},{64,32},{96,64},{128,96},{160,128},{192,160},{224,1... | collective-permute-start | bytes 294920 | tf_op jit(solution)/shard_map/ppermute | solution.py:14
  105.9 23.3 %all-to-all-start.2 = ((bf16[8,96,896]{2,1,0:T(8,128)(2,1)}), bf16[8,96,896]{2,1,0:T(8,128)(2,1)S(1)}, u32[]{:S(2)}, u32[]{:S(2)}) async-start(bf16[8,96,896]{2,1,0:T(8,128)(2,1)} %bitcast.17), calls=%async_computation.3 | async-start | bytes 2752512 | tf_op jit(solution)/shard_map/all_to_all | solution.py:146
  (26 other events, 262.8 us)
Sparse Core Ops, SparseCore 0:
  42.8 32.1 reduce-scatter.1

commit v3 on v2

--- a/solution.py
+++ b/solution.py
@@ -27,7 +27,7 @@
 SMEM = pl.BlockSpec(memory_space=pltpu.SMEM)
 
 
-def call(body, out, ins, specs, after=(), flops=10**6, moved=10**6, **more):
+def call(body, out, ins, specs, after=(), flops=10**6, moved=10**6, grant=16, **more):
     def kernel(*refs):
         body(*refs[: len(ins)], *refs[len(ins) + len(after) :])
 
@@ -35,7 +35,7 @@
         kernel,
         out_shape=out,
         in_specs=list(specs) + [ANY] * len(after),
-        compiler_params=pltpu.CompilerParams(vmem_limit_bytes=16 * 1024 * 1024),
+        compiler_params=pltpu.CompilerParams(vmem_limit_bytes=grant * 1024 * 1024),
         cost_estimate=pl.CostEstimate(flops=flops, bytes_accessed=moved, transcendentals=0),
         **more,
     )(*ins, *after)
@@ -58,46 +58,61 @@
     return shift(up, "z", 1, NZ), shift(down, "z", -1, NZ)
 
 
-def lap(x):
-    steps = [(z, c, (z + 1 - 2 * c) % NZ) for z in range(NZ) for c in (0, 1)]
+def lap(x, only=None):
+    steps = [(z, c, (z + 1 - 2 * c) % NZ) for z in range(NZ) for c in (0, 1) if only in (None, c)]
     return lax.ppermute(x, ("z", "c"), [(2 * z + c, 2 * to + c) for z, c, to in steps])
 
 
-def pick(where, pairs, after=()):
+def join(*arrays, cols=None, after=()):
+    cols = [cols or x.shape[1] for x in arrays]
+
+    def body(*refs):
+        start = 0
+        for ref, col in zip(refs, cols):
+            refs[-1][:, start : start + col] = ref[:, :col]
+            start += col
+
+    out = jax.ShapeDtypeStruct((arrays[0].shape[0], sum(cols)), arrays[0].dtype)
+    return call(body, out, arrays, [VMEM] * len(arrays), after, out_specs=VMEM)
+
+
+def rotate(where, blocks, bases, done=(), after=()):
+    parts = [block if isinstance(block, tuple) else (block,) for block in blocks]
+    rows, depth, width = parts[0][0].shape[0], bases[0].shape[0], bases[0].shape[1]
+    count, total = len(parts), sum(len(part) for part in parts)
+    before = sum(x.shape[0] for x in done)
+
     def body(where, *refs):
-        ins, outs = refs[: 2 * len(pairs)], refs[2 * len(pairs) :]
-        for k, out in enumerate(outs):
-
-            @pl.when(where[1] == 0)
-            def _():
-                out[...] = ins[2 * k][...]
-
-            @pl.when(where[1] != 0)
-            def _():
-                out[...] = ins[2 * k + 1][...]
-
-    out = [jax.ShapeDtypeStruct(x.shape, x.dtype) for x, _ in pairs]
-    ins = [where] + [x for pair in pairs for x in pair]
-    return call(body, out, ins, [SMEM] + [VMEM] * (len(ins) - 1), after, out_specs=[VMEM] * len(pairs))
-
-
-def rotate(blocks, bases, done=(), after=()):
-    rows, width = blocks[0][0].shape[0], bases[0].shape[1]
-    before = sum(x.shape[0] for x in done)
-    parts = [block[0] for block in blocks] + [block[1] for block in blocks]
-
-    def body(*refs):
-        refs, (first, second, *done, out) = refs[: len(parts)], refs[len(parts) :]
-        left = jnp.concatenate([ref[...] for ref in refs[: len(blocks)]], axis=0)
-        right = jnp.concatenate([ref[...] for ref in refs[len(blocks) :]], axis=0)
-        out[before:] = (dot(left, first[...]) + dot(right, second[...])).astype(out.dtype)
-        for x in done:
-            out[:before] = x[...]
-
-    out = jax.ShapeDtypeStruct((before + rows * len(blocks), width), jnp.bfloat16)
-    flops = 4 * rows * len(blocks) * width * width
-    ins = parts + list(bases) + list(done)
-    return call(body, out, ins, [VMEM] * len(ins), after, flops, 6 * 10**6, out_specs=VMEM)
+        refs, bases, (*done, out, x, sems) = list(refs[:total]), refs[total : total + 2], refs[total + 2 :]
+        copies = []
+        for k, part in enumerate(parts):
+            place, sem = x.at[pl.ds(k * rows, rows)], sems.at[k]
+            copies.append(pltpu.make_async_copy(refs[0], place, sem))
+            if len(part) == 1:
+                copies[-1].start()
+            else:
+                for core in (0, 1):
+
+                    @pl.when(where[1] == core)
+                    def _():
+                        pltpu.make_async_copy(refs[core], place, sem).start()
+
+            refs = refs[len(part) :]
+        for ref in done:
+            out[:before] = ref[...]
+        for copy in copies:
+            copy.wait()
+        out[before:] = (dot(x[:, :depth], bases[0][...]) + dot(x[:, depth:], bases[1][...])).astype(out.dtype)
+
+    out = jax.ShapeDtypeStruct((before + count * rows, width), jnp.bfloat16)
+    scratch = [
+        pltpu.VMEM((count * rows, 2 * depth), jnp.bfloat16),
+        pltpu.SemaphoreType.DMA((count,)),
+    ]
+    ins = [where, *(x for part in parts for x in part), *bases, *done]
+    specs = [SMEM] + [ANY] * total + [VMEM] * (2 + len(done))
+    flops = 4 * count * rows * depth * width
+    return call(body, out, ins, specs, after, flops, 5 * 10**6, 52, out_specs=VMEM, scratch_shapes=scratch)
 
 
 def summed(parts, count, copies, after=()):
@@ -123,9 +138,9 @@
         for k, ref in enumerate((mine, theirs)):
             total = dot(ref[:, :depth], first[...]) + dot(ref[:, depth:], second[...])
             for chip in range(8):
-                out[chip, k] = total[chip * rows : (chip + 1) * rows]
-
-    out = jax.ShapeDtypeStruct((8, 2, rows, width), jnp.float32)
+                out[chip, k] = total[chip * rows : (chip + 1) * rows].astype(out.dtype)
+
+    out = jax.ShapeDtypeStruct((8, 2, rows, width), jnp.bfloat16)
     return call(body, out, [own, other, *bases], [VMEM] * 4, after, 2 * 10**8, 2 * 10**6, out_specs=VMEM)
 
 
@@ -136,7 +151,7 @@
         start = pl.multiple_of(where[0] * half, half)
         for k in range(8):
             out[k * half : (k + 1) * half, :depth] = mine[pl.ds(start, half)]
-            out[k * half : (k + 1) * half, depth:] = theirs[pl.ds(start, half)]
+            out[k * half : (k + 1) * half, depth:] = theirs[pl.ds(start, half), -depth:]
 
     out = jax.ShapeDtypeStruct((8 * half, 2 * depth), mine.dtype)
     return call(body, out, [where, mine, theirs], [SMEM, VMEM, VMEM], after, out_specs=VMEM)
@@ -192,32 +207,36 @@
     rows, half, width = grad_outputs.shape[0], grad_outputs.shape[0] // 2, grad_outputs.shape[1]
     cols = act_basis.shape[1]
 
-    theirs = swap(grad_outputs, "xh")
-    laps = [((grad_outputs, swap(grad_outputs, "c")), (theirs, swap(theirs, "c")))]
-    for _ in range(3):
-        laps.append(tuple(tuple(lap(x) for x in side) for side in laps[-1]))
+    mate = swap(grad_outputs, "c")
+    theirs = swap(join(grad_outputs, activations), "xh")
+    act_basis2 = swap(act_basis, "xh")
+    theirs_mate = swap(theirs, "c")
+    act_copies = act_halves(where, activations, theirs, (mate, act_basis2))
+    act_own = spread(act_copies, CHIPS)
+    laps = [[join(grad_outputs, mate, after=(act_copies,)), join(theirs, theirs_mate, cols=width, after=(act_copies,))]]
+    laps.append([lap(x) for x in laps[-1]])
+    laps.append([lap(x) for x in laps[-1]])
     basis2 = swap(grad_basis, "c")
-
-    act_x, act_basis2 = swap(activations, "xh"), swap(act_basis, "xh")
-    act_copies = act_halves(where, activations, act_x, (laps[0][0][1],))
-    (act_own,) = gate([spread(act_copies, CHIPS)], (*laps[2][0], act_basis2))
+    (act_own,) = gate([act_own], (laps[1][0],))
     act_oth = swap(act_own, "c")
     act_terms = rotate_act(act_own, act_oth, (act_basis, act_basis2))
-    act_sum = lax.psum_scatter(act_terms.reshape(8 * rows, cols), "z", scatter_dimension=0, tiled=True)
+    act_parts = spread(act_terms.reshape(8 * rows, cols), "z")
+    laps[2] = [*gate(laps[2][:1], (act_terms,)), laps[2][1]]
+    laps.append([lap(x) for x in laps[-1]])
     bases = grad_basis, basis2
-    near = pick(where, list(zip(*laps[0])))
-    early = rotate([near, laps[1][0], laps[1][1], laps[2][0], laps[2][1]], bases)
-    far = [lap(x) for x in pick(where, list(zip(*laps[3])), (act_terms,))]
-    terms = rotate([laps[3][0], laps[3][1], far], bases, (early,))
-
+    early = rotate(where, [tuple(laps[0]), *laps[1], *laps[2]], bases)
+    laps[3] = [*gate(laps[3][:1], (early,)), laps[3][1]]
+    far = tuple(lap(x, core) for core, x in enumerate(laps[3]))
+    act_half = summed(act_parts, 8, 1, laps[3][:1])
+    act_mate = swap(act_half, "xh")
+    terms = rotate(where, [*laps[3], far], bases, (early,), (act_mate,))
     parts = spread(terms, CHIPS)
-    act_pair = summed(act_sum, 1, 1, (terms,))
-    act_pair = jnp.concatenate([act_pair, swap(act_pair, "xh")], axis=0)
+    act_pair = jnp.concatenate([act_half, act_mate], axis=0)
     one = hop(act_pair, act_pair)
-    own = spread(summed(parts, 8, 8, one), CHIPS)
     two = hop(*one)
     three = hop(*two)
     four = hop(three[0][:, : cols // 2], three[1][:, cols // 2 :])
+    own = spread(summed(parts, 8, 8, two), CHIPS)
     (own,) = gate([own], four)
     other = swap(own, "c")
 

time: 144 us -> 129 us (0.90)
  the two profiles are of different devices: /device:TPU:7 before, /device:TPU:97 now
where the time goes in v3:
time: 129 us
  starting transfers between devices  52.9 us (41%)
  waiting for transfers between devices  51.3 us (40%)
  Pallas kernels  21.5 us (17%)
  local copies, waits for them, and re-layouts  2.78 us (2%)
    all_to_all x4, starting transfers between devices, spread(): return lax.all_to_all(x, axis, 0, 0, tiled=True)  23.1 us
    pallas_call x14, Pallas kernels, call(): pl.pallas_call(kernel, out_shape=out, in_specs=list(specs) + [ANY] * len(...  21.5 us
    ppermute x8, starting transfers between devices, swap(): return lax.ppermute(x, axis, [(0, 1), (1, 0)])  17.3 us
    ppermute x8, waiting for transfers between devices, swap(): return lax.ppermute(x, axis, [(0, 1), (1, 0)])  14.6 us
    all_to_all x4, waiting for transfers between devices, spread(): return lax.all_to_all(x, axis, 0, 0, tiled=True)  13.9 us
    ppermute x8, waiting for transfers between devices, lap(): lax.ppermute(x, ('z', 'c'), [(2 * z + c, 2 * to + c) for z, c, to in steps])  11.7 us
    ppermute x8, waiting for transfers between devices, shift(): return lax.ppermute(x, axis, [(i, (i + by) % size) for i in range(size)])  11.1 us
    ppermute x8, starting transfers between devices, shift(): return lax.ppermute(x, axis, [(i, (i + by) % size) for i in range(size)])  8.59 us
  transfers between devices with their start and end apart: 28, of which 18 were waited for; matrix products, arithmetic and copies ran while one was open for 0% of the time, Pallas kernels for 8%

profile of v3, /device:TPU:97, one launch (start us, length us, event | category | flops | bytes accessed | tf_op | source)
XLA Modules:
  0.0 128.8 jit_solution(2826165195256845806)
XLA Ops:
  2.4 2.8 %collective-permute-start = (bf16[96,1152]{1,0:T(8,128)(2,1)S(1)}, bf16[96,1152]{1,0:T(8,128)(2,1)S(1)}, u32[]{:S(2)}, u32[]{:S(2)}) collective-permute-start(bf16[96,1152]{1,0:T(8,128)(2,1)S(1)} %shard_map.46), channel_id=1, source_target_pairs={{0,16},{16,0},{1,17},{17,1},{2,18},{18,2},{3,19},{19,3},{4,20},{20... | collective-permute-start | bytes 663560 | tf_op jit(solution)/shard_map/ppermute | solution.py:18
  5.2 5.8 %collective-permute-done.refs_2_.refs_0_ = bf16[96,1152]{1,0:T(8,128)(2,1)S(1)} collective-permute-done((bf16[96,1152]{1,0:T(8,128)(2,1)S(1)}, bf16[96,1152]{1,0:T(8,128)(2,1)S(1)}, u32[]{:S(2)}, u32[]{:S(2)}) %collective-permute-start) | collective-permute-done | bytes 221216 | tf_op jit(solution)/shard_map/ppermute | solution.py:18
  11.9 2.7 %collective-permute-start.2 = (bf16[256,256]{1,0:T(8,128)(2,1)}, bf16[256,256]{1,0:T(8,128)(2,1)S(1)}, u32[]{:S(2)}, u32[]{:S(2)}) collective-permute-start(bf16[256,256]{1,0:T(8,128)(2,1)} %refs_2_.1), channel_id=1, source_target_pairs={{0,16},{16,0},{1,17},{17,1},{2,18},{18,2},{3,19},{19,3},{4,20},{20... | collective-permute-start | bytes 393224 | tf_op jit(solution)/shard_map/ppermute | solution.py:18
  14.7 3.4 %collective-permute-done.2.refs_4_.refs_3_ = bf16[256,256]{1,0:T(8,128)(2,1)S(1)} collective-permute-done((bf16[256,256]{1,0:T(8,128)(2,1)}, bf16[256,256]{1,0:T(8,128)(2,1)S(1)}, u32[]{:S(2)}, u32[]{:S(2)}) %collective-permute-start.2) | collective-permute-done | bytes 131104 | tf_op jit(solution)/shard_map/ppermute | solution.py:18
  21.4 5.1 %all-to-all-start = ((bf16[8,48,512]{2,1,0:T(8,128)(2,1)}), bf16[8,48,512]{2,1,0:T(8,128)(2,1)S(1)}, u32[]{:S(2)}, u32[]{:S(2)}) async-start(bf16[8,48,512]{2,1,0:T(8,128)(2,1)} %bitcast.3), calls=%async_computation | async-start | bytes 786432 | tf_op jit(solution)/shard_map/all_to_all | solution.py:161
  27.9 3.7 %collective-permute-done.3.refs_1_.refs_3_ = bf16[96,1792]{1,0:T(8,128)(2,1)S(1)} collective-permute-done((bf16[96,1792]{1,0:T(8,128)(2,1)S(1)}, bf16[96,1792]{1,0:T(8,128)(2,1)S(1)}, u32[]{:S(2)}, u32[]{:S(2)}) %collective-permute-start.3) | collective-permute-done | bytes 344096 | tf_op jit(solution)/shard_map/ppermute | solution.py:63
  33.2 6.9 %collective-permute-start.4 = (bf16[384,512]{1,0:T(8,128)(2,1)S(1)}, bf16[384,512]{1,0:T(8,128)(2,1)S(1)}, u32[]{:S(2)}, u32[]{:S(2)}) collective-permute-start(bf16[384,512]{1,0:T(8,128)(2,1)S(1)} %shard_map.49.refs_0_), channel_id=1, source_target_pairs={{0,1},{1,0},{2,3},{3,2},{4,5},{5,4},{6,7},{7,6},{8,9},{9,8},{10,11... | collective-permute-start | bytes 1179656 | tf_op jit(solution)/shard_map/ppermute | solution.py:18
  42.5 6.3 %all-to-all-start.1 = ((bf16[8,96,256]{2,1,0:T(8,128)(2,1)}), bf16[8,96,256]{2,1,0:T(8,128)(2,1)S(1)}, u32[]{:S(2)}, u32[]{:S(2)}) async-start(bf16[8,96,256]{2,1,0:T(8,128)(2,1)} %bitcast.5), calls=%async_computation.1 | async-start | bytes 786432 | tf_op jit(solution)/shard_map/all_to_all | solution.py:161
  49.2 2.1 %collective-permute-done.20.refs_2_ = bf16[96,1792]{1,0:T(8,128)(2,1)S(1)} collective-permute-done((bf16[96,1792]{1,0:T(8,128)(2,1)S(1)}, bf16[96,1792]{1,0:T(8,128)(2,1)S(1)}, u32[]{:S(2)}, u32[]{:S(2)}) %collective-permute-start.20) | collective-permute-done | bytes 344096 | tf_op jit(solution)/shard_map/ppermute | solution.py:63
  53.3 6.5 %shard_map.53.refs_1_.refs_7_ = bf16[480,896]{1,0:T(8,128)(2,1)} custom-call(s32[3]{0:T(128)S(1)} %pad_add_fusion.refs_0_, bf16[96,1792]{1,0:T(8,128)(2,1)S(1)} %shard_map.48.refs_1_, bf16[96,1792]{1,0:T(8,128)(2,1)S(1)} %shard_map.52.refs_2_, bf16[96,1792]{1,0:T(8,128)(2,1)S(1)} %collective-permute-done.3.refs_1_.refs_3_, ...), custom_call_target="tpu_custom_call" | custom-call | flops 1541406720 | bytes 5000000 | tf_op jit(solution)/shard_map/pallas_call | solution.py:34
  59.8 4.6 %collective-permute-done.6.refs_0_ = bf16[96,1792]{1,0:T(8,128)(2,1)S(1)} collective-permute-done((bf16[96,1792]{1,0:T(8,128)(2,1)S(1)}, bf16[96,1792]{1,0:T(8,128)(2,1)S(1)}, u32[]{:S(2)}, u32[]{:S(2)}) %collective-permute-start.6) | collective-permute-done | bytes 344096 | tf_op jit(solution)/shard_map/ppermute | solution.py:63
  66.3 2.5 %collective-permute-start.11 = (bf16[96,256]{1,0:T(8,128)(2,1)S(1)}, bf16[96,256]{1,0:T(8,128)(2,1)S(1)}, u32[]{:S(2)}, u32[]{:S(2)}) collective-permute-start(bf16[96,256]{1,0:T(8,128)(2,1)S(1)} %shard_map.55), channel_id=1, source_target_pairs={{0,16},{16,0},{1,17},{17,1},{2,18},{18,2},{3,19},{19,3},{4,20},{20... | collective-permute-start | bytes 147464 | tf_op jit(solution)/shard_map/ppermute | solution.py:18
  70.8 5.2 %shard_map.56 = bf16[768,896]{1,0:T(8,128)(2,1)} custom-call(s32[3]{0:T(128)S(1)} %pad_add_fusion.refs_0_, bf16[96,1792]{1,0:T(8,128)(2,1)S(1)} %shard_map.54.refs_1_, bf16[96,1792]{1,0:T(8,128)(2,1)S(1)} %collective-permute-done.20.refs_2_, bf16[96,1792]{1,0:T(8,128)(2,1)S(1)} %collective-permute-done.21.refs_3_, ...), custom_call_target="tpu_custom_call" | custom-call | flops 924844032 | bytes 5000000 | tf_op jit(solution)/shard_map/pallas_call | solution.py:34
  76.0 3.6 %all-to-all-start.2 = ((bf16[8,96,896]{2,1,0:T(8,128)(2,1)}), bf16[8,96,896]{2,1,0:T(8,128)(2,1)S(1)}, u32[]{:S(2)}, u32[]{:S(2)}) async-start(bf16[8,96,896]{2,1,0:T(8,128)(2,1)} %bitcast.37), calls=%async_computation.2 | async-start | bytes 2752512 | tf_op jit(solution)/shard_map/all_to_all | solution.py:161
  79.7 2.7 %collective-permute-start.15 = (bf16[192,256]{1,0:T(8,128)(2,1)S(1)}, bf16[192,256]{1,0:T(8,128)(2,1)S(1)}, u32[]{:S(2)}, u32[]{:S(2)}) collective-permute-start(bf16[192,256]{1,0:T(8,128)(2,1)S(1)} %pad_maximum_fusion), channel_id=1, source_target_pairs={{0,32},{32,64},{64,96},{96,128},{128,160},{160,192},{192,224},{224... | collective-permute-start | bytes 294920 | tf_op jit(solution)/shard_map/ppermute | solution.py:14
  82.4 2.0 %collective-permute-done.12 = bf16[192,256]{1,0:T(8,128)(2,1)S(1)} collective-permute-done((bf16[192,256]{1,0:T(8,128)(2,1)S(1)}, bf16[192,256]{1,0:T(8,128)(2,1)S(1)}, u32[]{:S(2)}, u32[]{:S(2)}) %collective-permute-start.12) | collective-permute-done | bytes 98336 | tf_op jit(solution)/shard_map/ppermute | solution.py:14
  84.4 2.7 %collective-permute-start.16 = (bf16[192,256]{1,0:T(8,128)(2,1)S(1)}, bf16[192,256]{1,0:T(8,128)(2,1)S(1)}, u32[]{:S(2)}, u32[]{:S(2)}) collective-permute-start(bf16[192,256]{1,0:T(8,128)(2,1)S(1)} %collective-permute-done.15), channel_id=1, source_target_pairs={{0,32},{32,64},{64,96},{96,128},{128,160},{160,192},{192,224},{224... | collective-permute-start | bytes 294920 | tf_op jit(solution)/shard_map/ppermute | solution.py:14
  87.1 2.7 %collective-permute-done.13.refs_2_ = bf16[192,256]{1,0:T(8,128)(2,1)S(1)} collective-permute-done((bf16[192,256]{1,0:T(8,128)(2,1)S(1)}, bf16[192,256]{1,0:T(8,128)(2,1)S(1)}, u32[]{:S(2)}, u32[]{:S(2)}) %collective-permute-start.13) | collective-permute-done | bytes 98336 | tf_op jit(solution)/shard_map/ppermute | solution.py:14
  89.8 3.4 %all-to-all-done.2 = bf16[8,96,896]{2,1,0:T(8,128)(2,1)S(1)} async-done(((bf16[8,96,896]{2,1,0:T(8,128)(2,1)}), bf16[8,96,896]{2,1,0:T(8,128)(2,1)S(1)}, u32[]{:S(2)}, u32[]{:S(2)}) %all-to-all-start.2) | async-done | bytes 1376288 | tf_op jit(solution)/shard_map/all_to_all | solution.py:161
  94.5 8.0 %all-to-all-start.3 = ((bf16[8,96,896]{2,1,0:T(8,128)(2,1)}), bf16[8,96,896]{2,1,0:T(8,128)(2,1)S(1)}, u32[]{:S(2)}, u32[]{:S(2)}) async-start(bf16[8,96,896]{2,1,0:T(8,128)(2,1)} %bitcast.18), calls=%async_computation.3 | async-start | bytes 2752512 | tf_op jit(solution)/shard_map/all_to_all | solution.py:161
  109.2 2.9 %collective-permute-done.19.refs_2_ = bf16[192,128]{1,0:T(8,128)(2,1)S(1)} collective-permute-done((bf16[192,128]{1,0:T(8,128)(2,1)S(1)}, bf16[192,128]{1,0:T(8,128)(2,1)S(1)}, u32[]{:S(2)}, u32[]{:S(2)}) %collective-permute-start.19) | collective-permute-done | bytes 49184 | tf_op jit(solution)/shard_map/ppermute | solution.py:14
  112.1 8.8 %all-to-all-done.3 = bf16[8,96,896]{2,1,0:T(8,128)(2,1)S(1)} async-done(((bf16[8,96,896]{2,1,0:T(8,128)(2,1)}), bf16[8,96,896]{2,1,0:T(8,128)(2,1)S(1)}, u32[]{:S(2)}, u32[]{:S(2)}) %all-to-all-start.3) | async-done | bytes 1376288 | tf_op jit(solution)/shard_map/all_to_all | solution.py:161
  121.8 2.8 %collective-permute-done.23 = bf16[768,896]{1,0:T(8,128)(2,1)S(1)} collective-permute-done((bf16[768,896]{1,0:T(8,128)(2,1)S(1)}, bf16[768,896]{1,0:T(8,128)(2,1)S(1)}, u32[]{:S(2)}, u32[]{:S(2)}) %collective-permute-start.23) | collective-permute-done | bytes 1376288 | tf_op jit(solution)/shard_map/ppermute | solution.py:18
  124.5 4.1 %shard_map.59 = f32[256,896]{1,0:T(8,128)} custom-call(s32[3]{0:T(128)S(1)} %pad_add_fusion.refs_0_, bf16[2,2,48,256]{3,2,1,0:T(8,128)(2,1)S(1)} %bitcast.30, bf16[2,2,48,256]{3,2,1,0:T(8,128)(2,1)S(1)} %bitcast.35, bf16[2,2,48,256]{3,2,1,0:T(8,128)(2,1)S(1)} %bitcast.28, bf16[2,2,48,256]{3,2,1,0:T(8,128)(2,1)S(1)} %bitcast.32, ...), custom_call_target="tpu_custom_call" | custom-call | flops 703000000 | bytes 5000000 | tf_op jit(solution)/shard_map/pallas_call | solution.py:34
  (60 shorter events, 27.0 us)
Async XLA Ops:
  0.0 53.3 %collective-permute-start.10 = (bf16[896,896]{1,0:T(8,128)(2,1)}, bf16[896,896]{1,0:T(8,128)(2,1)}, u32[]{:S(2)}, u32[]{:S(2)}) collective-permute-start(bf16[896,896]{1,0:T(8,128)(2,1)} %refs_5_.1), channel_id=1, source_target_pairs={{0,1},{1,0},{2,3},{3,2},{4,5},{5,4},{6,7},{7,6},{8,9},{9,8},{10,11... | collective-permute-start | bytes 4816904 | tf_op jit(solution)/shard_map/ppermute | solution.py:18
  2.4 8.6 %collective-permute-start = (bf16[96,1152]{1,0:T(8,128)(2,1)S(1)}, bf16[96,1152]{1,0:T(8,128)(2,1)S(1)}, u32[]{:S(2)}, u32[]{:S(2)}) collective-permute-start(bf16[96,1152]{1,0:T(8,128)(2,1)S(1)} %shard_map.46), channel_id=1, source_target_pairs={{0,16},{16,0},{1,17},{17,1},{2,18},{18,2},{3,19},{19,3},{4,20},{20... | collective-permute-start | bytes 663560 | tf_op jit(solution)/shard_map/ppermute | solution.py:18
  11.1 9.2 %collective-permute-start.7 = (bf16[96,1152]{1,0:T(8,128)(2,1)S(1)}, bf16[96,1152]{1,0:T(8,128)(2,1)S(1)}, u32[]{:S(2)}, u32[]{:S(2)}) collective-permute-start(bf16[96,1152]{1,0:T(8,128)(2,1)S(1)} %collective-permute-done.refs_2_.refs_0_), channel_id=1, source_target_pairs={{0,1},{1,0},{2,3},{3,2},{4,5},{5,4},{6,7},{7,6},{8,9},{9,8},{10,11... | collective-permute-start | bytes 663560 | tf_op jit(solution)/shard_map/ppermute | solution.py:18
  11.8 6.3 %collective-permute-start.1 = (bf16[96,896]{1,0:T(8,128)(2,1)}, bf16[96,896]{1,0:T(8,128)(2,1)S(1)}, u32[]{:S(2)}, u32[]{:S(2)}) collective-permute-start(bf16[96,896]{1,0:T(8,128)(2,1)} %refs_0_.3), channel_id=1, source_target_pairs={{0,1},{1,0},{2,3},{3,2},{4,5},{5,4},{6,7},{7,6},{8,9},{9,8},{10,11... | collective-permute-start | bytes 516104 | tf_op jit(solution)/shard_map/ppermute | solution.py:18
  11.9 6.3 %collective-permute-start.2 = (bf16[256,256]{1,0:T(8,128)(2,1)}, bf16[256,256]{1,0:T(8,128)(2,1)S(1)}, u32[]{:S(2)}, u32[]{:S(2)}) collective-permute-start(bf16[256,256]{1,0:T(8,128)(2,1)} %refs_2_.1), channel_id=1, source_target_pairs={{0,16},{16,0},{1,17},{17,1},{2,18},{18,2},{3,19},{19,3},{4,20},{20... | collective-permute-start | bytes 393224 | tf_op jit(solution)/shard_map/ppermute | solution.py:18
  20.3 7.6 %collective-permute-start.8 = (bf16[96,1792]{1,0:T(8,128)(2,1)S(1)}, bf16[96,1792]{1,0:T(8,128)(2,1)S(1)}, u32[]{:S(2)}, u32[]{:S(2)}) collective-permute-start(bf16[96,1792]{1,0:T(8,128)(2,1)S(1)} %shard_map.52.refs_2_), channel_id=1, source_target_pairs={{0,32},{1,225},{32,64},{33,1},{64,96},{65,33},{96,128},{97,65},{12... | collective-permute-start | bytes 1032200 | tf_op jit(solution)/shard_map/ppermute | solution.py:63
  21.3 10.2 %collective-permute-start.3 = (bf16[96,1792]{1,0:T(8,128)(2,1)S(1)}, bf16[96,1792]{1,0:T(8,128)(2,1)S(1)}, u32[]{:S(2)}, u32[]{:S(2)}) collective-permute-start(bf16[96,1792]{1,0:T(8,128)(2,1)S(1)} %shard_map.48.refs_1_), channel_id=1, source_target_pairs={{0,32},{1,225},{32,64},{33,1},{64,96},{65,33},{96,128},{97,65},{12... | collective-permute-start | bytes 1032200 | tf_op jit(solution)/shard_map/ppermute | solution.py:63
  21.4 11.7 %all-to-all-start = ((bf16[8,48,512]{2,1,0:T(8,128)(2,1)}), bf16[8,48,512]{2,1,0:T(8,128)(2,1)S(1)}, u32[]{:S(2)}, u32[]{:S(2)}) async-start(bf16[8,48,512]{2,1,0:T(8,128)(2,1)} %bitcast.3), calls=%async_computation | async-start | bytes 786432 | tf_op jit(solution)/shard_map/all_to_all | solution.py:161
  27.9 12.9 %collective-permute-start.9 = (bf16[96,1792]{1,0:T(8,128)(2,1)S(1)}, bf16[96,1792]{1,0:T(8,128)(2,1)S(1)}, u32[]{:S(2)}, u32[]{:S(2)}) collective-permute-start(bf16[96,1792]{1,0:T(8,128)(2,1)S(1)} %collective-permute-done.8.refs_4_), channel_id=1, source_target_pairs={{0,32},{1,225},{32,64},{33,1},{64,96},{65,33},{96,128},{97,65},{12... | collective-permute-start | bytes 1032200 | tf_op jit(solution)/shard_map/ppermute | solution.py:63
  33.2 8.2 %collective-permute-start.4 = (bf16[384,512]{1,0:T(8,128)(2,1)S(1)}, bf16[384,512]{1,0:T(8,128)(2,1)S(1)}, u32[]{:S(2)}, u32[]{:S(2)}) collective-permute-start(bf16[384,512]{1,0:T(8,128)(2,1)S(1)} %shard_map.49.refs_0_), channel_id=1, source_target_pairs={{0,1},{1,0},{2,3},{3,2},{4,5},{5,4},{6,7},{7,6},{8,9},{9,8},{10,11... | collective-permute-start | bytes 1179656 | tf_op jit(solution)/shard_map/ppermute | solution.py:18
  40.1 8.8 %collective-permute-start.5 = (bf16[96,1792]{1,0:T(8,128)(2,1)S(1)}, bf16[96,1792]{1,0:T(8,128)(2,1)S(1)}, u32[]{:S(2)}, u32[]{:S(2)}) collective-permute-start(bf16[96,1792]{1,0:T(8,128)(2,1)S(1)} %collective-permute-done.3.refs_1_.refs_3_), channel_id=1, source_target_pairs={{0,32},{1,225},{32,64},{33,1},{64,96},{65,33},{96,128},{97,65},{12... | collective-permute-start | bytes 1032200 | tf_op jit(solution)/shard_map/ppermute | solution.py:63
  40.8 10.6 %collective-permute-start.20 = (bf16[96,1792]{1,0:T(8,128)(2,1)S(1)}, bf16[96,1792]{1,0:T(8,128)(2,1)S(1)}, u32[]{:S(2)}, u32[]{:S(2)}) collective-permute-start(bf16[96,1792]{1,0:T(8,128)(2,1)S(1)} %collective-permute-done.9.refs_6_), channel_id=1, source_target_pairs={{0,32},{1,225},{32,64},{33,1},{64,96},{65,33},{96,128},{97,65},{12... | collective-permute-start | bytes 1032200 | tf_op jit(solution)/shard_map/ppermute | solution.py:63
  42.5 23.7 %all-to-all-start.1 = ((bf16[8,96,256]{2,1,0:T(8,128)(2,1)}), bf16[8,96,256]{2,1,0:T(8,128)(2,1)S(1)}, u32[]{:S(2)}, u32[]{:S(2)}) async-start(bf16[8,96,256]{2,1,0:T(8,128)(2,1)} %bitcast.5), calls=%async_computation.1 | async-start | bytes 786432 | tf_op jit(solution)/shard_map/all_to_all | solution.py:161
  48.9 15.5 %collective-permute-start.6 = (bf16[96,1792]{1,0:T(8,128)(2,1)S(1)}, bf16[96,1792]{1,0:T(8,128)(2,1)S(1)}, u32[]{:S(2)}, u32[]{:S(2)}) collective-permute-start(bf16[96,1792]{1,0:T(8,128)(2,1)S(1)} %shard_map.51.refs_5_), channel_id=1, source_target_pairs={{0,32},{1,225},{32,64},{33,1},{64,96},{65,33},{96,128},{97,65},{12... | collective-permute-start | bytes 1032200 | tf_op jit(solution)/shard_map/ppermute | solution.py:63
  51.3 19.4 %collective-permute-start.22 = (bf16[96,1792]{1,0:T(8,128)(2,1)S(1)}, bf16[96,1792]{1,0:T(8,128)(2,1)S(1)}, u32[]{:S(2)}, u32[]{:S(2)}) collective-permute-start(bf16[96,1792]{1,0:T(8,128)(2,1)S(1)} %collective-permute-done.20.refs_2_), channel_id=1, source_target_pairs={{1,225},{33,1},{65,33},{97,65},{129,97},{161,129},{193,161},{225,1... | collective-permute-start | bytes 1032200 | tf_op jit(solution)/shard_map/ppermute | solution.py:63
  65.5 5.3 %collective-permute-start.21 = (bf16[96,1792]{1,0:T(8,128)(2,1)S(1)}, bf16[96,1792]{1,0:T(8,128)(2,1)S(1)}, u32[]{:S(2)}, u32[]{:S(2)}) collective-permute-start(bf16[96,1792]{1,0:T(8,128)(2,1)S(1)} %shard_map.54.refs_1_), channel_id=1, source_target_pairs={{0,32},{32,64},{64,96},{96,128},{128,160},{160,192},{192,224},{224... | collective-permute-start | bytes 1032200 | tf_op jit(solution)/shard_map/ppermute | solution.py:63
  76.0 17.2 %all-to-all-start.2 = ((bf16[8,96,896]{2,1,0:T(8,128)(2,1)}), bf16[8,96,896]{2,1,0:T(8,128)(2,1)S(1)}, u32[]{:S(2)}, u32[]{:S(2)}) async-start(bf16[8,96,896]{2,1,0:T(8,128)(2,1)} %bitcast.37), calls=%async_computation.2 | async-start | bytes 2752512 | tf_op jit(solution)/shard_map/all_to_all | solution.py:161
  79.6 4.8 %collective-permute-start.12 = (bf16[192,256]{1,0:T(8,128)(2,1)S(1)}, bf16[192,256]{1,0:T(8,128)(2,1)S(1)}, u32[]{:S(2)}, u32[]{:S(2)}) collective-permute-start(bf16[192,256]{1,0:T(8,128)(2,1)S(1)} %pad_maximum_fusion), channel_id=1, source_target_pairs={{0,224},{32,0},{64,32},{96,64},{128,96},{160,128},{192,160},{224,1... | collective-permute-start | bytes 294920 | tf_op jit(solution)/shard_map/ppermute | solution.py:14
  79.7 4.7 %collective-permute-start.15 = (bf16[192,256]{1,0:T(8,128)(2,1)S(1)}, bf16[192,256]{1,0:T(8,128)(2,1)S(1)}, u32[]{:S(2)}, u32[]{:S(2)}) collective-permute-start(bf16[192,256]{1,0:T(8,128)(2,1)S(1)} %pad_maximum_fusion), channel_id=1, source_target_pairs={{0,32},{32,64},{64,96},{96,128},{128,160},{160,192},{192,224},{224... | collective-permute-start | bytes 294920 | tf_op jit(solution)/shard_map/ppermute | solution.py:14
  84.4 5.4 %collective-permute-start.13 = (bf16[192,256]{1,0:T(8,128)(2,1)S(1)}, bf16[192,256]{1,0:T(8,128)(2,1)S(1)}, u32[]{:S(2)}, u32[]{:S(2)}) collective-permute-start(bf16[192,256]{1,0:T(8,128)(2,1)S(1)} %collective-permute-done.12), channel_id=1, source_target_pairs={{0,224},{32,0},{64,32},{96,64},{128,96},{160,128},{192,160},{224,1... | collective-permute-start | bytes 294920 | tf_op jit(solution)/shard_map/ppermute | solution.py:14
  84.4 5.4 %collective-permute-start.16 = (bf16[192,256]{1,0:T(8,128)(2,1)S(1)}, bf16[192,256]{1,0:T(8,128)(2,1)S(1)}, u32[]{:S(2)}, u32[]{:S(2)}) collective-permute-start(bf16[192,256]{1,0:T(8,128)(2,1)S(1)} %collective-permute-done.15), channel_id=1, source_target_pairs={{0,32},{32,64},{64,96},{96,128},{128,160},{160,192},{192,224},{224... | collective-permute-start | bytes 294920 | tf_op jit(solution)/shard_map/ppermute | solution.py:14
  94.5 26.4 %all-to-all-start.3 = ((bf16[8,96,896]{2,1,0:T(8,128)(2,1)}), bf16[8,96,896]{2,1,0:T(8,128)(2,1)S(1)}, u32[]{:S(2)}, u32[]{:S(2)}) async-start(bf16[8,96,896]{2,1,0:T(8,128)(2,1)} %bitcast.18), calls=%async_computation.3 | async-start | bytes 2752512 | tf_op jit(solution)/shard_map/all_to_all | solution.py:161
  102.6 4.7 %collective-permute-start.14 = (bf16[192,256]{1,0:T(8,128)(2,1)S(1)}, bf16[192,256]{1,0:T(8,128)(2,1)S(1)}, u32[]{:S(2)}, u32[]{:S(2)}) collective-permute-start(bf16[192,256]{1,0:T(8,128)(2,1)S(1)} %collective-permute-done.13.refs_2_), channel_id=1, source_target_pairs={{0,224},{32,0},{64,32},{96,64},{128,96},{160,128},{192,160},{224,1... | collective-permute-start | bytes 294920 | tf_op jit(solution)/shard_map/ppermute | solution.py:14
  107.3 4.8 %collective-permute-start.19 = (bf16[192,128]{1,0:T(8,128)(2,1)S(1)}, bf16[192,128]{1,0:T(8,128)(2,1)S(1)}, u32[]{:S(2)}, u32[]{:S(2)}) collective-permute-start(bf16[192,128]{1,0:T(8,128)(2,1)S(1)} %slice.9), channel_id=1, source_target_pairs={{0,224},{32,0},{64,32},{96,64},{128,96},{160,128},{192,160},{224,1... | collective-permute-start | bytes 147464 | tf_op jit(solution)/shard_map/ppermute | solution.py:14
  (9 other events, 46.8 us)

commit v4 on v3

--- a/solution.py
+++ b/solution.py
@@ -54,8 +54,8 @@
     )
 
 
-def hop(up, down):
-    return shift(up, "z", 1, NZ), shift(down, "z", -1, NZ)
+def hop(up, down, by=1):
+    return shift(up, "z", by, NZ), shift(down, "z", -by, NZ)
 
 
 def lap(x, only=None):
@@ -76,15 +76,18 @@
     return call(body, out, arrays, [VMEM] * len(arrays), after, out_specs=VMEM)
 
 
-def rotate(where, blocks, bases, done=(), after=()):
+def rotate(where, blocks, bases, start, total, sums=(), after=()):
     parts = [block if isinstance(block, tuple) else (block,) for block in blocks]
     rows, depth, width = parts[0][0].shape[0], bases[0].shape[0], bases[0].shape[1]
-    count, total = len(parts), sum(len(part) for part in parts)
-    before = sum(x.shape[0] for x in done)
+    count, many = len(parts), sum(len(part) for part in parts)
 
     def body(where, *refs):
-        refs, bases, (*done, out, x, sems) = list(refs[:total]), refs[total : total + 2], refs[total + 2 :]
-        copies = []
+        refs, bases, (out, token, x, base, result, sems, out_sems, base_sems) = list(refs[:many]), refs[many : many + 2], refs[-8:]
+        copies, slab = [], depth // 7
+        for k in range(14):
+            source = bases[k // 7].at[pl.ds(k % 7 * slab, slab)]
+            copies.append(pltpu.make_async_copy(source, base.at[pl.ds(k * slab, slab)], base_sems.at[k]))
+            copies[-1].start()
         for k, part in enumerate(parts):
             place, sem = x.at[pl.ds(k * rows, rows)], sems.at[k]
             copies.append(pltpu.make_async_copy(refs[0], place, sem))
@@ -98,21 +101,32 @@
                         pltpu.make_async_copy(refs[core], place, sem).start()
 
             refs = refs[len(part) :]
-        for ref in done:
-            out[:before] = ref[...]
         for copy in copies:
             copy.wait()
-        out[before:] = (dot(x[:, :depth], bases[0][...]) + dot(x[:, depth:], bases[1][...])).astype(out.dtype)
-
-    out = jax.ShapeDtypeStruct((before + count * rows, width), jnp.bfloat16)
+        result[...] = dot(x[...], base[...]).astype(result.dtype)
+        token[...] = jnp.zeros_like(token)
+        copies = []
+        for k in range(count):
+            here, there = pl.ds(k * rows, rows), pl.ds(start + k * rows, rows)
+            copies.append(pltpu.make_async_copy(result.at[here], out.at[there], out_sems.at[k]))
+            copies[-1].start()
+        for copy in copies:
+            copy.wait()
+
+    out = [jax.ShapeDtypeStruct((total, width), jnp.bfloat16), jax.ShapeDtypeStruct((8, 128), jnp.float32)]
     scratch = [
         pltpu.VMEM((count * rows, 2 * depth), jnp.bfloat16),
+        pltpu.VMEM((2 * depth, width), jnp.bfloat16),
+        pltpu.VMEM((count * rows, width), jnp.bfloat16),
         pltpu.SemaphoreType.DMA((count,)),
+        pltpu.SemaphoreType.DMA((count,)),
+        pltpu.SemaphoreType.DMA((14,)),
     ]
-    ins = [where, *(x for part in parts for x in part), *bases, *done]
-    specs = [SMEM] + [ANY] * total + [VMEM] * (2 + len(done))
+    ins = [where, *(x for part in parts for x in part), *bases, *sums]
+    specs = [SMEM] + [ANY] * (len(ins) - 1)
     flops = 4 * count * rows * depth * width
-    return call(body, out, ins, specs, after, flops, 5 * 10**6, 52, out_specs=VMEM, scratch_shapes=scratch)
+    more = {"input_output_aliases": {len(ins) - 1: 0}} if sums else {}
+    return call(body, out, ins, specs, after, flops, 5 * 10**6, 52, out_specs=[ANY, VMEM], scratch_shapes=scratch, **more)
 
 
 def summed(parts, count, copies, after=()):
@@ -162,19 +176,12 @@
 
 
 def coeffs_kernel(where, *refs):
-    sources, (out, grads, act, sems) = refs[:11], refs[11:]
+    sources, (mine, other, out, act) = refs[:9], refs[9:]
     width = act.shape[-1] // 2
-    copies = []
     for k, src in enumerate(sources[:7]):
-        copies.append(pltpu.make_async_copy(src, act.at[k + (k >= 4)], sems.at[k]))
-    for k, src in enumerate(sources[7:9]):
-        copies.append(pltpu.make_async_copy(src, act.at[NZ // 2, :, :, :, pl.ds(k * width, width)], sems.at[7 + k]))
-    for k, src in enumerate(sources[9:]):
-        copies.append(pltpu.make_async_copy(src, grads.at[k], sems.at[9 + k]))
-    for copy in copies:
-        copy.start()
-    for copy in copies:
-        copy.wait()
+        act[k + (k >= 4)] = src[...]
+    for k, src in enumerate(sources[7:]):
+        act[NZ // 2, :, :, :, k * width : (k + 1) * width] = src[...]
     xh, c, z = where[0], where[1], where[2]
     total = None
     for seq in range(SEQS):
@@ -189,7 +196,7 @@
                 place = jnp.where(halved, 7 * (rel // (NZ // 2)), place)
                 parity = jnp.bitwise_xor(jnp.bitwise_xor(xh, side), c)
                 left += [act[rel, xh, parity], act[rel, 1 - xh, parity]]
-                right.append(grads[jnp.bitwise_xor(core, c), place])
+                right.append(jnp.where(core == c, mine[place], other[place]))
         coeffs = lax.dot_general(
             jnp.concatenate(left, axis=0),
             jnp.concatenate(right, axis=0),
@@ -211,33 +218,33 @@
     theirs = swap(join(grad_outputs, activations), "xh")
     act_basis2 = swap(act_basis, "xh")
     theirs_mate = swap(theirs, "c")
-    act_copies = act_halves(where, activations, theirs, (mate, act_basis2))
+    act_copies = act_halves(where, activations, theirs, (mate,))
     act_own = spread(act_copies, CHIPS)
     laps = [[join(grad_outputs, mate, after=(act_copies,)), join(theirs, theirs_mate, cols=width, after=(act_copies,))]]
     laps.append([lap(x) for x in laps[-1]])
     laps.append([lap(x) for x in laps[-1]])
     basis2 = swap(grad_basis, "c")
-    (act_own,) = gate([act_own], (laps[1][0],))
+    (act_own,) = gate([act_own], (laps[1][0], act_basis2))
     act_oth = swap(act_own, "c")
     act_terms = rotate_act(act_own, act_oth, (act_basis, act_basis2))
     act_parts = spread(act_terms.reshape(8 * rows, cols), "z")
     laps[2] = [*gate(laps[2][:1], (act_terms,)), laps[2][1]]
     laps.append([lap(x) for x in laps[-1]])
     bases = grad_basis, basis2
-    early = rotate(where, [tuple(laps[0]), *laps[1], *laps[2]], bases)
-    laps[3] = [*gate(laps[3][:1], (early,)), laps[3][1]]
+    early, token = rotate(where, [tuple(laps[0]), *laps[1], *laps[2]], bases, 0, 8 * rows)
+    laps[3] = [*gate(laps[3][:1], (token,)), laps[3][1]]
     far = tuple(lap(x, core) for core, x in enumerate(laps[3]))
     act_half = summed(act_parts, 8, 1, laps[3][:1])
     act_mate = swap(act_half, "xh")
-    terms = rotate(where, [*laps[3], far], bases, (early,), (act_mate,))
+    terms, _ = rotate(where, [*laps[3], far], bases, 5 * rows, 8 * rows, (early,), (act_mate,))
     parts = spread(terms, CHIPS)
     act_pair = jnp.concatenate([act_half, act_mate], axis=0)
     one = hop(act_pair, act_pair)
-    two = hop(*one)
+    two = hop(act_pair, act_pair, 2)
+    own = spread(summed(parts, 8, 8, one + two), CHIPS)
     three = hop(*two)
-    four = hop(three[0][:, : cols // 2], three[1][:, cols // 2 :])
-    own = spread(summed(parts, 8, 8, two), CHIPS)
-    (own,) = gate([own], four)
+    four = hop(two[0][:, : cols // 2], two[1][:, cols // 2 :], 2)
+    (own,) = gate([own], three + four)
     other = swap(own, "c")
 
     acts = [x.reshape(2, 2, half, cols) for x in (act_pair, one[1], two[1], three[1], three[0], two[0], one[0])]
@@ -246,14 +253,12 @@
         coeffs_kernel,
         jax.ShapeDtypeStruct((cols, width), jnp.float32),
         [where] + acts + [x.reshape(8, rows, width) for x in (own, other)],
-        [SMEM] + [ANY] * 11,
+        [SMEM] + [VMEM] * 11,
         flops=703 * 10**6,
         moved=5 * 10**6,
         out_specs=VMEM,
         scratch_shapes=[
-            pltpu.VMEM((2, 8, rows, width), jnp.bfloat16),
             pltpu.VMEM((NZ, 2, 2, half, cols), jnp.bfloat16),
-            pltpu.SemaphoreType.DMA((11,)),
         ],
     )
 

time: 129 us -> 124 us (0.961)
  waiting for transfers between devices: 51.3 us -> 47.1 us
  Pallas kernels: 21.5 us -> 19.7 us
  starting transfers between devices: 52.9 us -> 54.3 us
    ppermute x8, waiting for transfers between devices: 11.1 us -> 5.46 us  [shift(): return lax.ppermute(x, axis, [(i, (i + by) % size) for i in range(size)])]
    ppermute x8, waiting for transfers between devices: 11.7 us -> 7.58 us  [lap(): lax.ppermute(x, ('z', 'c'), [(2 * z + c, 2 * to + c) for z, c, to in steps])]
    ppermute x8, waiting for transfers between devices: 14.6 us -> 18.1 us  [swap(): return lax.ppermute(x, axis, [(0, 1), (1, 0)])]
    ppermute x8, starting transfers between devices: 17.3 us -> 14.4 us  [swap(): return lax.ppermute(x, axis, [(0, 1), (1, 0)])]
    all_to_all x4, waiting for transfers between devices: 13.9 us -> 16 us  [spread(): return lax.all_to_all(x, axis, 0, 0, tiled=True)]
    pallas_call x14, Pallas kernels: 21.5 us -> 19.7 us  [call(): pl.pallas_call(kernel, out_shape=out, in_specs=list(specs) + [ANY] * len(...]
    ppermute x8, starting transfers between devices: 8.59 us -> 10.3 us  [shift(): return lax.ppermute(x, axis, [(i, (i + by) % size) for i in range(size)])]
    ppermute x8, starting transfers between devices: 3.92 us -> 5.36 us  [lap(): lax.ppermute(x, ('z', 'c'), [(2 * z + c, 2 * to + c) for z, c, to in steps])]
  transfers between devices with their start and end apart: 28 -> 28, of which waited for: 18 -> 14; matrix products, arithmetic and copies ran while one was open for 0% -> 0% of each run, Pallas kernels for 8% -> 8%
where the time goes in v4:
time: 124 us; the launch traced here: 123 us
  starting transfers between devices  54.3 us (44%)
  waiting for transfers between devices  47.1 us (38%)
  Pallas kernels  19.7 us (16%)
  local copies, waits for them, and re-layouts  1.61 us (1%)
    all_to_all x4, starting transfers between devices, spread(): return lax.all_to_all(x, axis, 0, 0, tiled=True)  24.2 us
    pallas_call x14, Pallas kernels, call(): pl.pallas_call(kernel, out_shape=out, in_specs=list(specs) + [ANY] * len(...  19.7 us
    ppermute x8, waiting for transfers between devices, swap(): return lax.ppermute(x, axis, [(0, 1), (1, 0)])  18.1 us
    all_to_all x4, waiting for transfers between devices, spread(): return lax.all_to_all(x, axis, 0, 0, tiled=True)  16 us
    ppermute x8, starting transfers between devices, swap(): return lax.ppermute(x, axis, [(0, 1), (1, 0)])  14.4 us
    ppermute x8, starting transfers between devices, shift(): return lax.ppermute(x, axis, [(i, (i + by) % size) for i in range(size)])  10.3 us
    ppermute x8, waiting for transfers between devices, lap(): lax.ppermute(x, ('z', 'c'), [(2 * z + c, 2 * to + c) for z, c, to in steps])  7.58 us
    ppermute x8, waiting for transfers between devices, shift(): return lax.ppermute(x, axis, [(i, (i + by) % size) for i in range(size)])  5.46 us
  transfers between devices with their start and end apart: 28, of which 14 were waited for; matrix products, arithmetic and copies ran while one was open for 0% of the time, Pallas kernels for 8%

profile of v4, /device:TPU:97, one launch (start us, length us, event | category | flops | bytes accessed | tf_op | source)
XLA Modules:
  0.0 122.9 jit_solution(18164128388128275400)
XLA Ops:
  2.4 2.8 %collective-permute-start = (bf16[96,1152]{1,0:T(8,128)(2,1)S(1)}, bf16[96,1152]{1,0:T(8,128)(2,1)S(1)}, u32[]{:S(2)}, u32[]{:S(2)}) collective-permute-start(bf16[96,1152]{1,0:T(8,128)(2,1)S(1)} %shard_map.46), channel_id=1, source_target_pairs={{0,16},{16,0},{1,17},{17,1},{2,18},{18,2},{3,19},{19,3},{4,20},{20... | collective-permute-start | bytes 663560 | tf_op jit(solution)/shard_map/ppermute | solution.py:18
  5.2 5.8 %collective-permute-done.refs_2_.refs_0_ = bf16[96,1152]{1,0:T(8,128)(2,1)S(1)} collective-permute-done((bf16[96,1152]{1,0:T(8,128)(2,1)S(1)}, bf16[96,1152]{1,0:T(8,128)(2,1)S(1)}, u32[]{:S(2)}, u32[]{:S(2)}) %collective-permute-start) | collective-permute-done | bytes 221216 | tf_op jit(solution)/shard_map/ppermute | solution.py:18
  11.9 1.5 %collective-permute-done.1.refs_3_.refs_1_ = bf16[96,896]{1,0:T(8,128)(2,1)S(1)} collective-permute-done((bf16[96,896]{1,0:T(8,128)(2,1)}, bf16[96,896]{1,0:T(8,128)(2,1)S(1)}, u32[]{:S(2)}, u32[]{:S(2)}) %collective-permute-start.1) | collective-permute-done | bytes 172064 | tf_op jit(solution)/shard_map/ppermute | solution.py:18
  16.8 5.1 %all-to-all-start = ((bf16[8,48,512]{2,1,0:T(8,128)(2,1)}), bf16[8,48,512]{2,1,0:T(8,128)(2,1)S(1)}, u32[]{:S(2)}, u32[]{:S(2)}) async-start(bf16[8,48,512]{2,1,0:T(8,128)(2,1)} %bitcast.3), calls=%async_computation | async-start | bytes 786432 | tf_op jit(solution)/shard_map/all_to_all | solution.py:175
  21.9 2.5 %collective-permute-start.3 = (bf16[256,256]{1,0:T(8,128)(2,1)S(1)}, bf16[256,256]{1,0:T(8,128)(2,1)S(1)}, u32[]{:S(2)}, u32[]{:S(2)}) collective-permute-start(bf16[256,256]{1,0:T(8,128)(2,1)S(1)} %copy-done.2), channel_id=1, source_target_pairs={{0,16},{16,0},{1,17},{17,1},{2,18},{18,2},{3,19},{19,3},{4,20},{20... | collective-permute-start | bytes 393224 | tf_op jit(solution)/shard_map/ppermute | solution.py:18
  24.4 4.6 %collective-permute-done.3.refs_2_.refs_3_ = bf16[256,256]{1,0:T(8,128)(2,1)S(1)} collective-permute-done((bf16[256,256]{1,0:T(8,128)(2,1)S(1)}, bf16[256,256]{1,0:T(8,128)(2,1)S(1)}, u32[]{:S(2)}, u32[]{:S(2)}) %collective-permute-start.3) | collective-permute-done | bytes 131104 | tf_op jit(solution)/shard_map/ppermute | solution.py:18
  29.1 5.6 %collective-permute-start.4 = (bf16[384,512]{1,0:T(8,128)(2,1)S(1)}, bf16[384,512]{1,0:T(8,128)(2,1)S(1)}, u32[]{:S(2)}, u32[]{:S(2)}) collective-permute-start(bf16[384,512]{1,0:T(8,128)(2,1)S(1)} %shard_map.49.refs_0_), channel_id=1, source_target_pairs={{0,1},{1,0},{2,3},{3,2},{4,5},{5,4},{6,7},{7,6},{8,9},{9,8},{10,11... | collective-permute-start | bytes 1179656 | tf_op jit(solution)/shard_map/ppermute | solution.py:18
  35.4 1.5 %collective-permute-start.20 = (bf16[96,1792]{1,0:T(8,128)(2,1)S(1)}, bf16[96,1792]{1,0:T(8,128)(2,1)S(1)}, u32[]{:S(2)}, u32[]{:S(2)}) collective-permute-start(bf16[96,1792]{1,0:T(8,128)(2,1)S(1)} %collective-permute-done.9.refs_6_), channel_id=1, source_target_pairs={{0,32},{1,225},{32,64},{33,1},{64,96},{65,33},{96,128},{97,65},{12... | collective-permute-start | bytes 1032200 | tf_op jit(solution)/shard_map/ppermute | solution.py:63
  38.0 6.5 %all-to-all-start.1 = ((bf16[8,96,256]{2,1,0:T(8,128)(2,1)}), bf16[8,96,256]{2,1,0:T(8,128)(2,1)S(1)}, u32[]{:S(2)}, u32[]{:S(2)}) async-start(bf16[8,96,256]{2,1,0:T(8,128)(2,1)} %bitcast.5), calls=%async_computation.1 | async-start | bytes 786432 | tf_op jit(solution)/shard_map/all_to_all | solution.py:175
  45.6 1.9 %collective-permute-start.22 = (bf16[96,1792]{1,0:T(8,128)(2,1)S(1)}, bf16[96,1792]{1,0:T(8,128)(2,1)S(1)}, u32[]{:S(2)}, u32[]{:S(2)}) collective-permute-start(bf16[96,1792]{1,0:T(8,128)(2,1)S(1)} %collective-permute-done.20.refs_2_), channel_id=1, source_target_pairs={{1,225},{33,1},{65,33},{97,65},{129,97},{161,129},{193,161},{225,1... | collective-permute-start | bytes 1032200 | tf_op jit(solution)/shard_map/ppermute | solution.py:63
  47.6 5.8 %shard_map.53 = (bf16[768,896]{1,0:T(8,128)(2,1)}, f32[8,128]{1,0:T(8,128)S(1)}) custom-call(s32[3]{0:T(128)S(1)} %pad_add_fusion.refs_0_, bf16[96,1792]{1,0:T(8,128)(2,1)S(1)} %shard_map.48.refs_1_, bf16[96,1792]{1,0:T(8,128)(2,1)S(1)} %shard_map.52.refs_2_, bf16[96,1792]{1,0:T(8,128)(2,1)S(1)} %collective-permute-done.2.refs_1_.refs_3_, ...), custom_call_target="tpu_custom_call" | custom-call | flops 1541406720 | bytes 5000000 | tf_op jit(solution)/shard_map/pallas_call | solution.py:34
  53.4 6.8 %collective-permute-done.6.refs_0_ = bf16[96,1792]{1,0:T(8,128)(2,1)S(1)} collective-permute-done((bf16[96,1792]{1,0:T(8,128)(2,1)S(1)}, bf16[96,1792]{1,0:T(8,128)(2,1)S(1)}, u32[]{:S(2)}, u32[]{:S(2)}) %collective-permute-start.6) | collective-permute-done | bytes 344096 | tf_op jit(solution)/shard_map/ppermute | solution.py:63
  62.1 3.4 %collective-permute-done.11.refs_8_ = bf16[96,256]{1,0:T(8,128)(2,1)S(1)} collective-permute-done((bf16[96,256]{1,0:T(8,128)(2,1)S(1)}, bf16[96,256]{1,0:T(8,128)(2,1)S(1)}, u32[]{:S(2)}, u32[]{:S(2)}) %collective-permute-start.11) | collective-permute-done | bytes 49184 | tf_op jit(solution)/shard_map/ppermute | solution.py:18
  65.4 5.3 %shard_map.56 = (bf16[768,896]{1,0:T(8,128)(2,1)}, f32[8,128]{1,0:T(8,128)}) custom-call(s32[3]{0:T(128)S(1)} %pad_add_fusion.refs_0_, bf16[96,1792]{1,0:T(8,128)(2,1)S(1)} %shard_map.54.refs_1_, bf16[96,1792]{1,0:T(8,128)(2,1)S(1)} %collective-permute-done.20.refs_2_, ...), custom_call_target="tpu_custom_call", output_to_operand_aliasing={{0}: (7, {})} | custom-call | flops 924844032 | bytes 5000000 | tf_op jit(solution)/shard_map/pallas_call | solution.py:34
  70.7 4.5 %all-to-all-start.2 = ((bf16[8,96,896]{2,1,0:T(8,128)(2,1)}), bf16[8,96,896]{2,1,0:T(8,128)(2,1)S(1)}, u32[]{:S(2)}, u32[]{:S(2)}) async-start(bf16[8,96,896]{2,1,0:T(8,128)(2,1)} %bitcast.37), calls=%async_computation.2 | async-start | bytes 2752512 | tf_op jit(solution)/shard_map/all_to_all | solution.py:175
  75.6 3.6 %collective-permute-start.15 = (bf16[192,256]{1,0:T(8,128)(2,1)S(1)}, bf16[192,256]{1,0:T(8,128)(2,1)S(1)}, u32[]{:S(2)}, u32[]{:S(2)}) collective-permute-start(bf16[192,256]{1,0:T(8,128)(2,1)S(1)} %pad_maximum_fusion), channel_id=1, source_target_pairs={{0,64},{32,96},{64,128},{96,160},{128,192},{160,224},{192,0},{224,... | collective-permute-start | bytes 294920 | tf_op jit(solution)/shard_map/ppermute | solution.py:14
  83.0 5.7 %all-to-all-done.2 = bf16[8,96,896]{2,1,0:T(8,128)(2,1)S(1)} async-done(((bf16[8,96,896]{2,1,0:T(8,128)(2,1)}), bf16[8,96,896]{2,1,0:T(8,128)(2,1)S(1)}, u32[]{:S(2)}, u32[]{:S(2)}) %all-to-all-start.2) | async-done | bytes 1376288 | tf_op jit(solution)/shard_map/all_to_all | solution.py:175
  90.0 8.1 %all-to-all-start.3 = ((bf16[8,96,896]{2,1,0:T(8,128)(2,1)}), bf16[8,96,896]{2,1,0:T(8,128)(2,1)S(1)}, u32[]{:S(2)}, u32[]{:S(2)}) async-start(bf16[8,96,896]{2,1,0:T(8,128)(2,1)} %bitcast.18), calls=%async_computation.3 | async-start | bytes 2752512 | tf_op jit(solution)/shard_map/all_to_all | solution.py:175
  98.0 2.7 %collective-permute-start.16 = (bf16[192,256]{1,0:T(8,128)(2,1)S(1)}, bf16[192,256]{1,0:T(8,128)(2,1)S(1)}, u32[]{:S(2)}, u32[]{:S(2)}) collective-permute-start(bf16[192,256]{1,0:T(8,128)(2,1)S(1)} %collective-permute-done.15.refs_3_), channel_id=1, source_target_pairs={{0,32},{32,64},{64,96},{96,128},{128,160},{160,192},{192,224},{224... | collective-permute-start | bytes 294920 | tf_op jit(solution)/shard_map/ppermute | solution.py:14
  100.7 2.4 %collective-permute-start.19 = (bf16[192,128]{1,0:T(8,128)(2,1)S(1)}, bf16[192,128]{1,0:T(8,128)(2,1)S(1)}, u32[]{:S(2)}, u32[]{:S(2)}) collective-permute-start(bf16[192,128]{1,0:T(8,128)(2,1)S(1)} %slice.9), channel_id=1, source_target_pairs={{0,192},{32,224},{64,0},{96,32},{128,64},{160,96},{192,128},{224,1... | collective-permute-start | bytes 147464 | tf_op jit(solution)/shard_map/ppermute | solution.py:14
  103.1 1.8 %collective-permute-done.18.refs_3_ = bf16[192,128]{1,0:T(8,128)(2,1)S(1)} collective-permute-done((bf16[192,128]{1,0:T(8,128)(2,1)S(1)}, bf16[192,128]{1,0:T(8,128)(2,1)S(1)}, u32[]{:S(2)}, u32[]{:S(2)}) %collective-permute-start.18) | collective-permute-done | bytes 49184 | tf_op jit(solution)/shard_map/ppermute | solution.py:14
  106.2 10.3 %all-to-all-done.3 = bf16[8,96,896]{2,1,0:T(8,128)(2,1)S(1)} async-done(((bf16[8,96,896]{2,1,0:T(8,128)(2,1)}), bf16[8,96,896]{2,1,0:T(8,128)(2,1)S(1)}, u32[]{:S(2)}, u32[]{:S(2)}) %all-to-all-start.3) | async-done | bytes 1376288 | tf_op jit(solution)/shard_map/all_to_all | solution.py:175
  117.3 2.8 %collective-permute-done.23 = bf16[768,896]{1,0:T(8,128)(2,1)S(1)} collective-permute-done((bf16[768,896]{1,0:T(8,128)(2,1)S(1)}, bf16[768,896]{1,0:T(8,128)(2,1)S(1)}, u32[]{:S(2)}, u32[]{:S(2)}) %collective-permute-start.23) | collective-permute-done | bytes 1376288 | tf_op jit(solution)/shard_map/ppermute | solution.py:18
  120.1 2.9 %shard_map.59 = f32[256,896]{1,0:T(8,128)} custom-call(s32[3]{0:T(128)S(1)} %pad_add_fusion.refs_0_, bf16[2,2,48,256]{3,2,1,0:T(8,128)(2,1)S(1)} %bitcast.34, bf16[2,2,48,256]{3,2,1,0:T(8,128)(2,1)S(1)} %bitcast.30, bf16[2,2,48,256]{3,2,1,0:T(8,128)(2,1)S(1)} %bitcast.28, bf16[2,2,48,256]{3,2,1,0:T(8,128)(2,1)S(1)} %bitcast.32, ...), custom_call_target="tpu_custom_call" | custom-call | flops 703000000 | bytes 5000000 | tf_op jit(solution)/shard_map/pallas_call | solution.py:34
  (58 shorter events, 19.0 us)
Async XLA Ops:
  0.0 47.6 %collective-permute-start.10 = (bf16[896,896]{1,0:T(8,128)(2,1)}, bf16[896,896]{1,0:T(8,128)(2,1)}, u32[]{:S(2)}, u32[]{:S(2)}) collective-permute-start(bf16[896,896]{1,0:T(8,128)(2,1)} %refs_5_.1), channel_id=1, source_target_pairs={{0,1},{1,0},{2,3},{3,2},{4,5},{5,4},{6,7},{7,6},{8,9},{9,8},{10,11... | collective-permute-start | bytes 4816904 | tf_op jit(solution)/shard_map/ppermute | solution.py:18
  2.4 8.6 %collective-permute-start = (bf16[96,1152]{1,0:T(8,128)(2,1)S(1)}, bf16[96,1152]{1,0:T(8,128)(2,1)S(1)}, u32[]{:S(2)}, u32[]{:S(2)}) collective-permute-start(bf16[96,1152]{1,0:T(8,128)(2,1)S(1)} %shard_map.46), channel_id=1, source_target_pairs={{0,16},{16,0},{1,17},{17,1},{2,18},{18,2},{3,19},{19,3},{4,20},{20... | collective-permute-start | bytes 663560 | tf_op jit(solution)/shard_map/ppermute | solution.py:18
  11.1 4.5 %collective-permute-start.7 = (bf16[96,1152]{1,0:T(8,128)(2,1)S(1)}, bf16[96,1152]{1,0:T(8,128)(2,1)S(1)}, u32[]{:S(2)}, u32[]{:S(2)}) collective-permute-start(bf16[96,1152]{1,0:T(8,128)(2,1)S(1)} %collective-permute-done.refs_2_.refs_0_), channel_id=1, source_target_pairs={{0,1},{1,0},{2,3},{3,2},{4,5},{5,4},{6,7},{7,6},{8,9},{9,8},{10,11... | collective-permute-start | bytes 663560 | tf_op jit(solution)/shard_map/ppermute | solution.py:18
  15.6 8.8 %collective-permute-start.8 = (bf16[96,1792]{1,0:T(8,128)(2,1)S(1)}, bf16[96,1792]{1,0:T(8,128)(2,1)S(1)}, u32[]{:S(2)}, u32[]{:S(2)}) collective-permute-start(bf16[96,1792]{1,0:T(8,128)(2,1)S(1)} %shard_map.52.refs_2_), channel_id=1, source_target_pairs={{0,32},{1,225},{32,64},{33,1},{64,96},{65,33},{96,128},{97,65},{12... | collective-permute-start | bytes 1032200 | tf_op jit(solution)/shard_map/ppermute | solution.py:63
  16.7 12.4 %collective-permute-start.2 = (bf16[96,1792]{1,0:T(8,128)(2,1)S(1)}, bf16[96,1792]{1,0:T(8,128)(2,1)S(1)}, u32[]{:S(2)}, u32[]{:S(2)}) collective-permute-start(bf16[96,1792]{1,0:T(8,128)(2,1)S(1)} %shard_map.48.refs_1_), channel_id=1, source_target_pairs={{0,32},{1,225},{32,64},{33,1},{64,96},{65,33},{96,128},{97,65},{12... | collective-permute-start | bytes 1032200 | tf_op jit(solution)/shard_map/ppermute | solution.py:63
  16.8 12.3 %all-to-all-start = ((bf16[8,48,512]{2,1,0:T(8,128)(2,1)}), bf16[8,48,512]{2,1,0:T(8,128)(2,1)S(1)}, u32[]{:S(2)}, u32[]{:S(2)}) async-start(bf16[8,48,512]{2,1,0:T(8,128)(2,1)} %bitcast.3), calls=%async_computation | async-start | bytes 786432 | tf_op jit(solution)/shard_map/all_to_all | solution.py:175
  21.9 7.2 %collective-permute-start.3 = (bf16[256,256]{1,0:T(8,128)(2,1)S(1)}, bf16[256,256]{1,0:T(8,128)(2,1)S(1)}, u32[]{:S(2)}, u32[]{:S(2)}) collective-permute-start(bf16[256,256]{1,0:T(8,128)(2,1)S(1)} %copy-done.2), channel_id=1, source_target_pairs={{0,16},{16,0},{1,17},{17,1},{2,18},{18,2},{3,19},{19,3},{4,20},{20... | collective-permute-start | bytes 393224 | tf_op jit(solution)/shard_map/ppermute | solution.py:18
  24.4 10.9 %collective-permute-start.9 = (bf16[96,1792]{1,0:T(8,128)(2,1)S(1)}, bf16[96,1792]{1,0:T(8,128)(2,1)S(1)}, u32[]{:S(2)}, u32[]{:S(2)}) collective-permute-start(bf16[96,1792]{1,0:T(8,128)(2,1)S(1)} %collective-permute-done.8.refs_4_), channel_id=1, source_target_pairs={{0,32},{1,225},{32,64},{33,1},{64,96},{65,33},{96,128},{97,65},{12... | collective-permute-start | bytes 1032200 | tf_op jit(solution)/shard_map/ppermute | solution.py:63
  29.1 7.8 %collective-permute-start.4 = (bf16[384,512]{1,0:T(8,128)(2,1)S(1)}, bf16[384,512]{1,0:T(8,128)(2,1)S(1)}, u32[]{:S(2)}, u32[]{:S(2)}) collective-permute-start(bf16[384,512]{1,0:T(8,128)(2,1)S(1)} %shard_map.49.refs_0_), channel_id=1, source_target_pairs={{0,1},{1,0},{2,3},{3,2},{4,5},{5,4},{6,7},{7,6},{8,9},{9,8},{10,11... | collective-permute-start | bytes 1179656 | tf_op jit(solution)/shard_map/ppermute | solution.py:18
  34.6 9.8 %collective-permute-start.5 = (bf16[96,1792]{1,0:T(8,128)(2,1)S(1)}, bf16[96,1792]{1,0:T(8,128)(2,1)S(1)}, u32[]{:S(2)}, u32[]{:S(2)}) collective-permute-start(bf16[96,1792]{1,0:T(8,128)(2,1)S(1)} %collective-permute-done.2.refs_1_.refs_3_), channel_id=1, source_target_pairs={{0,32},{1,225},{32,64},{33,1},{64,96},{65,33},{96,128},{97,65},{12... | collective-permute-start | bytes 1032200 | tf_op jit(solution)/shard_map/ppermute | solution.py:63
  35.4 10.3 %collective-permute-start.20 = (bf16[96,1792]{1,0:T(8,128)(2,1)S(1)}, bf16[96,1792]{1,0:T(8,128)(2,1)S(1)}, u32[]{:S(2)}, u32[]{:S(2)}) collective-permute-start(bf16[96,1792]{1,0:T(8,128)(2,1)S(1)} %collective-permute-done.9.refs_6_), channel_id=1, source_target_pairs={{0,32},{1,225},{32,64},{33,1},{64,96},{65,33},{96,128},{97,65},{12... | collective-permute-start | bytes 1032200 | tf_op jit(solution)/shard_map/ppermute | solution.py:63
  38.0 22.8 %all-to-all-start.1 = ((bf16[8,96,256]{2,1,0:T(8,128)(2,1)}), bf16[8,96,256]{2,1,0:T(8,128)(2,1)S(1)}, u32[]{:S(2)}, u32[]{:S(2)}) async-start(bf16[8,96,256]{2,1,0:T(8,128)(2,1)} %bitcast.5), calls=%async_computation.1 | async-start | bytes 786432 | tf_op jit(solution)/shard_map/all_to_all | solution.py:175
  44.5 15.7 %collective-permute-start.6 = (bf16[96,1792]{1,0:T(8,128)(2,1)S(1)}, bf16[96,1792]{1,0:T(8,128)(2,1)S(1)}, u32[]{:S(2)}, u32[]{:S(2)}) collective-permute-start(bf16[96,1792]{1,0:T(8,128)(2,1)S(1)} %shard_map.51.refs_5_), channel_id=1, source_target_pairs={{0,32},{1,225},{32,64},{33,1},{64,96},{65,33},{96,128},{97,65},{12... | collective-permute-start | bytes 1032200 | tf_op jit(solution)/shard_map/ppermute | solution.py:63
  45.6 19.8 %collective-permute-start.22 = (bf16[96,1792]{1,0:T(8,128)(2,1)S(1)}, bf16[96,1792]{1,0:T(8,128)(2,1)S(1)}, u32[]{:S(2)}, u32[]{:S(2)}) collective-permute-start(bf16[96,1792]{1,0:T(8,128)(2,1)S(1)} %collective-permute-done.20.refs_2_), channel_id=1, source_target_pairs={{1,225},{33,1},{65,33},{97,65},{129,97},{161,129},{193,161},{225,1... | collective-permute-start | bytes 1032200 | tf_op jit(solution)/shard_map/ppermute | solution.py:63
  60.1 5.3 %collective-permute-start.21 = (bf16[96,1792]{1,0:T(8,128)(2,1)S(1)}, bf16[96,1792]{1,0:T(8,128)(2,1)S(1)}, u32[]{:S(2)}, u32[]{:S(2)}) collective-permute-start(bf16[96,1792]{1,0:T(8,128)(2,1)S(1)} %shard_map.54.refs_1_), channel_id=1, source_target_pairs={{0,32},{32,64},{64,96},{96,128},{128,160},{160,192},{192,224},{224... | collective-permute-start | bytes 1032200 | tf_op jit(solution)/shard_map/ppermute | solution.py:63
  60.9 4.5 %collective-permute-start.11 = (bf16[96,256]{1,0:T(8,128)(2,1)S(1)}, bf16[96,256]{1,0:T(8,128)(2,1)S(1)}, u32[]{:S(2)}, u32[]{:S(2)}) collective-permute-start(bf16[96,256]{1,0:T(8,128)(2,1)S(1)} %shard_map.55), channel_id=1, source_target_pairs={{0,16},{16,0},{1,17},{17,1},{2,18},{18,2},{3,19},{19,3},{4,20},{20... | collective-permute-start | bytes 147464 | tf_op jit(solution)/shard_map/ppermute | solution.py:18
  70.7 17.9 %all-to-all-start.2 = ((bf16[8,96,896]{2,1,0:T(8,128)(2,1)}), bf16[8,96,896]{2,1,0:T(8,128)(2,1)S(1)}, u32[]{:S(2)}, u32[]{:S(2)}) async-start(bf16[8,96,896]{2,1,0:T(8,128)(2,1)} %bitcast.37), calls=%async_computation.2 | async-start | bytes 2752512 | tf_op jit(solution)/shard_map/all_to_all | solution.py:175
  75.3 5.3 %collective-permute-start.12 = (bf16[192,256]{1,0:T(8,128)(2,1)S(1)}, bf16[192,256]{1,0:T(8,128)(2,1)S(1)}, u32[]{:S(2)}, u32[]{:S(2)}) collective-permute-start(bf16[192,256]{1,0:T(8,128)(2,1)S(1)} %pad_maximum_fusion), channel_id=1, source_target_pairs={{0,224},{32,0},{64,32},{96,64},{128,96},{160,128},{192,160},{224,1... | collective-permute-start | bytes 294920 | tf_op jit(solution)/shard_map/ppermute | solution.py:14
  75.5 5.8 %collective-permute-start.13 = (bf16[192,256]{1,0:T(8,128)(2,1)S(1)}, bf16[192,256]{1,0:T(8,128)(2,1)S(1)}, u32[]{:S(2)}, u32[]{:S(2)}) collective-permute-start(bf16[192,256]{1,0:T(8,128)(2,1)S(1)} %pad_maximum_fusion), channel_id=1, source_target_pairs={{0,192},{32,224},{64,0},{96,32},{128,64},{160,96},{192,128},{224,1... | collective-permute-start | bytes 294920 | tf_op jit(solution)/shard_map/ppermute | solution.py:14
  75.6 6.1 %collective-permute-start.15 = (bf16[192,256]{1,0:T(8,128)(2,1)S(1)}, bf16[192,256]{1,0:T(8,128)(2,1)S(1)}, u32[]{:S(2)}, u32[]{:S(2)}) collective-permute-start(bf16[192,256]{1,0:T(8,128)(2,1)S(1)} %pad_maximum_fusion), channel_id=1, source_target_pairs={{0,64},{32,96},{64,128},{96,160},{128,192},{160,224},{192,0},{224,... | collective-permute-start | bytes 294920 | tf_op jit(solution)/shard_map/ppermute | solution.py:14
  90.0 26.5 %all-to-all-start.3 = ((bf16[8,96,896]{2,1,0:T(8,128)(2,1)}), bf16[8,96,896]{2,1,0:T(8,128)(2,1)S(1)}, u32[]{:S(2)}, u32[]{:S(2)}) async-start(bf16[8,96,896]{2,1,0:T(8,128)(2,1)} %bitcast.18), calls=%async_computation.3 | async-start | bytes 2752512 | tf_op jit(solution)/shard_map/all_to_all | solution.py:175
  98.0 8.1 %collective-permute-start.14 = (bf16[192,256]{1,0:T(8,128)(2,1)S(1)}, bf16[192,256]{1,0:T(8,128)(2,1)S(1)}, u32[]{:S(2)}, u32[]{:S(2)}) collective-permute-start(bf16[192,256]{1,0:T(8,128)(2,1)S(1)} %collective-permute-done.13.refs_4_), channel_id=1, source_target_pairs={{0,224},{32,0},{64,32},{96,64},{128,96},{160,128},{192,160},{224,1... | collective-permute-start | bytes 294920 | tf_op jit(solution)/shard_map/ppermute | solution.py:14
  98.0 8.1 %collective-permute-start.16 = (bf16[192,256]{1,0:T(8,128)(2,1)S(1)}, bf16[192,256]{1,0:T(8,128)(2,1)S(1)}, u32[]{:S(2)}, u32[]{:S(2)}) collective-permute-start(bf16[192,256]{1,0:T(8,128)(2,1)S(1)} %collective-permute-done.15.refs_3_), channel_id=1, source_target_pairs={{0,32},{32,64},{64,96},{96,128},{128,160},{160,192},{192,224},{224... | collective-permute-start | bytes 294920 | tf_op jit(solution)/shard_map/ppermute | solution.py:14
  100.7 5.4 %collective-permute-start.19 = (bf16[192,128]{1,0:T(8,128)(2,1)S(1)}, bf16[192,128]{1,0:T(8,128)(2,1)S(1)}, u32[]{:S(2)}, u32[]{:S(2)}) collective-permute-start(bf16[192,128]{1,0:T(8,128)(2,1)S(1)} %slice.9), channel_id=1, source_target_pairs={{0,192},{32,224},{64,0},{96,32},{128,64},{160,96},{192,128},{224,1... | collective-permute-start | bytes 147464 | tf_op jit(solution)/shard_map/ppermute | solution.py:14
  (8 other events, 30.1 us)

commit v5 on v4

--- a/solution.py
+++ b/solution.py
@@ -76,7 +76,7 @@
     return call(body, out, arrays, [VMEM] * len(arrays), after, out_specs=VMEM)
 
 
-def rotate(where, blocks, bases, start, total, sums=(), after=()):
+def rotate(where, blocks, bases, start, total, sums=(), after=(), fetch=True):
     parts = [block if isinstance(block, tuple) else (block,) for block in blocks]
     rows, depth, width = parts[0][0].shape[0], bases[0].shape[0], bases[0].shape[1]
     count, many = len(parts), sum(len(part) for part in parts)
@@ -84,7 +84,7 @@
     def body(where, *refs):
         refs, bases, (out, token, x, base, result, sems, out_sems, base_sems) = list(refs[:many]), refs[many : many + 2], refs[-8:]
         copies, slab = [], depth // 7
-        for k in range(14):
+        for k in range(14 if fetch else 0):
             source = bases[k // 7].at[pl.ds(k % 7 * slab, slab)]
             copies.append(pltpu.make_async_copy(source, base.at[pl.ds(k * slab, slab)], base_sems.at[k]))
             copies[-1].start()
@@ -103,7 +103,8 @@
             refs = refs[len(part) :]
         for copy in copies:
             copy.wait()
-        result[...] = dot(x[...], base[...]).astype(result.dtype)
+        first, second = (base[:depth], base[depth:]) if fetch else (bases[0][...], bases[1][...])
+        result[...] = (dot(x[:, :depth], first) + dot(x[:, depth:], second)).astype(result.dtype)
         token[...] = jnp.zeros_like(token)
         copies = []
         for k in range(count):
@@ -116,14 +117,14 @@
     out = [jax.ShapeDtypeStruct((total, width), jnp.bfloat16), jax.ShapeDtypeStruct((8, 128), jnp.float32)]
     scratch = [
         pltpu.VMEM((count * rows, 2 * depth), jnp.bfloat16),
-        pltpu.VMEM((2 * depth, width), jnp.bfloat16),
+        pltpu.VMEM((2 * depth if fetch else 16, width), jnp.bfloat16),
         pltpu.VMEM((count * rows, width), jnp.bfloat16),
         pltpu.SemaphoreType.DMA((count,)),
         pltpu.SemaphoreType.DMA((count,)),
         pltpu.SemaphoreType.DMA((14,)),
     ]
     ins = [where, *(x for part in parts for x in part), *bases, *sums]
-    specs = [SMEM] + [ANY] * (len(ins) - 1)
+    specs = [SMEM] + [ANY] * many + [ANY if fetch else VMEM] * 2 + [ANY] * len(sums)
     flops = 4 * count * rows * depth * width
     more = {"input_output_aliases": {len(ins) - 1: 0}} if sums else {}
     return call(body, out, ins, specs, after, flops, 5 * 10**6, 52, out_specs=[ANY, VMEM], scratch_shapes=scratch, **more)
@@ -158,14 +159,14 @@
     return call(body, out, [own, other, *bases], [VMEM] * 4, after, 2 * 10**8, 2 * 10**6, out_specs=VMEM)
 
 
-def act_halves(where, mine, theirs, after=()):
-    half, depth = mine.shape[0] // 2, mine.shape[1]
+def act_halves(where, mine, theirs, depth, after=()):
+    half, width = mine.shape[0] // 2, mine.shape[1]
 
     def body(where, mine, theirs, out):
         start = pl.multiple_of(where[0] * half, half)
         for k in range(8):
-            out[k * half : (k + 1) * half, :depth] = mine[pl.ds(start, half)]
-            out[k * half : (k + 1) * half, depth:] = theirs[pl.ds(start, half), -depth:]
+            out[k * half : (k + 1) * half, :depth] = mine[pl.ds(start, half), width - depth :]
+            out[k * half : (k + 1) * half, depth:] = theirs[pl.ds(start, half), width - depth :]
 
     out = jax.ShapeDtypeStruct((8 * half, 2 * depth), mine.dtype)
     return call(body, out, [where, mine, theirs], [SMEM, VMEM, VMEM], after, out_specs=VMEM)
@@ -215,10 +216,11 @@
     cols = act_basis.shape[1]
 
     mate = swap(grad_outputs, "c")
-    theirs = swap(join(grad_outputs, activations), "xh")
+    mine = join(grad_outputs, activations)
+    theirs = swap(mine, "xh")
     act_basis2 = swap(act_basis, "xh")
     theirs_mate = swap(theirs, "c")
-    act_copies = act_halves(where, activations, theirs, (mate,))
+    act_copies = act_halves(where, mine, theirs, activations.shape[1])
     act_own = spread(act_copies, CHIPS)
     laps = [[join(grad_outputs, mate, after=(act_copies,)), join(theirs, theirs_mate, cols=width, after=(act_copies,))]]
     laps.append([lap(x) for x in laps[-1]])
@@ -236,7 +238,7 @@
     far = tuple(lap(x, core) for core, x in enumerate(laps[3]))
     act_half = summed(act_parts, 8, 1, laps[3][:1])
     act_mate = swap(act_half, "xh")
-    terms, _ = rotate(where, [*laps[3], far], bases, 5 * rows, 8 * rows, (early,), (act_mate,))
+    terms, _ = rotate(where, [*laps[3], far], bases, 5 * rows, 8 * rows, (early,), (act_mate,), False)
     parts = spread(terms, CHIPS)
     act_pair = jnp.concatenate([act_half, act_mate], axis=0)
     one = hop(act_pair, act_pair)

time: 124 us -> 121 us (0.976)
  waiting for transfers between devices: 47.1 us -> 45.4 us
    ppermute x8, waiting for transfers between devices: 18.1 us -> 16.4 us  [swap(): return lax.ppermute(x, axis, [(0, 1), (1, 0)])]
  transfers between devices with their start and end apart: 28 -> 28, of which waited for: 14 -> 14; matrix products, arithmetic and copies ran while one was open for 0% -> 0% of each run, Pallas kernels for 8% -> 9%
where the time goes in v5:
time: 121 us
  starting transfers between devices  54.3 us (45%)
  waiting for transfers between devices  45.4 us (38%)
  Pallas kernels  19.9 us (16%)
    all_to_all x4, starting transfers between devices, spread(): return lax.all_to_all(x, axis, 0, 0, tiled=True)  23.9 us
    pallas_call x14, Pallas kernels, call(): pl.pallas_call(kernel, out_shape=out, in_specs=list(specs) + [ANY] * len(...  19.9 us
    ppermute x8, waiting for transfers between devices, swap(): return lax.ppermute(x, axis, [(0, 1), (1, 0)])  16.4 us
    all_to_all x4, waiting for transfers between devices, spread(): return lax.all_to_all(x, axis, 0, 0, tiled=True)  16.4 us
    ppermute x8, starting transfers between devices, swap(): return lax.ppermute(x, axis, [(0, 1), (1, 0)])  14.8 us
    ppermute x8, starting transfers between devices, shift(): return lax.ppermute(x, axis, [(i, (i + by) % size) for i in range(size)])  10.1 us
    ppermute x8, waiting for transfers between devices, lap(): lax.ppermute(x, ('z', 'c'), [(2 * z + c, 2 * to + c) for z, c, to in steps])  7.4 us
    ppermute x8, starting transfers between devices, lap(): lax.ppermute(x, ('z', 'c'), [(2 * z + c, 2 * to + c) for z, c, to in steps])  5.41 us
  transfers between devices with their start and end apart: 28, of which 14 were waited for; matrix products, arithmetic and copies ran while one was open for 0% of the time, Pallas kernels for 9%

profile of v5, /device:TPU:97, one launch (start us, length us, event | category | flops | bytes accessed | tf_op | source)
XLA Modules:
  0.0 120.7 jit_solution(17599165946545876838)
XLA Ops:
  2.4 2.8 %collective-permute-start = (bf16[96,1152]{1,0:T(8,128)(2,1)S(1)}, bf16[96,1152]{1,0:T(8,128)(2,1)S(1)}, u32[]{:S(2)}, u32[]{:S(2)}) collective-permute-start(bf16[96,1152]{1,0:T(8,128)(2,1)S(1)} %shard_map.46.refs_1_), channel_id=1, source_target_pairs={{0,16},{16,0},{1,17},{17,1},{2,18},{18,2},{3,19},{19,3},{4,20},{20... | collective-permute-start | bytes 663560 | tf_op jit(solution)/shard_map/ppermute | solution.py:18
  5.2 5.8 %collective-permute-done.refs_2_.refs_0_ = bf16[96,1152]{1,0:T(8,128)(2,1)S(1)} collective-permute-done((bf16[96,1152]{1,0:T(8,128)(2,1)S(1)}, bf16[96,1152]{1,0:T(8,128)(2,1)S(1)}, u32[]{:S(2)}, u32[]{:S(2)}) %collective-permute-start) | collective-permute-done | bytes 221216 | tf_op jit(solution)/shard_map/ppermute | solution.py:18
  14.5 5.1 %all-to-all-start = ((bf16[8,48,512]{2,1,0:T(8,128)(2,1)}), bf16[8,48,512]{2,1,0:T(8,128)(2,1)S(1)}, u32[]{:S(2)}, u32[]{:S(2)}) async-start(bf16[8,48,512]{2,1,0:T(8,128)(2,1)} %bitcast.3), calls=%async_computation | async-start | bytes 786432 | tf_op jit(solution)/shard_map/all_to_all | solution.py:176
  19.6 2.5 %collective-permute-start.3 = (bf16[256,256]{1,0:T(8,128)(2,1)S(1)}, bf16[256,256]{1,0:T(8,128)(2,1)S(1)}, u32[]{:S(2)}, u32[]{:S(2)}) collective-permute-start(bf16[256,256]{1,0:T(8,128)(2,1)S(1)} %copy-done), channel_id=1, source_target_pairs={{0,16},{16,0},{1,17},{17,1},{2,18},{18,2},{3,19},{19,3},{4,20},{20... | collective-permute-start | bytes 393224 | tf_op jit(solution)/shard_map/ppermute | solution.py:18
  22.2 4.6 %collective-permute-done.3.refs_2_.refs_3_ = bf16[256,256]{1,0:T(8,128)(2,1)S(1)} collective-permute-done((bf16[256,256]{1,0:T(8,128)(2,1)S(1)}, bf16[256,256]{1,0:T(8,128)(2,1)S(1)}, u32[]{:S(2)}, u32[]{:S(2)}) %collective-permute-start.3) | collective-permute-done | bytes 131104 | tf_op jit(solution)/shard_map/ppermute | solution.py:18
  26.8 5.7 %collective-permute-start.4 = (bf16[384,512]{1,0:T(8,128)(2,1)S(1)}, bf16[384,512]{1,0:T(8,128)(2,1)S(1)}, u32[]{:S(2)}, u32[]{:S(2)}) collective-permute-start(bf16[384,512]{1,0:T(8,128)(2,1)S(1)} %shard_map.49.refs_0_), channel_id=1, source_target_pairs={{0,1},{1,0},{2,3},{3,2},{4,5},{5,4},{6,7},{7,6},{8,9},{9,8},{10,11... | collective-permute-start | bytes 1179656 | tf_op jit(solution)/shard_map/ppermute | solution.py:18
  33.3 1.6 %collective-permute-start.20 = (bf16[96,1792]{1,0:T(8,128)(2,1)S(1)}, bf16[96,1792]{1,0:T(8,128)(2,1)S(1)}, u32[]{:S(2)}, u32[]{:S(2)}) collective-permute-start(bf16[96,1792]{1,0:T(8,128)(2,1)S(1)} %collective-permute-done.9.refs_6_), channel_id=1, source_target_pairs={{0,32},{1,225},{32,64},{33,1},{64,96},{65,33},{96,128},{97,65},{12... | collective-permute-start | bytes 1032200 | tf_op jit(solution)/shard_map/ppermute | solution.py:63
  36.0 6.2 %all-to-all-start.1 = ((bf16[8,96,256]{2,1,0:T(8,128)(2,1)}), bf16[8,96,256]{2,1,0:T(8,128)(2,1)S(1)}, u32[]{:S(2)}, u32[]{:S(2)}) async-start(bf16[8,96,256]{2,1,0:T(8,128)(2,1)} %bitcast.5), calls=%async_computation.1 | async-start | bytes 786432 | tf_op jit(solution)/shard_map/all_to_all | solution.py:176
  43.5 1.9 %collective-permute-start.22 = (bf16[96,1792]{1,0:T(8,128)(2,1)S(1)}, bf16[96,1792]{1,0:T(8,128)(2,1)S(1)}, u32[]{:S(2)}, u32[]{:S(2)}) collective-permute-start(bf16[96,1792]{1,0:T(8,128)(2,1)S(1)} %collective-permute-done.20.refs_2_), channel_id=1, source_target_pairs={{1,225},{33,1},{65,33},{97,65},{129,97},{161,129},{193,161},{225,1... | collective-permute-start | bytes 1032200 | tf_op jit(solution)/shard_map/ppermute | solution.py:63
  45.5 6.0 %shard_map.53 = (bf16[768,896]{1,0:T(8,128)(2,1)}, f32[8,128]{1,0:T(8,128)S(1)}) custom-call(s32[3]{0:T(128)S(1)} %pad_add_fusion.refs_0_, bf16[96,1792]{1,0:T(8,128)(2,1)S(1)} %shard_map.48.refs_1_, bf16[96,1792]{1,0:T(8,128)(2,1)S(1)} %shard_map.52.refs_2_, bf16[96,1792]{1,0:T(8,128)(2,1)S(1)} %collective-permute-done.2.refs_1_.refs_3_, ...), custom_call_target="tpu_custom_call" | custom-call | flops 1541406720 | bytes 5000000 | tf_op jit(solution)/shard_map/pallas_call | solution.py:34
  51.4 6.3 %collective-permute-done.6.refs_0_ = bf16[96,1792]{1,0:T(8,128)(2,1)S(1)} collective-permute-done((bf16[96,1792]{1,0:T(8,128)(2,1)S(1)}, bf16[96,1792]{1,0:T(8,128)(2,1)S(1)}, u32[]{:S(2)}, u32[]{:S(2)}) %collective-permute-start.6) | collective-permute-done | bytes 344096 | tf_op jit(solution)/shard_map/ppermute | solution.py:63
  58.5 1.4 %collective-permute-start.11 = (bf16[96,256]{1,0:T(8,128)(2,1)S(1)}, bf16[96,256]{1,0:T(8,128)(2,1)S(1)}, u32[]{:S(2)}, u32[]{:S(2)}) collective-permute-start(bf16[96,256]{1,0:T(8,128)(2,1)S(1)} %shard_map.55), channel_id=1, source_target_pairs={{0,16},{16,0},{1,17},{17,1},{2,18},{18,2},{3,19},{19,3},{4,20},{20... | collective-permute-start | bytes 147464 | tf_op jit(solution)/shard_map/ppermute | solution.py:18
  59.9 3.1 %collective-permute-done.11.refs_8_ = bf16[96,256]{1,0:T(8,128)(2,1)S(1)} collective-permute-done((bf16[96,256]{1,0:T(8,128)(2,1)S(1)}, bf16[96,256]{1,0:T(8,128)(2,1)S(1)}, u32[]{:S(2)}, u32[]{:S(2)}) %collective-permute-start.11) | collective-permute-done | bytes 49184 | tf_op jit(solution)/shard_map/ppermute | solution.py:18
  63.1 5.4 %shard_map.56 = (bf16[768,896]{1,0:T(8,128)(2,1)}, f32[8,128]{1,0:T(8,128)}) custom-call(s32[3]{0:T(128)S(1)} %pad_add_fusion.refs_0_, bf16[96,1792]{1,0:T(8,128)(2,1)S(1)} %shard_map.54.refs_1_, bf16[96,1792]{1,0:T(8,128)(2,1)S(1)} %collective-permute-done.20.refs_2_, ...), custom_call_target="tpu_custom_call", output_to_operand_aliasing={{0}: (7, {})} | custom-call | flops 924844032 | bytes 5000000 | tf_op jit(solution)/shard_map/pallas_call | solution.py:34
  68.5 4.6 %all-to-all-start.2 = ((bf16[8,96,896]{2,1,0:T(8,128)(2,1)}), bf16[8,96,896]{2,1,0:T(8,128)(2,1)S(1)}, u32[]{:S(2)}, u32[]{:S(2)}) async-start(bf16[8,96,896]{2,1,0:T(8,128)(2,1)} %bitcast.37), calls=%async_computation.2 | async-start | bytes 2752512 | tf_op jit(solution)/shard_map/all_to_all | solution.py:176
  73.2 3.6 %collective-permute-start.15 = (bf16[192,256]{1,0:T(8,128)(2,1)S(1)}, bf16[192,256]{1,0:T(8,128)(2,1)S(1)}, u32[]{:S(2)}, u32[]{:S(2)}) collective-permute-start(bf16[192,256]{1,0:T(8,128)(2,1)S(1)} %pad_maximum_fusion), channel_id=1, source_target_pairs={{0,64},{32,96},{64,128},{96,160},{128,192},{160,224},{192,0},{224,... | collective-permute-start | bytes 294920 | tf_op jit(solution)/shard_map/ppermute | solution.py:14
  80.4 6.1 %all-to-all-done.2 = bf16[8,96,896]{2,1,0:T(8,128)(2,1)S(1)} async-done(((bf16[8,96,896]{2,1,0:T(8,128)(2,1)}), bf16[8,96,896]{2,1,0:T(8,128)(2,1)S(1)}, u32[]{:S(2)}, u32[]{:S(2)}) %all-to-all-start.2) | async-done | bytes 1376288 | tf_op jit(solution)/shard_map/all_to_all | solution.py:176
  87.7 8.1 %all-to-all-start.3 = ((bf16[8,96,896]{2,1,0:T(8,128)(2,1)}), bf16[8,96,896]{2,1,0:T(8,128)(2,1)S(1)}, u32[]{:S(2)}, u32[]{:S(2)}) async-start(bf16[8,96,896]{2,1,0:T(8,128)(2,1)} %bitcast.18), calls=%async_computation.3 | async-start | bytes 2752512 | tf_op jit(solution)/shard_map/all_to_all | solution.py:176
  95.8 2.7 %collective-permute-start.16 = (bf16[192,256]{1,0:T(8,128)(2,1)S(1)}, bf16[192,256]{1,0:T(8,128)(2,1)S(1)}, u32[]{:S(2)}, u32[]{:S(2)}) collective-permute-start(bf16[192,256]{1,0:T(8,128)(2,1)S(1)} %collective-permute-done.15.refs_3_), channel_id=1, source_target_pairs={{0,32},{32,64},{64,96},{96,128},{128,160},{160,192},{192,224},{224... | collective-permute-start | bytes 294920 | tf_op jit(solution)/shard_map/ppermute | solution.py:14
  98.5 2.4 %collective-permute-start.19 = (bf16[192,128]{1,0:T(8,128)(2,1)S(1)}, bf16[192,128]{1,0:T(8,128)(2,1)S(1)}, u32[]{:S(2)}, u32[]{:S(2)}) collective-permute-start(bf16[192,128]{1,0:T(8,128)(2,1)S(1)} %slice.9), channel_id=1, source_target_pairs={{0,192},{32,224},{64,0},{96,32},{128,64},{160,96},{192,128},{224,1... | collective-permute-start | bytes 147464 | tf_op jit(solution)/shard_map/ppermute | solution.py:14
  100.8 1.8 %collective-permute-done.18.refs_3_ = bf16[192,128]{1,0:T(8,128)(2,1)S(1)} collective-permute-done((bf16[192,128]{1,0:T(8,128)(2,1)S(1)}, bf16[192,128]{1,0:T(8,128)(2,1)S(1)}, u32[]{:S(2)}, u32[]{:S(2)}) %collective-permute-start.18) | collective-permute-done | bytes 49184 | tf_op jit(solution)/shard_map/ppermute | solution.py:14
  103.9 10.3 %all-to-all-done.3 = bf16[8,96,896]{2,1,0:T(8,128)(2,1)S(1)} async-done(((bf16[8,96,896]{2,1,0:T(8,128)(2,1)}), bf16[8,96,896]{2,1,0:T(8,128)(2,1)S(1)}, u32[]{:S(2)}, u32[]{:S(2)}) %all-to-all-start.3) | async-done | bytes 1376288 | tf_op jit(solution)/shard_map/all_to_all | solution.py:176
  115.1 2.8 %collective-permute-done.23 = bf16[768,896]{1,0:T(8,128)(2,1)S(1)} collective-permute-done((bf16[768,896]{1,0:T(8,128)(2,1)S(1)}, bf16[768,896]{1,0:T(8,128)(2,1)S(1)}, u32[]{:S(2)}, u32[]{:S(2)}) %collective-permute-start.23) | collective-permute-done | bytes 1376288 | tf_op jit(solution)/shard_map/ppermute | solution.py:18
  117.8 2.9 %shard_map.59 = f32[256,896]{1,0:T(8,128)} custom-call(s32[3]{0:T(128)S(1)} %pad_add_fusion.refs_0_, bf16[2,2,48,256]{3,2,1,0:T(8,128)(2,1)S(1)} %bitcast.34, bf16[2,2,48,256]{3,2,1,0:T(8,128)(2,1)S(1)} %bitcast.30, bf16[2,2,48,256]{3,2,1,0:T(8,128)(2,1)S(1)} %bitcast.28, bf16[2,2,48,256]{3,2,1,0:T(8,128)(2,1)S(1)} %bitcast.32, ...), custom_call_target="tpu_custom_call" | custom-call | flops 703000000 | bytes 5000000 | tf_op jit(solution)/shard_map/pallas_call | solution.py:34
  (56 shorter events, 17.0 us)
Async XLA Ops:
  0.0 45.4 %collective-permute-start.10 = (bf16[896,896]{1,0:T(8,128)(2,1)}, bf16[896,896]{1,0:T(8,128)(2,1)}, u32[]{:S(2)}, u32[]{:S(2)}) collective-permute-start(bf16[896,896]{1,0:T(8,128)(2,1)} %refs_5_.1), channel_id=1, source_target_pairs={{0,1},{1,0},{2,3},{3,2},{4,5},{5,4},{6,7},{7,6},{8,9},{9,8},{10,11... | collective-permute-start | bytes 4816904 | tf_op jit(solution)/shard_map/ppermute | solution.py:18
  2.4 8.6 %collective-permute-start = (bf16[96,1152]{1,0:T(8,128)(2,1)S(1)}, bf16[96,1152]{1,0:T(8,128)(2,1)S(1)}, u32[]{:S(2)}, u32[]{:S(2)}) collective-permute-start(bf16[96,1152]{1,0:T(8,128)(2,1)S(1)} %shard_map.46.refs_1_), channel_id=1, source_target_pairs={{0,16},{16,0},{1,17},{17,1},{2,18},{18,2},{3,19},{19,3},{4,20},{20... | collective-permute-start | bytes 663560 | tf_op jit(solution)/shard_map/ppermute | solution.py:18
  13.3 8.9 %collective-permute-start.8 = (bf16[96,1792]{1,0:T(8,128)(2,1)S(1)}, bf16[96,1792]{1,0:T(8,128)(2,1)S(1)}, u32[]{:S(2)}, u32[]{:S(2)}) collective-permute-start(bf16[96,1792]{1,0:T(8,128)(2,1)S(1)} %shard_map.52.refs_2_), channel_id=1, source_target_pairs={{0,32},{1,225},{32,64},{33,1},{64,96},{65,33},{96,128},{97,65},{12... | collective-permute-start | bytes 1032200 | tf_op jit(solution)/shard_map/ppermute | solution.py:63
  14.4 12.4 %collective-permute-start.2 = (bf16[96,1792]{1,0:T(8,128)(2,1)S(1)}, bf16[96,1792]{1,0:T(8,128)(2,1)S(1)}, u32[]{:S(2)}, u32[]{:S(2)}) collective-permute-start(bf16[96,1792]{1,0:T(8,128)(2,1)S(1)} %shard_map.48.refs_1_), channel_id=1, source_target_pairs={{0,32},{1,225},{32,64},{33,1},{64,96},{65,33},{96,128},{97,65},{12... | collective-permute-start | bytes 1032200 | tf_op jit(solution)/shard_map/ppermute | solution.py:63
  14.5 12.3 %all-to-all-start = ((bf16[8,48,512]{2,1,0:T(8,128)(2,1)}), bf16[8,48,512]{2,1,0:T(8,128)(2,1)S(1)}, u32[]{:S(2)}, u32[]{:S(2)}) async-start(bf16[8,48,512]{2,1,0:T(8,128)(2,1)} %bitcast.3), calls=%async_computation | async-start | bytes 786432 | tf_op jit(solution)/shard_map/all_to_all | solution.py:176
  19.6 7.2 %collective-permute-start.3 = (bf16[256,256]{1,0:T(8,128)(2,1)S(1)}, bf16[256,256]{1,0:T(8,128)(2,1)S(1)}, u32[]{:S(2)}, u32[]{:S(2)}) collective-permute-start(bf16[256,256]{1,0:T(8,128)(2,1)S(1)} %copy-done), channel_id=1, source_target_pairs={{0,16},{16,0},{1,17},{17,1},{2,18},{18,2},{3,19},{19,3},{4,20},{20... | collective-permute-start | bytes 393224 | tf_op jit(solution)/shard_map/ppermute | solution.py:18
  22.2 11.1 %collective-permute-start.9 = (bf16[96,1792]{1,0:T(8,128)(2,1)S(1)}, bf16[96,1792]{1,0:T(8,128)(2,1)S(1)}, u32[]{:S(2)}, u32[]{:S(2)}) collective-permute-start(bf16[96,1792]{1,0:T(8,128)(2,1)S(1)} %collective-permute-done.8.refs_4_), channel_id=1, source_target_pairs={{0,32},{1,225},{32,64},{33,1},{64,96},{65,33},{96,128},{97,65},{12... | collective-permute-start | bytes 1032200 | tf_op jit(solution)/shard_map/ppermute | solution.py:63
  26.8 8.0 %collective-permute-start.4 = (bf16[384,512]{1,0:T(8,128)(2,1)S(1)}, bf16[384,512]{1,0:T(8,128)(2,1)S(1)}, u32[]{:S(2)}, u32[]{:S(2)}) collective-permute-start(bf16[384,512]{1,0:T(8,128)(2,1)S(1)} %shard_map.49.refs_0_), channel_id=1, source_target_pairs={{0,1},{1,0},{2,3},{3,2},{4,5},{5,4},{6,7},{7,6},{8,9},{9,8},{10,11... | collective-permute-start | bytes 1179656 | tf_op jit(solution)/shard_map/ppermute | solution.py:18
  32.5 9.6 %collective-permute-start.5 = (bf16[96,1792]{1,0:T(8,128)(2,1)S(1)}, bf16[96,1792]{1,0:T(8,128)(2,1)S(1)}, u32[]{:S(2)}, u32[]{:S(2)}) collective-permute-start(bf16[96,1792]{1,0:T(8,128)(2,1)S(1)} %collective-permute-done.2.refs_1_.refs_3_), channel_id=1, source_target_pairs={{0,32},{1,225},{32,64},{33,1},{64,96},{65,33},{96,128},{97,65},{12... | collective-permute-start | bytes 1032200 | tf_op jit(solution)/shard_map/ppermute | solution.py:63
  33.3 10.3 %collective-permute-start.20 = (bf16[96,1792]{1,0:T(8,128)(2,1)S(1)}, bf16[96,1792]{1,0:T(8,128)(2,1)S(1)}, u32[]{:S(2)}, u32[]{:S(2)}) collective-permute-start(bf16[96,1792]{1,0:T(8,128)(2,1)S(1)} %collective-permute-done.9.refs_6_), channel_id=1, source_target_pairs={{0,32},{1,225},{32,64},{33,1},{64,96},{65,33},{96,128},{97,65},{12... | collective-permute-start | bytes 1032200 | tf_op jit(solution)/shard_map/ppermute | solution.py:63
  36.0 22.5 %all-to-all-start.1 = ((bf16[8,96,256]{2,1,0:T(8,128)(2,1)}), bf16[8,96,256]{2,1,0:T(8,128)(2,1)S(1)}, u32[]{:S(2)}, u32[]{:S(2)}) async-start(bf16[8,96,256]{2,1,0:T(8,128)(2,1)} %bitcast.5), calls=%async_computation.1 | async-start | bytes 786432 | tf_op jit(solution)/shard_map/all_to_all | solution.py:176
  42.1 15.7 %collective-permute-start.6 = (bf16[96,1792]{1,0:T(8,128)(2,1)S(1)}, bf16[96,1792]{1,0:T(8,128)(2,1)S(1)}, u32[]{:S(2)}, u32[]{:S(2)}) collective-permute-start(bf16[96,1792]{1,0:T(8,128)(2,1)S(1)} %shard_map.51.refs_5_), channel_id=1, source_target_pairs={{0,32},{1,225},{32,64},{33,1},{64,96},{65,33},{96,128},{97,65},{12... | collective-permute-start | bytes 1032200 | tf_op jit(solution)/shard_map/ppermute | solution.py:63
  43.5 19.5 %collective-permute-start.22 = (bf16[96,1792]{1,0:T(8,128)(2,1)S(1)}, bf16[96,1792]{1,0:T(8,128)(2,1)S(1)}, u32[]{:S(2)}, u32[]{:S(2)}) collective-permute-start(bf16[96,1792]{1,0:T(8,128)(2,1)S(1)} %collective-permute-done.20.refs_2_), channel_id=1, source_target_pairs={{1,225},{33,1},{65,33},{97,65},{129,97},{161,129},{193,161},{225,1... | collective-permute-start | bytes 1032200 | tf_op jit(solution)/shard_map/ppermute | solution.py:63
  57.8 5.3 %collective-permute-start.21 = (bf16[96,1792]{1,0:T(8,128)(2,1)S(1)}, bf16[96,1792]{1,0:T(8,128)(2,1)S(1)}, u32[]{:S(2)}, u32[]{:S(2)}) collective-permute-start(bf16[96,1792]{1,0:T(8,128)(2,1)S(1)} %shard_map.54.refs_1_), channel_id=1, source_target_pairs={{0,32},{32,64},{64,96},{96,128},{128,160},{160,192},{192,224},{224... | collective-permute-start | bytes 1032200 | tf_op jit(solution)/shard_map/ppermute | solution.py:63
  58.5 4.5 %collective-permute-start.11 = (bf16[96,256]{1,0:T(8,128)(2,1)S(1)}, bf16[96,256]{1,0:T(8,128)(2,1)S(1)}, u32[]{:S(2)}, u32[]{:S(2)}) collective-permute-start(bf16[96,256]{1,0:T(8,128)(2,1)S(1)} %shard_map.55), channel_id=1, source_target_pairs={{0,16},{16,0},{1,17},{17,1},{2,18},{18,2},{3,19},{19,3},{4,20},{20... | collective-permute-start | bytes 147464 | tf_op jit(solution)/shard_map/ppermute | solution.py:18
  68.5 18.0 %all-to-all-start.2 = ((bf16[8,96,896]{2,1,0:T(8,128)(2,1)}), bf16[8,96,896]{2,1,0:T(8,128)(2,1)S(1)}, u32[]{:S(2)}, u32[]{:S(2)}) async-start(bf16[8,96,896]{2,1,0:T(8,128)(2,1)} %bitcast.37), calls=%async_computation.2 | async-start | bytes 2752512 | tf_op jit(solution)/shard_map/all_to_all | solution.py:176
  73.0 5.1 %collective-permute-start.12 = (bf16[192,256]{1,0:T(8,128)(2,1)S(1)}, bf16[192,256]{1,0:T(8,128)(2,1)S(1)}, u32[]{:S(2)}, u32[]{:S(2)}) collective-permute-start(bf16[192,256]{1,0:T(8,128)(2,1)S(1)} %pad_maximum_fusion), channel_id=1, source_target_pairs={{0,224},{32,0},{64,32},{96,64},{128,96},{160,128},{192,160},{224,1... | collective-permute-start | bytes 294920 | tf_op jit(solution)/shard_map/ppermute | solution.py:14
  73.1 5.8 %collective-permute-start.13 = (bf16[192,256]{1,0:T(8,128)(2,1)S(1)}, bf16[192,256]{1,0:T(8,128)(2,1)S(1)}, u32[]{:S(2)}, u32[]{:S(2)}) collective-permute-start(bf16[192,256]{1,0:T(8,128)(2,1)S(1)} %pad_maximum_fusion), channel_id=1, source_target_pairs={{0,192},{32,224},{64,0},{96,32},{128,64},{160,96},{192,128},{224,1... | collective-permute-start | bytes 294920 | tf_op jit(solution)/shard_map/ppermute | solution.py:14
  73.2 6.1 %collective-permute-start.15 = (bf16[192,256]{1,0:T(8,128)(2,1)S(1)}, bf16[192,256]{1,0:T(8,128)(2,1)S(1)}, u32[]{:S(2)}, u32[]{:S(2)}) collective-permute-start(bf16[192,256]{1,0:T(8,128)(2,1)S(1)} %pad_maximum_fusion), channel_id=1, source_target_pairs={{0,64},{32,96},{64,128},{96,160},{128,192},{160,224},{192,0},{224,... | collective-permute-start | bytes 294920 | tf_op jit(solution)/shard_map/ppermute | solution.py:14
  87.7 26.5 %all-to-all-start.3 = ((bf16[8,96,896]{2,1,0:T(8,128)(2,1)}), bf16[8,96,896]{2,1,0:T(8,128)(2,1)S(1)}, u32[]{:S(2)}, u32[]{:S(2)}) async-start(bf16[8,96,896]{2,1,0:T(8,128)(2,1)} %bitcast.18), calls=%async_computation.3 | async-start | bytes 2752512 | tf_op jit(solution)/shard_map/all_to_all | solution.py:176
  95.8 8.1 %collective-permute-start.14 = (bf16[192,256]{1,0:T(8,128)(2,1)S(1)}, bf16[192,256]{1,0:T(8,128)(2,1)S(1)}, u32[]{:S(2)}, u32[]{:S(2)}) collective-permute-start(bf16[192,256]{1,0:T(8,128)(2,1)S(1)} %collective-permute-done.13.refs_4_), channel_id=1, source_target_pairs={{0,224},{32,0},{64,32},{96,64},{128,96},{160,128},{192,160},{224,1... | collective-permute-start | bytes 294920 | tf_op jit(solution)/shard_map/ppermute | solution.py:14
  95.8 8.1 %collective-permute-start.16 = (bf16[192,256]{1,0:T(8,128)(2,1)S(1)}, bf16[192,256]{1,0:T(8,128)(2,1)S(1)}, u32[]{:S(2)}, u32[]{:S(2)}) collective-permute-start(bf16[192,256]{1,0:T(8,128)(2,1)S(1)} %collective-permute-done.15.refs_3_), channel_id=1, source_target_pairs={{0,32},{32,64},{64,96},{96,128},{128,160},{160,192},{192,224},{224... | collective-permute-start | bytes 294920 | tf_op jit(solution)/shard_map/ppermute | solution.py:14
  98.5 4.1 %collective-permute-start.18 = (bf16[192,128]{1,0:T(8,128)(2,1)S(1)}, bf16[192,128]{1,0:T(8,128)(2,1)S(1)}, u32[]{:S(2)}, u32[]{:S(2)}) collective-permute-start(bf16[192,128]{1,0:T(8,128)(2,1)S(1)} %slice.8), channel_id=1, source_target_pairs={{0,64},{32,96},{64,128},{96,160},{128,192},{160,224},{192,0},{224,... | collective-permute-start | bytes 147464 | tf_op jit(solution)/shard_map/ppermute | solution.py:14
  98.5 5.4 %collective-permute-start.19 = (bf16[192,128]{1,0:T(8,128)(2,1)S(1)}, bf16[192,128]{1,0:T(8,128)(2,1)S(1)}, u32[]{:S(2)}, u32[]{:S(2)}) collective-permute-start(bf16[192,128]{1,0:T(8,128)(2,1)S(1)} %slice.9), channel_id=1, source_target_pairs={{0,192},{32,224},{64,0},{96,32},{128,64},{160,96},{192,128},{224,1... | collective-permute-start | bytes 147464 | tf_op jit(solution)/shard_map/ppermute | solution.py:14
  (7 other events, 27.0 us)

commit v6 on v5

--- a/solution.py
+++ b/solution.py
@@ -76,7 +76,7 @@
     return call(body, out, arrays, [VMEM] * len(arrays), after, out_specs=VMEM)
 
 
-def rotate(where, blocks, bases, start, total, sums=(), after=(), fetch=True):
+def rotate(where, blocks, bases, start, total, sums=(), after=()):
     parts = [block if isinstance(block, tuple) else (block,) for block in blocks]
     rows, depth, width = parts[0][0].shape[0], bases[0].shape[0], bases[0].shape[1]
     count, many = len(parts), sum(len(part) for part in parts)
@@ -84,7 +84,7 @@
     def body(where, *refs):
         refs, bases, (out, token, x, base, result, sems, out_sems, base_sems) = list(refs[:many]), refs[many : many + 2], refs[-8:]
         copies, slab = [], depth // 7
-        for k in range(14 if fetch else 0):
+        for k in range(14):
             source = bases[k // 7].at[pl.ds(k % 7 * slab, slab)]
             copies.append(pltpu.make_async_copy(source, base.at[pl.ds(k * slab, slab)], base_sems.at[k]))
             copies[-1].start()
@@ -101,10 +101,12 @@
                         pltpu.make_async_copy(refs[core], place, sem).start()
 
             refs = refs[len(part) :]
-        for copy in copies:
+        for copy in copies[:7] + copies[14:]:
             copy.wait()
-        first, second = (base[:depth], base[depth:]) if fetch else (bases[0][...], bases[1][...])
-        result[...] = (dot(x[:, :depth], first) + dot(x[:, depth:], second)).astype(result.dtype)
+        total_first = dot(x[:, :depth], base[:depth])
+        for copy in copies[7:14]:
+            copy.wait()
+        result[...] = (total_first + dot(x[:, depth:], base[depth:])).astype(result.dtype)
         token[...] = jnp.zeros_like(token)
         copies = []
         for k in range(count):
@@ -117,14 +119,14 @@
     out = [jax.ShapeDtypeStruct((total, width), jnp.bfloat16), jax.ShapeDtypeStruct((8, 128), jnp.float32)]
     scratch = [
         pltpu.VMEM((count * rows, 2 * depth), jnp.bfloat16),
-        pltpu.VMEM((2 * depth if fetch else 16, width), jnp.bfloat16),
+        pltpu.VMEM((2 * depth, width), jnp.bfloat16),
         pltpu.VMEM((count * rows, width), jnp.bfloat16),
         pltpu.SemaphoreType.DMA((count,)),
         pltpu.SemaphoreType.DMA((count,)),
         pltpu.SemaphoreType.DMA((14,)),
     ]
     ins = [where, *(x for part in parts for x in part), *bases, *sums]
-    specs = [SMEM] + [ANY] * many + [ANY if fetch else VMEM] * 2 + [ANY] * len(sums)
+    specs = [SMEM] + [ANY] * (len(ins) - 1)
     flops = 4 * count * rows * depth * width
     more = {"input_output_aliases": {len(ins) - 1: 0}} if sums else {}
     return call(body, out, ins, specs, after, flops, 5 * 10**6, 52, out_specs=[ANY, VMEM], scratch_shapes=scratch, **more)
@@ -238,7 +240,7 @@
     far = tuple(lap(x, core) for core, x in enumerate(laps[3]))
     act_half = summed(act_parts, 8, 1, laps[3][:1])
     act_mate = swap(act_half, "xh")
-    terms, _ = rotate(where, [*laps[3], far], bases, 5 * rows, 8 * rows, (early,), (act_mate,), False)
+    terms, _ = rotate(where, [*laps[3], far], bases, 5 * rows, 8 * rows, (early,), (act_mate,))
     parts = spread(terms, CHIPS)
     act_pair = jnp.concatenate([act_half, act_mate], axis=0)
     one = hop(act_pair, act_pair)

time: 121 us -> 121 us (level)
  no operation moved by 1% of the time
where the time goes in v6:
time: 121 us
  starting transfers between devices  54.3 us (45%)
  waiting for transfers between devices  45.2 us (37%)
  Pallas kernels  20.2 us (17%)
    all_to_all x4, starting transfers between devices, spread(): return lax.all_to_all(x, axis, 0, 0, tiled=True)  23.9 us
    pallas_call x14, Pallas kernels, call(): pl.pallas_call(kernel, out_shape=out, in_specs=list(specs) + [ANY] * len(...  20.2 us
    ppermute x8, waiting for transfers between devices, swap(): return lax.ppermute(x, axis, [(0, 1), (1, 0)])  16.4 us
    all_to_all x4, waiting for transfers between devices, spread(): return lax.all_to_all(x, axis, 0, 0, tiled=True)  16.4 us
    ppermute x8, starting transfers between devices, swap(): return lax.ppermute(x, axis, [(0, 1), (1, 0)])  14.8 us
    ppermute x8, starting transfers between devices, shift(): return lax.ppermute(x, axis, [(i, (i + by) % size) for i in range(size)])  10.1 us
    ppermute x8, waiting for transfers between devices, lap(): lax.ppermute(x, ('z', 'c'), [(2 * z + c, 2 * to + c) for z, c, to in steps])  7.21 us
    ppermute x8, starting transfers between devices, lap(): lax.ppermute(x, ('z', 'c'), [(2 * z + c, 2 * to + c) for z, c, to in steps])  5.41 us
  transfers between devices with their start and end apart: 28, of which 14 were waited for; matrix products, arithmetic and copies ran while one was open for 0% of the time, Pallas kernels for 9%

profile of v6, /device:TPU:97, one launch (start us, length us, event | category | flops | bytes accessed | tf_op | source)
XLA Modules:
  0.0 120.7 jit_solution(3949057961789976004)
XLA Ops:
  2.4 2.8 %collective-permute-start = (bf16[96,1152]{1,0:T(8,128)(2,1)S(1)}, bf16[96,1152]{1,0:T(8,128)(2,1)S(1)}, u32[]{:S(2)}, u32[]{:S(2)}) collective-permute-start(bf16[96,1152]{1,0:T(8,128)(2,1)S(1)} %shard_map.46.refs_1_), channel_id=1, source_target_pairs={{0,16},{16,0},{1,17},{17,1},{2,18},{18,2},{3,19},{19,3},{4,20},{20... | collective-permute-start | bytes 663560 | tf_op jit(solution)/shard_map/ppermute | solution.py:18
  5.2 5.8 %collective-permute-done.refs_2_.refs_0_ = bf16[96,1152]{1,0:T(8,128)(2,1)S(1)} collective-permute-done((bf16[96,1152]{1,0:T(8,128)(2,1)S(1)}, bf16[96,1152]{1,0:T(8,128)(2,1)S(1)}, u32[]{:S(2)}, u32[]{:S(2)}) %collective-permute-start) | collective-permute-done | bytes 221216 | tf_op jit(solution)/shard_map/ppermute | solution.py:18
  14.5 5.1 %all-to-all-start = ((bf16[8,48,512]{2,1,0:T(8,128)(2,1)}), bf16[8,48,512]{2,1,0:T(8,128)(2,1)S(1)}, u32[]{:S(2)}, u32[]{:S(2)}) async-start(bf16[8,48,512]{2,1,0:T(8,128)(2,1)} %bitcast.3), calls=%async_computation | async-start | bytes 786432 | tf_op jit(solution)/shard_map/all_to_all | solution.py:178
  19.6 2.5 %collective-permute-start.3 = (bf16[256,256]{1,0:T(8,128)(2,1)S(1)}, bf16[256,256]{1,0:T(8,128)(2,1)S(1)}, u32[]{:S(2)}, u32[]{:S(2)}) collective-permute-start(bf16[256,256]{1,0:T(8,128)(2,1)S(1)} %copy-done), channel_id=1, source_target_pairs={{0,16},{16,0},{1,17},{17,1},{2,18},{18,2},{3,19},{19,3},{4,20},{20... | collective-permute-start | bytes 393224 | tf_op jit(solution)/shard_map/ppermute | solution.py:18
  22.2 4.6 %collective-permute-done.3.refs_2_.refs_3_ = bf16[256,256]{1,0:T(8,128)(2,1)S(1)} collective-permute-done((bf16[256,256]{1,0:T(8,128)(2,1)S(1)}, bf16[256,256]{1,0:T(8,128)(2,1)S(1)}, u32[]{:S(2)}, u32[]{:S(2)}) %collective-permute-start.3) | collective-permute-done | bytes 131104 | tf_op jit(solution)/shard_map/ppermute | solution.py:18
  26.8 5.7 %collective-permute-start.4 = (bf16[384,512]{1,0:T(8,128)(2,1)S(1)}, bf16[384,512]{1,0:T(8,128)(2,1)S(1)}, u32[]{:S(2)}, u32[]{:S(2)}) collective-permute-start(bf16[384,512]{1,0:T(8,128)(2,1)S(1)} %shard_map.49.refs_0_), channel_id=1, source_target_pairs={{0,1},{1,0},{2,3},{3,2},{4,5},{5,4},{6,7},{7,6},{8,9},{9,8},{10,11... | collective-permute-start | bytes 1179656 | tf_op jit(solution)/shard_map/ppermute | solution.py:18
  33.3 1.6 %collective-permute-start.20 = (bf16[96,1792]{1,0:T(8,128)(2,1)S(1)}, bf16[96,1792]{1,0:T(8,128)(2,1)S(1)}, u32[]{:S(2)}, u32[]{:S(2)}) collective-permute-start(bf16[96,1792]{1,0:T(8,128)(2,1)S(1)} %collective-permute-done.9.refs_6_), channel_id=1, source_target_pairs={{0,32},{1,225},{32,64},{33,1},{64,96},{65,33},{96,128},{97,65},{12... | collective-permute-start | bytes 1032200 | tf_op jit(solution)/shard_map/ppermute | solution.py:63
  36.0 6.2 %all-to-all-start.1 = ((bf16[8,96,256]{2,1,0:T(8,128)(2,1)}), bf16[8,96,256]{2,1,0:T(8,128)(2,1)S(1)}, u32[]{:S(2)}, u32[]{:S(2)}) async-start(bf16[8,96,256]{2,1,0:T(8,128)(2,1)} %bitcast.5), calls=%async_computation.1 | async-start | bytes 786432 | tf_op jit(solution)/shard_map/all_to_all | solution.py:178
  43.5 1.9 %collective-permute-start.22 = (bf16[96,1792]{1,0:T(8,128)(2,1)S(1)}, bf16[96,1792]{1,0:T(8,128)(2,1)S(1)}, u32[]{:S(2)}, u32[]{:S(2)}) collective-permute-start(bf16[96,1792]{1,0:T(8,128)(2,1)S(1)} %collective-permute-done.20.refs_2_), channel_id=1, source_target_pairs={{1,225},{33,1},{65,33},{97,65},{129,97},{161,129},{193,161},{225,1... | collective-permute-start | bytes 1032200 | tf_op jit(solution)/shard_map/ppermute | solution.py:63
  45.5 6.2 %shard_map.53 = (bf16[768,896]{1,0:T(8,128)(2,1)}, f32[8,128]{1,0:T(8,128)S(1)}) custom-call(s32[3]{0:T(128)S(1)} %pad_add_fusion.refs_0_, bf16[96,1792]{1,0:T(8,128)(2,1)S(1)} %shard_map.48.refs_1_, bf16[96,1792]{1,0:T(8,128)(2,1)S(1)} %shard_map.52.refs_2_, bf16[96,1792]{1,0:T(8,128)(2,1)S(1)} %collective-permute-done.2.refs_1_.refs_3_, ...), custom_call_target="tpu_custom_call" | custom-call | flops 1541406720 | bytes 5000000 | tf_op jit(solution)/shard_map/pallas_call | solution.py:34
  51.6 6.1 %collective-permute-done.6.refs_0_ = bf16[96,1792]{1,0:T(8,128)(2,1)S(1)} collective-permute-done((bf16[96,1792]{1,0:T(8,128)(2,1)S(1)}, bf16[96,1792]{1,0:T(8,128)(2,1)S(1)}, u32[]{:S(2)}, u32[]{:S(2)}) %collective-permute-start.6) | collective-permute-done | bytes 344096 | tf_op jit(solution)/shard_map/ppermute | solution.py:63
  58.5 1.4 %collective-permute-start.11 = (bf16[96,256]{1,0:T(8,128)(2,1)S(1)}, bf16[96,256]{1,0:T(8,128)(2,1)S(1)}, u32[]{:S(2)}, u32[]{:S(2)}) collective-permute-start(bf16[96,256]{1,0:T(8,128)(2,1)S(1)} %shard_map.55), channel_id=1, source_target_pairs={{0,16},{16,0},{1,17},{17,1},{2,18},{18,2},{3,19},{19,3},{4,20},{20... | collective-permute-start | bytes 147464 | tf_op jit(solution)/shard_map/ppermute | solution.py:18
  59.9 3.1 %collective-permute-done.11.refs_8_ = bf16[96,256]{1,0:T(8,128)(2,1)S(1)} collective-permute-done((bf16[96,256]{1,0:T(8,128)(2,1)S(1)}, bf16[96,256]{1,0:T(8,128)(2,1)S(1)}, u32[]{:S(2)}, u32[]{:S(2)}) %collective-permute-start.11) | collective-permute-done | bytes 49184 | tf_op jit(solution)/shard_map/ppermute | solution.py:18
  63.1 5.4 %shard_map.56 = (bf16[768,896]{1,0:T(8,128)(2,1)}, f32[8,128]{1,0:T(8,128)}) custom-call(s32[3]{0:T(128)S(1)} %pad_add_fusion.refs_0_, bf16[96,1792]{1,0:T(8,128)(2,1)S(1)} %shard_map.54.refs_1_, bf16[96,1792]{1,0:T(8,128)(2,1)S(1)} %collective-permute-done.20.refs_2_, ...), custom_call_target="tpu_custom_call", output_to_operand_aliasing={{0}: (7, {})} | custom-call | flops 924844032 | bytes 5000000 | tf_op jit(solution)/shard_map/pallas_call | solution.py:34
  68.5 4.6 %all-to-all-start.2 = ((bf16[8,96,896]{2,1,0:T(8,128)(2,1)}), bf16[8,96,896]{2,1,0:T(8,128)(2,1)S(1)}, u32[]{:S(2)}, u32[]{:S(2)}) async-start(bf16[8,96,896]{2,1,0:T(8,128)(2,1)} %bitcast.37), calls=%async_computation.2 | async-start | bytes 2752512 | tf_op jit(solution)/shard_map/all_to_all | solution.py:178
  73.2 3.6 %collective-permute-start.15 = (bf16[192,256]{1,0:T(8,128)(2,1)S(1)}, bf16[192,256]{1,0:T(8,128)(2,1)S(1)}, u32[]{:S(2)}, u32[]{:S(2)}) collective-permute-start(bf16[192,256]{1,0:T(8,128)(2,1)S(1)} %pad_maximum_fusion), channel_id=1, source_target_pairs={{0,64},{32,96},{64,128},{96,160},{128,192},{160,224},{192,0},{224,... | collective-permute-start | bytes 294920 | tf_op jit(solution)/shard_map/ppermute | solution.py:14
  80.4 6.1 %all-to-all-done.2 = bf16[8,96,896]{2,1,0:T(8,128)(2,1)S(1)} async-done(((bf16[8,96,896]{2,1,0:T(8,128)(2,1)}), bf16[8,96,896]{2,1,0:T(8,128)(2,1)S(1)}, u32[]{:S(2)}, u32[]{:S(2)}) %all-to-all-start.2) | async-done | bytes 1376288 | tf_op jit(solution)/shard_map/all_to_all | solution.py:178
  87.7 8.1 %all-to-all-start.3 = ((bf16[8,96,896]{2,1,0:T(8,128)(2,1)}), bf16[8,96,896]{2,1,0:T(8,128)(2,1)S(1)}, u32[]{:S(2)}, u32[]{:S(2)}) async-start(bf16[8,96,896]{2,1,0:T(8,128)(2,1)} %bitcast.18), calls=%async_computation.3 | async-start | bytes 2752512 | tf_op jit(solution)/shard_map/all_to_all | solution.py:178
  95.8 2.7 %collective-permute-start.16 = (bf16[192,256]{1,0:T(8,128)(2,1)S(1)}, bf16[192,256]{1,0:T(8,128)(2,1)S(1)}, u32[]{:S(2)}, u32[]{:S(2)}) collective-permute-start(bf16[192,256]{1,0:T(8,128)(2,1)S(1)} %collective-permute-done.15.refs_3_), channel_id=1, source_target_pairs={{0,32},{32,64},{64,96},{96,128},{128,160},{160,192},{192,224},{224... | collective-permute-start | bytes 294920 | tf_op jit(solution)/shard_map/ppermute | solution.py:14
  98.5 2.4 %collective-permute-start.19 = (bf16[192,128]{1,0:T(8,128)(2,1)S(1)}, bf16[192,128]{1,0:T(8,128)(2,1)S(1)}, u32[]{:S(2)}, u32[]{:S(2)}) collective-permute-start(bf16[192,128]{1,0:T(8,128)(2,1)S(1)} %slice.9), channel_id=1, source_target_pairs={{0,192},{32,224},{64,0},{96,32},{128,64},{160,96},{192,128},{224,1... | collective-permute-start | bytes 147464 | tf_op jit(solution)/shard_map/ppermute | solution.py:14
  100.9 1.8 %collective-permute-done.18.refs_3_ = bf16[192,128]{1,0:T(8,128)(2,1)S(1)} collective-permute-done((bf16[192,128]{1,0:T(8,128)(2,1)S(1)}, bf16[192,128]{1,0:T(8,128)(2,1)S(1)}, u32[]{:S(2)}, u32[]{:S(2)}) %collective-permute-start.18) | collective-permute-done | bytes 49184 | tf_op jit(solution)/shard_map/ppermute | solution.py:14
  103.9 10.3 %all-to-all-done.3 = bf16[8,96,896]{2,1,0:T(8,128)(2,1)S(1)} async-done(((bf16[8,96,896]{2,1,0:T(8,128)(2,1)}), bf16[8,96,896]{2,1,0:T(8,128)(2,1)S(1)}, u32[]{:S(2)}, u32[]{:S(2)}) %all-to-all-start.3) | async-done | bytes 1376288 | tf_op jit(solution)/shard_map/all_to_all | solution.py:178
  115.1 2.8 %collective-permute-done.23 = bf16[768,896]{1,0:T(8,128)(2,1)S(1)} collective-permute-done((bf16[768,896]{1,0:T(8,128)(2,1)S(1)}, bf16[768,896]{1,0:T(8,128)(2,1)S(1)}, u32[]{:S(2)}, u32[]{:S(2)}) %collective-permute-start.23) | collective-permute-done | bytes 1376288 | tf_op jit(solution)/shard_map/ppermute | solution.py:18
  117.8 2.9 %shard_map.59 = f32[256,896]{1,0:T(8,128)} custom-call(s32[3]{0:T(128)S(1)} %pad_add_fusion.refs_0_, bf16[2,2,48,256]{3,2,1,0:T(8,128)(2,1)S(1)} %bitcast.34, bf16[2,2,48,256]{3,2,1,0:T(8,128)(2,1)S(1)} %bitcast.30, bf16[2,2,48,256]{3,2,1,0:T(8,128)(2,1)S(1)} %bitcast.28, bf16[2,2,48,256]{3,2,1,0:T(8,128)(2,1)S(1)} %bitcast.32, ...), custom_call_target="tpu_custom_call" | custom-call | flops 703000000 | bytes 5000000 | tf_op jit(solution)/shard_map/pallas_call | solution.py:34
  (56 shorter events, 17.0 us)
Async XLA Ops:
  0.0 45.4 %collective-permute-start.10 = (bf16[896,896]{1,0:T(8,128)(2,1)}, bf16[896,896]{1,0:T(8,128)(2,1)}, u32[]{:S(2)}, u32[]{:S(2)}) collective-permute-start(bf16[896,896]{1,0:T(8,128)(2,1)} %refs_5_.1), channel_id=1, source_target_pairs={{0,1},{1,0},{2,3},{3,2},{4,5},{5,4},{6,7},{7,6},{8,9},{9,8},{10,11... | collective-permute-start | bytes 4816904 | tf_op jit(solution)/shard_map/ppermute | solution.py:18
  2.4 8.6 %collective-permute-start = (bf16[96,1152]{1,0:T(8,128)(2,1)S(1)}, bf16[96,1152]{1,0:T(8,128)(2,1)S(1)}, u32[]{:S(2)}, u32[]{:S(2)}) collective-permute-start(bf16[96,1152]{1,0:T(8,128)(2,1)S(1)} %shard_map.46.refs_1_), channel_id=1, source_target_pairs={{0,16},{16,0},{1,17},{17,1},{2,18},{18,2},{3,19},{19,3},{4,20},{20... | collective-permute-start | bytes 663560 | tf_op jit(solution)/shard_map/ppermute | solution.py:18
  13.3 8.9 %collective-permute-start.8 = (bf16[96,1792]{1,0:T(8,128)(2,1)S(1)}, bf16[96,1792]{1,0:T(8,128)(2,1)S(1)}, u32[]{:S(2)}, u32[]{:S(2)}) collective-permute-start(bf16[96,1792]{1,0:T(8,128)(2,1)S(1)} %shard_map.52.refs_2_), channel_id=1, source_target_pairs={{0,32},{1,225},{32,64},{33,1},{64,96},{65,33},{96,128},{97,65},{12... | collective-permute-start | bytes 1032200 | tf_op jit(solution)/shard_map/ppermute | solution.py:63
  14.4 12.4 %collective-permute-start.2 = (bf16[96,1792]{1,0:T(8,128)(2,1)S(1)}, bf16[96,1792]{1,0:T(8,128)(2,1)S(1)}, u32[]{:S(2)}, u32[]{:S(2)}) collective-permute-start(bf16[96,1792]{1,0:T(8,128)(2,1)S(1)} %shard_map.48.refs_1_), channel_id=1, source_target_pairs={{0,32},{1,225},{32,64},{33,1},{64,96},{65,33},{96,128},{97,65},{12... | collective-permute-start | bytes 1032200 | tf_op jit(solution)/shard_map/ppermute | solution.py:63
  14.5 12.3 %all-to-all-start = ((bf16[8,48,512]{2,1,0:T(8,128)(2,1)}), bf16[8,48,512]{2,1,0:T(8,128)(2,1)S(1)}, u32[]{:S(2)}, u32[]{:S(2)}) async-start(bf16[8,48,512]{2,1,0:T(8,128)(2,1)} %bitcast.3), calls=%async_computation | async-start | bytes 786432 | tf_op jit(solution)/shard_map/all_to_all | solution.py:178
  19.6 7.2 %collective-permute-start.3 = (bf16[256,256]{1,0:T(8,128)(2,1)S(1)}, bf16[256,256]{1,0:T(8,128)(2,1)S(1)}, u32[]{:S(2)}, u32[]{:S(2)}) collective-permute-start(bf16[256,256]{1,0:T(8,128)(2,1)S(1)} %copy-done), channel_id=1, source_target_pairs={{0,16},{16,0},{1,17},{17,1},{2,18},{18,2},{3,19},{19,3},{4,20},{20... | collective-permute-start | bytes 393224 | tf_op jit(solution)/shard_map/ppermute | solution.py:18
  22.2 11.1 %collective-permute-start.9 = (bf16[96,1792]{1,0:T(8,128)(2,1)S(1)}, bf16[96,1792]{1,0:T(8,128)(2,1)S(1)}, u32[]{:S(2)}, u32[]{:S(2)}) collective-permute-start(bf16[96,1792]{1,0:T(8,128)(2,1)S(1)} %collective-permute-done.8.refs_4_), channel_id=1, source_target_pairs={{0,32},{1,225},{32,64},{33,1},{64,96},{65,33},{96,128},{97,65},{12... | collective-permute-start | bytes 1032200 | tf_op jit(solution)/shard_map/ppermute | solution.py:63
  26.8 8.0 %collective-permute-start.4 = (bf16[384,512]{1,0:T(8,128)(2,1)S(1)}, bf16[384,512]{1,0:T(8,128)(2,1)S(1)}, u32[]{:S(2)}, u32[]{:S(2)}) collective-permute-start(bf16[384,512]{1,0:T(8,128)(2,1)S(1)} %shard_map.49.refs_0_), channel_id=1, source_target_pairs={{0,1},{1,0},{2,3},{3,2},{4,5},{5,4},{6,7},{7,6},{8,9},{9,8},{10,11... | collective-permute-start | bytes 1179656 | tf_op jit(solution)/shard_map/ppermute | solution.py:18
  32.5 9.6 %collective-permute-start.5 = (bf16[96,1792]{1,0:T(8,128)(2,1)S(1)}, bf16[96,1792]{1,0:T(8,128)(2,1)S(1)}, u32[]{:S(2)}, u32[]{:S(2)}) collective-permute-start(bf16[96,1792]{1,0:T(8,128)(2,1)S(1)} %collective-permute-done.2.refs_1_.refs_3_), channel_id=1, source_target_pairs={{0,32},{1,225},{32,64},{33,1},{64,96},{65,33},{96,128},{97,65},{12... | collective-permute-start | bytes 1032200 | tf_op jit(solution)/shard_map/ppermute | solution.py:63
  33.3 10.3 %collective-permute-start.20 = (bf16[96,1792]{1,0:T(8,128)(2,1)S(1)}, bf16[96,1792]{1,0:T(8,128)(2,1)S(1)}, u32[]{:S(2)}, u32[]{:S(2)}) collective-permute-start(bf16[96,1792]{1,0:T(8,128)(2,1)S(1)} %collective-permute-done.9.refs_6_), channel_id=1, source_target_pairs={{0,32},{1,225},{32,64},{33,1},{64,96},{65,33},{96,128},{97,65},{12... | collective-permute-start | bytes 1032200 | tf_op jit(solution)/shard_map/ppermute | solution.py:63
  36.0 22.5 %all-to-all-start.1 = ((bf16[8,96,256]{2,1,0:T(8,128)(2,1)}), bf16[8,96,256]{2,1,0:T(8,128)(2,1)S(1)}, u32[]{:S(2)}, u32[]{:S(2)}) async-start(bf16[8,96,256]{2,1,0:T(8,128)(2,1)} %bitcast.5), calls=%async_computation.1 | async-start | bytes 786432 | tf_op jit(solution)/shard_map/all_to_all | solution.py:178
  42.1 15.7 %collective-permute-start.6 = (bf16[96,1792]{1,0:T(8,128)(2,1)S(1)}, bf16[96,1792]{1,0:T(8,128)(2,1)S(1)}, u32[]{:S(2)}, u32[]{:S(2)}) collective-permute-start(bf16[96,1792]{1,0:T(8,128)(2,1)S(1)} %shard_map.51.refs_5_), channel_id=1, source_target_pairs={{0,32},{1,225},{32,64},{33,1},{64,96},{65,33},{96,128},{97,65},{12... | collective-permute-start | bytes 1032200 | tf_op jit(solution)/shard_map/ppermute | solution.py:63
  43.5 19.5 %collective-permute-start.22 = (bf16[96,1792]{1,0:T(8,128)(2,1)S(1)}, bf16[96,1792]{1,0:T(8,128)(2,1)S(1)}, u32[]{:S(2)}, u32[]{:S(2)}) collective-permute-start(bf16[96,1792]{1,0:T(8,128)(2,1)S(1)} %collective-permute-done.20.refs_2_), channel_id=1, source_target_pairs={{1,225},{33,1},{65,33},{97,65},{129,97},{161,129},{193,161},{225,1... | collective-permute-start | bytes 1032200 | tf_op jit(solution)/shard_map/ppermute | solution.py:63
  57.8 5.3 %collective-permute-start.21 = (bf16[96,1792]{1,0:T(8,128)(2,1)S(1)}, bf16[96,1792]{1,0:T(8,128)(2,1)S(1)}, u32[]{:S(2)}, u32[]{:S(2)}) collective-permute-start(bf16[96,1792]{1,0:T(8,128)(2,1)S(1)} %shard_map.54.refs_1_), channel_id=1, source_target_pairs={{0,32},{32,64},{64,96},{96,128},{128,160},{160,192},{192,224},{224... | collective-permute-start | bytes 1032200 | tf_op jit(solution)/shard_map/ppermute | solution.py:63
  58.5 4.5 %collective-permute-start.11 = (bf16[96,256]{1,0:T(8,128)(2,1)S(1)}, bf16[96,256]{1,0:T(8,128)(2,1)S(1)}, u32[]{:S(2)}, u32[]{:S(2)}) collective-permute-start(bf16[96,256]{1,0:T(8,128)(2,1)S(1)} %shard_map.55), channel_id=1, source_target_pairs={{0,16},{16,0},{1,17},{17,1},{2,18},{18,2},{3,19},{19,3},{4,20},{20... | collective-permute-start | bytes 147464 | tf_op jit(solution)/shard_map/ppermute | solution.py:18
  68.5 18.0 %all-to-all-start.2 = ((bf16[8,96,896]{2,1,0:T(8,128)(2,1)}), bf16[8,96,896]{2,1,0:T(8,128)(2,1)S(1)}, u32[]{:S(2)}, u32[]{:S(2)}) async-start(bf16[8,96,896]{2,1,0:T(8,128)(2,1)} %bitcast.37), calls=%async_computation.2 | async-start | bytes 2752512 | tf_op jit(solution)/shard_map/all_to_all | solution.py:178
  73.1 5.1 %collective-permute-start.12 = (bf16[192,256]{1,0:T(8,128)(2,1)S(1)}, bf16[192,256]{1,0:T(8,128)(2,1)S(1)}, u32[]{:S(2)}, u32[]{:S(2)}) collective-permute-start(bf16[192,256]{1,0:T(8,128)(2,1)S(1)} %pad_maximum_fusion), channel_id=1, source_target_pairs={{0,224},{32,0},{64,32},{96,64},{128,96},{160,128},{192,160},{224,1... | collective-permute-start | bytes 294920 | tf_op jit(solution)/shard_map/ppermute | solution.py:14
  73.2 5.8 %collective-permute-start.13 = (bf16[192,256]{1,0:T(8,128)(2,1)S(1)}, bf16[192,256]{1,0:T(8,128)(2,1)S(1)}, u32[]{:S(2)}, u32[]{:S(2)}) collective-permute-start(bf16[192,256]{1,0:T(8,128)(2,1)S(1)} %pad_maximum_fusion), channel_id=1, source_target_pairs={{0,192},{32,224},{64,0},{96,32},{128,64},{160,96},{192,128},{224,1... | collective-permute-start | bytes 294920 | tf_op jit(solution)/shard_map/ppermute | solution.py:14
  73.2 6.1 %collective-permute-start.15 = (bf16[192,256]{1,0:T(8,128)(2,1)S(1)}, bf16[192,256]{1,0:T(8,128)(2,1)S(1)}, u32[]{:S(2)}, u32[]{:S(2)}) collective-permute-start(bf16[192,256]{1,0:T(8,128)(2,1)S(1)} %pad_maximum_fusion), channel_id=1, source_target_pairs={{0,64},{32,96},{64,128},{96,160},{128,192},{160,224},{192,0},{224,... | collective-permute-start | bytes 294920 | tf_op jit(solution)/shard_map/ppermute | solution.py:14
  87.7 26.5 %all-to-all-start.3 = ((bf16[8,96,896]{2,1,0:T(8,128)(2,1)}), bf16[8,96,896]{2,1,0:T(8,128)(2,1)S(1)}, u32[]{:S(2)}, u32[]{:S(2)}) async-start(bf16[8,96,896]{2,1,0:T(8,128)(2,1)} %bitcast.18), calls=%async_computation.3 | async-start | bytes 2752512 | tf_op jit(solution)/shard_map/all_to_all | solution.py:178
  95.8 8.1 %collective-permute-start.14 = (bf16[192,256]{1,0:T(8,128)(2,1)S(1)}, bf16[192,256]{1,0:T(8,128)(2,1)S(1)}, u32[]{:S(2)}, u32[]{:S(2)}) collective-permute-start(bf16[192,256]{1,0:T(8,128)(2,1)S(1)} %collective-permute-done.13.refs_4_), channel_id=1, source_target_pairs={{0,224},{32,0},{64,32},{96,64},{128,96},{160,128},{192,160},{224,1... | collective-permute-start | bytes 294920 | tf_op jit(solution)/shard_map/ppermute | solution.py:14
  95.8 8.1 %collective-permute-start.16 = (bf16[192,256]{1,0:T(8,128)(2,1)S(1)}, bf16[192,256]{1,0:T(8,128)(2,1)S(1)}, u32[]{:S(2)}, u32[]{:S(2)}) collective-permute-start(bf16[192,256]{1,0:T(8,128)(2,1)S(1)} %collective-permute-done.15.refs_3_), channel_id=1, source_target_pairs={{0,32},{32,64},{64,96},{96,128},{128,160},{160,192},{192,224},{224... | collective-permute-start | bytes 294920 | tf_op jit(solution)/shard_map/ppermute | solution.py:14
  98.5 4.1 %collective-permute-start.18 = (bf16[192,128]{1,0:T(8,128)(2,1)S(1)}, bf16[192,128]{1,0:T(8,128)(2,1)S(1)}, u32[]{:S(2)}, u32[]{:S(2)}) collective-permute-start(bf16[192,128]{1,0:T(8,128)(2,1)S(1)} %slice.8), channel_id=1, source_target_pairs={{0,64},{32,96},{64,128},{96,160},{128,192},{160,224},{192,0},{224,... | collective-permute-start | bytes 147464 | tf_op jit(solution)/shard_map/ppermute | solution.py:14
  98.5 5.4 %collective-permute-start.19 = (bf16[192,128]{1,0:T(8,128)(2,1)S(1)}, bf16[192,128]{1,0:T(8,128)(2,1)S(1)}, u32[]{:S(2)}, u32[]{:S(2)}) collective-permute-start(bf16[192,128]{1,0:T(8,128)(2,1)S(1)} %slice.9), channel_id=1, source_target_pairs={{0,192},{32,224},{64,0},{96,32},{128,64},{160,96},{192,128},{224,1... | collective-permute-start | bytes 147464 | tf_op jit(solution)/shard_map/ppermute | solution.py:14
  (7 other events, 27.0 us)

commit v7 on v5

--- a/solution.py
+++ b/solution.py
@@ -236,7 +236,7 @@
     early, token = rotate(where, [tuple(laps[0]), *laps[1], *laps[2]], bases, 0, 8 * rows)
     laps[3] = [*gate(laps[3][:1], (token,)), laps[3][1]]
     far = tuple(lap(x, core) for core, x in enumerate(laps[3]))
-    act_half = summed(act_parts, 8, 1, laps[3][:1])
+    act_half = summed(act_parts, 8, 1, (token,))
     act_mate = swap(act_half, "xh")
     terms, _ = rotate(where, [*laps[3], far], bases, 5 * rows, 8 * rows, (early,), (act_mate,), False)
     parts = spread(terms, CHIPS)

time: 121 us -> 121 us (level)
  no operation moved by 1% of the time
where the time goes in v7:
time: 121 us
  starting transfers between devices  54.3 us (45%)
  waiting for transfers between devices  45.4 us (38%)
  Pallas kernels  19.9 us (16%)
    all_to_all x4, starting transfers between devices, spread(): return lax.all_to_all(x, axis, 0, 0, tiled=True)  23.9 us
    pallas_call x14, Pallas kernels, call(): pl.pallas_call(kernel, out_shape=out, in_specs=list(specs) + [ANY] * len(...  19.9 us
    ppermute x8, waiting for transfers between devices, swap(): return lax.ppermute(x, axis, [(0, 1), (1, 0)])  16.4 us
    all_to_all x4, waiting for transfers between devices, spread(): return lax.all_to_all(x, axis, 0, 0, tiled=True)  16.4 us
    ppermute x8, starting transfers between devices, swap(): return lax.ppermute(x, axis, [(0, 1), (1, 0)])  14.8 us
    ppermute x8, starting transfers between devices, shift(): return lax.ppermute(x, axis, [(i, (i + by) % size) for i in range(size)])  10.1 us
    ppermute x8, waiting for transfers between devices, lap(): lax.ppermute(x, ('z', 'c'), [(2 * z + c, 2 * to + c) for z, c, to in steps])  7.4 us
    ppermute x8, starting transfers between devices, lap(): lax.ppermute(x, ('z', 'c'), [(2 * z + c, 2 * to + c) for z, c, to in steps])  5.41 us
  transfers between devices with their start and end apart: 28, of which 14 were waited for; matrix products, arithmetic and copies ran while one was open for 0% of the time, Pallas kernels for 9%

profile of v7, /device:TPU:97, one launch (start us, length us, event | category | flops | bytes accessed | tf_op | source)
XLA Modules:
  0.0 120.7 jit_solution(13759568364288259563)
XLA Ops:
  2.4 2.8 %collective-permute-start = (bf16[96,1152]{1,0:T(8,128)(2,1)S(1)}, bf16[96,1152]{1,0:T(8,128)(2,1)S(1)}, u32[]{:S(2)}, u32[]{:S(2)}) collective-permute-start(bf16[96,1152]{1,0:T(8,128)(2,1)S(1)} %shard_map.46.refs_1_), channel_id=1, source_target_pairs={{0,16},{16,0},{1,17},{17,1},{2,18},{18,2},{3,19},{19,3},{4,20},{20... | collective-permute-start | bytes 663560 | tf_op jit(solution)/shard_map/ppermute | solution.py:18
  5.2 5.8 %collective-permute-done.refs_2_.refs_0_ = bf16[96,1152]{1,0:T(8,128)(2,1)S(1)} collective-permute-done((bf16[96,1152]{1,0:T(8,128)(2,1)S(1)}, bf16[96,1152]{1,0:T(8,128)(2,1)S(1)}, u32[]{:S(2)}, u32[]{:S(2)}) %collective-permute-start) | collective-permute-done | bytes 221216 | tf_op jit(solution)/shard_map/ppermute | solution.py:18
  14.5 5.1 %all-to-all-start = ((bf16[8,48,512]{2,1,0:T(8,128)(2,1)}), bf16[8,48,512]{2,1,0:T(8,128)(2,1)S(1)}, u32[]{:S(2)}, u32[]{:S(2)}) async-start(bf16[8,48,512]{2,1,0:T(8,128)(2,1)} %bitcast.3), calls=%async_computation | async-start | bytes 786432 | tf_op jit(solution)/shard_map/all_to_all | solution.py:176
  19.6 2.5 %collective-permute-start.3 = (bf16[256,256]{1,0:T(8,128)(2,1)S(1)}, bf16[256,256]{1,0:T(8,128)(2,1)S(1)}, u32[]{:S(2)}, u32[]{:S(2)}) collective-permute-start(bf16[256,256]{1,0:T(8,128)(2,1)S(1)} %copy-done), channel_id=1, source_target_pairs={{0,16},{16,0},{1,17},{17,1},{2,18},{18,2},{3,19},{19,3},{4,20},{20... | collective-permute-start | bytes 393224 | tf_op jit(solution)/shard_map/ppermute | solution.py:18
  22.2 4.6 %collective-permute-done.3.refs_2_.refs_3_ = bf16[256,256]{1,0:T(8,128)(2,1)S(1)} collective-permute-done((bf16[256,256]{1,0:T(8,128)(2,1)S(1)}, bf16[256,256]{1,0:T(8,128)(2,1)S(1)}, u32[]{:S(2)}, u32[]{:S(2)}) %collective-permute-start.3) | collective-permute-done | bytes 131104 | tf_op jit(solution)/shard_map/ppermute | solution.py:18
  26.8 5.7 %collective-permute-start.4 = (bf16[384,512]{1,0:T(8,128)(2,1)S(1)}, bf16[384,512]{1,0:T(8,128)(2,1)S(1)}, u32[]{:S(2)}, u32[]{:S(2)}) collective-permute-start(bf16[384,512]{1,0:T(8,128)(2,1)S(1)} %shard_map.49.refs_0_), channel_id=1, source_target_pairs={{0,1},{1,0},{2,3},{3,2},{4,5},{5,4},{6,7},{7,6},{8,9},{9,8},{10,11... | collective-permute-start | bytes 1179656 | tf_op jit(solution)/shard_map/ppermute | solution.py:18
  33.3 1.6 %collective-permute-start.20 = (bf16[96,1792]{1,0:T(8,128)(2,1)S(1)}, bf16[96,1792]{1,0:T(8,128)(2,1)S(1)}, u32[]{:S(2)}, u32[]{:S(2)}) collective-permute-start(bf16[96,1792]{1,0:T(8,128)(2,1)S(1)} %collective-permute-done.8.refs_6_), channel_id=1, source_target_pairs={{0,32},{1,225},{32,64},{33,1},{64,96},{65,33},{96,128},{97,65},{12... | collective-permute-start | bytes 1032200 | tf_op jit(solution)/shard_map/ppermute | solution.py:63
  36.0 6.2 %all-to-all-start.1 = ((bf16[8,96,256]{2,1,0:T(8,128)(2,1)}), bf16[8,96,256]{2,1,0:T(8,128)(2,1)S(1)}, u32[]{:S(2)}, u32[]{:S(2)}) async-start(bf16[8,96,256]{2,1,0:T(8,128)(2,1)} %bitcast.5), calls=%async_computation.1 | async-start | bytes 786432 | tf_op jit(solution)/shard_map/all_to_all | solution.py:176
  43.5 1.9 %collective-permute-start.22 = (bf16[96,1792]{1,0:T(8,128)(2,1)S(1)}, bf16[96,1792]{1,0:T(8,128)(2,1)S(1)}, u32[]{:S(2)}, u32[]{:S(2)}) collective-permute-start(bf16[96,1792]{1,0:T(8,128)(2,1)S(1)} %collective-permute-done.20.refs_2_), channel_id=1, source_target_pairs={{1,225},{33,1},{65,33},{97,65},{129,97},{161,129},{193,161},{225,1... | collective-permute-start | bytes 1032200 | tf_op jit(solution)/shard_map/ppermute | solution.py:63
  45.5 6.0 %shard_map.53 = (bf16[768,896]{1,0:T(8,128)(2,1)}, f32[8,128]{1,0:T(8,128)S(1)}) custom-call(s32[3]{0:T(128)S(1)} %pad_add_fusion.refs_0_, bf16[96,1792]{1,0:T(8,128)(2,1)S(1)} %shard_map.48.refs_1_, bf16[96,1792]{1,0:T(8,128)(2,1)S(1)} %shard_map.51.refs_2_, bf16[96,1792]{1,0:T(8,128)(2,1)S(1)} %collective-permute-done.2.refs_1_.refs_3_, ...), custom_call_target="tpu_custom_call" | custom-call | flops 1541406720 | bytes 5000000 | tf_op jit(solution)/shard_map/pallas_call | solution.py:34
  51.4 6.3 %collective-permute-done.19.refs_0_ = bf16[96,1792]{1,0:T(8,128)(2,1)S(1)} collective-permute-done((bf16[96,1792]{1,0:T(8,128)(2,1)S(1)}, bf16[96,1792]{1,0:T(8,128)(2,1)S(1)}, u32[]{:S(2)}, u32[]{:S(2)}) %collective-permute-start.19) | collective-permute-done | bytes 344096 | tf_op jit(solution)/shard_map/ppermute | solution.py:63
  58.5 1.4 %collective-permute-start.10 = (bf16[96,256]{1,0:T(8,128)(2,1)S(1)}, bf16[96,256]{1,0:T(8,128)(2,1)S(1)}, u32[]{:S(2)}, u32[]{:S(2)}) collective-permute-start(bf16[96,256]{1,0:T(8,128)(2,1)S(1)} %shard_map.54), channel_id=1, source_target_pairs={{0,16},{16,0},{1,17},{17,1},{2,18},{18,2},{3,19},{19,3},{4,20},{20... | collective-permute-start | bytes 147464 | tf_op jit(solution)/shard_map/ppermute | solution.py:18
  59.9 3.1 %collective-permute-done.10.refs_8_ = bf16[96,256]{1,0:T(8,128)(2,1)S(1)} collective-permute-done((bf16[96,256]{1,0:T(8,128)(2,1)S(1)}, bf16[96,256]{1,0:T(8,128)(2,1)S(1)}, u32[]{:S(2)}, u32[]{:S(2)}) %collective-permute-start.10) | collective-permute-done | bytes 49184 | tf_op jit(solution)/shard_map/ppermute | solution.py:18
  63.1 5.4 %shard_map.56 = (bf16[768,896]{1,0:T(8,128)(2,1)}, f32[8,128]{1,0:T(8,128)}) custom-call(s32[3]{0:T(128)S(1)} %pad_add_fusion.refs_0_, bf16[96,1792]{1,0:T(8,128)(2,1)S(1)} %shard_map.55.refs_1_, bf16[96,1792]{1,0:T(8,128)(2,1)S(1)} %collective-permute-done.20.refs_2_, ...), custom_call_target="tpu_custom_call", output_to_operand_aliasing={{0}: (7, {})} | custom-call | flops 924844032 | bytes 5000000 | tf_op jit(solution)/shard_map/pallas_call | solution.py:34
  68.5 4.6 %all-to-all-start.2 = ((bf16[8,96,896]{2,1,0:T(8,128)(2,1)}), bf16[8,96,896]{2,1,0:T(8,128)(2,1)S(1)}, u32[]{:S(2)}, u32[]{:S(2)}) async-start(bf16[8,96,896]{2,1,0:T(8,128)(2,1)} %bitcast.37), calls=%async_computation.2 | async-start | bytes 2752512 | tf_op jit(solution)/shard_map/all_to_all | solution.py:176
  73.2 3.6 %collective-permute-start.14 = (bf16[192,256]{1,0:T(8,128)(2,1)S(1)}, bf16[192,256]{1,0:T(8,128)(2,1)S(1)}, u32[]{:S(2)}, u32[]{:S(2)}) collective-permute-start(bf16[192,256]{1,0:T(8,128)(2,1)S(1)} %pad_maximum_fusion), channel_id=1, source_target_pairs={{0,64},{32,96},{64,128},{96,160},{128,192},{160,224},{192,0},{224,... | collective-permute-start | bytes 294920 | tf_op jit(solution)/shard_map/ppermute | solution.py:14
  80.4 6.1 %all-to-all-done.2 = bf16[8,96,896]{2,1,0:T(8,128)(2,1)S(1)} async-done(((bf16[8,96,896]{2,1,0:T(8,128)(2,1)}), bf16[8,96,896]{2,1,0:T(8,128)(2,1)S(1)}, u32[]{:S(2)}, u32[]{:S(2)}) %all-to-all-start.2) | async-done | bytes 1376288 | tf_op jit(solution)/shard_map/all_to_all | solution.py:176
  87.7 8.1 %all-to-all-start.3 = ((bf16[8,96,896]{2,1,0:T(8,128)(2,1)}), bf16[8,96,896]{2,1,0:T(8,128)(2,1)S(1)}, u32[]{:S(2)}, u32[]{:S(2)}) async-start(bf16[8,96,896]{2,1,0:T(8,128)(2,1)} %bitcast.18), calls=%async_computation.3 | async-start | bytes 2752512 | tf_op jit(solution)/shard_map/all_to_all | solution.py:176
  95.8 2.7 %collective-permute-start.15 = (bf16[192,256]{1,0:T(8,128)(2,1)S(1)}, bf16[192,256]{1,0:T(8,128)(2,1)S(1)}, u32[]{:S(2)}, u32[]{:S(2)}) collective-permute-start(bf16[192,256]{1,0:T(8,128)(2,1)S(1)} %collective-permute-done.14.refs_3_), channel_id=1, source_target_pairs={{0,32},{32,64},{64,96},{96,128},{128,160},{160,192},{192,224},{224... | collective-permute-start | bytes 294920 | tf_op jit(solution)/shard_map/ppermute | solution.py:14
  98.5 2.4 %collective-permute-start.18 = (bf16[192,128]{1,0:T(8,128)(2,1)S(1)}, bf16[192,128]{1,0:T(8,128)(2,1)S(1)}, u32[]{:S(2)}, u32[]{:S(2)}) collective-permute-start(bf16[192,128]{1,0:T(8,128)(2,1)S(1)} %slice.9), channel_id=1, source_target_pairs={{0,192},{32,224},{64,0},{96,32},{128,64},{160,96},{192,128},{224,1... | collective-permute-start | bytes 147464 | tf_op jit(solution)/shard_map/ppermute | solution.py:14
  100.8 1.8 %collective-permute-done.17.refs_3_ = bf16[192,128]{1,0:T(8,128)(2,1)S(1)} collective-permute-done((bf16[192,128]{1,0:T(8,128)(2,1)S(1)}, bf16[192,128]{1,0:T(8,128)(2,1)S(1)}, u32[]{:S(2)}, u32[]{:S(2)}) %collective-permute-start.17) | collective-permute-done | bytes 49184 | tf_op jit(solution)/shard_map/ppermute | solution.py:14
  103.9 10.3 %all-to-all-done.3 = bf16[8,96,896]{2,1,0:T(8,128)(2,1)S(1)} async-done(((bf16[8,96,896]{2,1,0:T(8,128)(2,1)}), bf16[8,96,896]{2,1,0:T(8,128)(2,1)S(1)}, u32[]{:S(2)}, u32[]{:S(2)}) %all-to-all-start.3) | async-done | bytes 1376288 | tf_op jit(solution)/shard_map/all_to_all | solution.py:176
  115.1 2.8 %collective-permute-done.23 = bf16[768,896]{1,0:T(8,128)(2,1)S(1)} collective-permute-done((bf16[768,896]{1,0:T(8,128)(2,1)S(1)}, bf16[768,896]{1,0:T(8,128)(2,1)S(1)}, u32[]{:S(2)}, u32[]{:S(2)}) %collective-permute-start.23) | collective-permute-done | bytes 1376288 | tf_op jit(solution)/shard_map/ppermute | solution.py:18
  117.8 2.9 %shard_map.59 = f32[256,896]{1,0:T(8,128)} custom-call(s32[3]{0:T(128)S(1)} %pad_add_fusion.refs_0_, bf16[2,2,48,256]{3,2,1,0:T(8,128)(2,1)S(1)} %bitcast.34, bf16[2,2,48,256]{3,2,1,0:T(8,128)(2,1)S(1)} %bitcast.30, bf16[2,2,48,256]{3,2,1,0:T(8,128)(2,1)S(1)} %bitcast.28, bf16[2,2,48,256]{3,2,1,0:T(8,128)(2,1)S(1)} %bitcast.32, ...), custom_call_target="tpu_custom_call" | custom-call | flops 703000000 | bytes 5000000 | tf_op jit(solution)/shard_map/pallas_call | solution.py:34
  (56 shorter events, 17.0 us)
Async XLA Ops:
  0.0 45.4 %collective-permute-start.9 = (bf16[896,896]{1,0:T(8,128)(2,1)}, bf16[896,896]{1,0:T(8,128)(2,1)}, u32[]{:S(2)}, u32[]{:S(2)}) collective-permute-start(bf16[896,896]{1,0:T(8,128)(2,1)} %refs_5_.1), channel_id=1, source_target_pairs={{0,1},{1,0},{2,3},{3,2},{4,5},{5,4},{6,7},{7,6},{8,9},{9,8},{10,11... | collective-permute-start | bytes 4816904 | tf_op jit(solution)/shard_map/ppermute | solution.py:18
  2.4 8.6 %collective-permute-start = (bf16[96,1152]{1,0:T(8,128)(2,1)S(1)}, bf16[96,1152]{1,0:T(8,128)(2,1)S(1)}, u32[]{:S(2)}, u32[]{:S(2)}) collective-permute-start(bf16[96,1152]{1,0:T(8,128)(2,1)S(1)} %shard_map.46.refs_1_), channel_id=1, source_target_pairs={{0,16},{16,0},{1,17},{17,1},{2,18},{18,2},{3,19},{19,3},{4,20},{20... | collective-permute-start | bytes 663560 | tf_op jit(solution)/shard_map/ppermute | solution.py:18
  13.3 8.9 %collective-permute-start.6 = (bf16[96,1792]{1,0:T(8,128)(2,1)S(1)}, bf16[96,1792]{1,0:T(8,128)(2,1)S(1)}, u32[]{:S(2)}, u32[]{:S(2)}) collective-permute-start(bf16[96,1792]{1,0:T(8,128)(2,1)S(1)} %shard_map.51.refs_2_), channel_id=1, source_target_pairs={{0,32},{1,225},{32,64},{33,1},{64,96},{65,33},{96,128},{97,65},{12... | collective-permute-start | bytes 1032200 | tf_op jit(solution)/shard_map/ppermute | solution.py:63
  14.4 12.4 %collective-permute-start.2 = (bf16[96,1792]{1,0:T(8,128)(2,1)S(1)}, bf16[96,1792]{1,0:T(8,128)(2,1)S(1)}, u32[]{:S(2)}, u32[]{:S(2)}) collective-permute-start(bf16[96,1792]{1,0:T(8,128)(2,1)S(1)} %shard_map.48.refs_1_), channel_id=1, source_target_pairs={{0,32},{1,225},{32,64},{33,1},{64,96},{65,33},{96,128},{97,65},{12... | collective-permute-start | bytes 1032200 | tf_op jit(solution)/shard_map/ppermute | solution.py:63
  14.5 12.3 %all-to-all-start = ((bf16[8,48,512]{2,1,0:T(8,128)(2,1)}), bf16[8,48,512]{2,1,0:T(8,128)(2,1)S(1)}, u32[]{:S(2)}, u32[]{:S(2)}) async-start(bf16[8,48,512]{2,1,0:T(8,128)(2,1)} %bitcast.3), calls=%async_computation | async-start | bytes 786432 | tf_op jit(solution)/shard_map/all_to_all | solution.py:176
  19.6 7.2 %collective-permute-start.3 = (bf16[256,256]{1,0:T(8,128)(2,1)S(1)}, bf16[256,256]{1,0:T(8,128)(2,1)S(1)}, u32[]{:S(2)}, u32[]{:S(2)}) collective-permute-start(bf16[256,256]{1,0:T(8,128)(2,1)S(1)} %copy-done), channel_id=1, source_target_pairs={{0,16},{16,0},{1,17},{17,1},{2,18},{18,2},{3,19},{19,3},{4,20},{20... | collective-permute-start | bytes 393224 | tf_op jit(solution)/shard_map/ppermute | solution.py:18
  22.2 11.1 %collective-permute-start.8 = (bf16[96,1792]{1,0:T(8,128)(2,1)S(1)}, bf16[96,1792]{1,0:T(8,128)(2,1)S(1)}, u32[]{:S(2)}, u32[]{:S(2)}) collective-permute-start(bf16[96,1792]{1,0:T(8,128)(2,1)S(1)} %collective-permute-done.6.refs_4_), channel_id=1, source_target_pairs={{0,32},{1,225},{32,64},{33,1},{64,96},{65,33},{96,128},{97,65},{12... | collective-permute-start | bytes 1032200 | tf_op jit(solution)/shard_map/ppermute | solution.py:63
  26.8 8.0 %collective-permute-start.4 = (bf16[384,512]{1,0:T(8,128)(2,1)S(1)}, bf16[384,512]{1,0:T(8,128)(2,1)S(1)}, u32[]{:S(2)}, u32[]{:S(2)}) collective-permute-start(bf16[384,512]{1,0:T(8,128)(2,1)S(1)} %shard_map.49.refs_0_), channel_id=1, source_target_pairs={{0,1},{1,0},{2,3},{3,2},{4,5},{5,4},{6,7},{7,6},{8,9},{9,8},{10,11... | collective-permute-start | bytes 1179656 | tf_op jit(solution)/shard_map/ppermute | solution.py:18
  32.5 9.6 %collective-permute-start.7 = (bf16[96,1792]{1,0:T(8,128)(2,1)S(1)}, bf16[96,1792]{1,0:T(8,128)(2,1)S(1)}, u32[]{:S(2)}, u32[]{:S(2)}) collective-permute-start(bf16[96,1792]{1,0:T(8,128)(2,1)S(1)} %collective-permute-done.2.refs_1_.refs_3_), channel_id=1, source_target_pairs={{0,32},{1,225},{32,64},{33,1},{64,96},{65,33},{96,128},{97,65},{12... | collective-permute-start | bytes 1032200 | tf_op jit(solution)/shard_map/ppermute | solution.py:63
  33.3 10.3 %collective-permute-start.20 = (bf16[96,1792]{1,0:T(8,128)(2,1)S(1)}, bf16[96,1792]{1,0:T(8,128)(2,1)S(1)}, u32[]{:S(2)}, u32[]{:S(2)}) collective-permute-start(bf16[96,1792]{1,0:T(8,128)(2,1)S(1)} %collective-permute-done.8.refs_6_), channel_id=1, source_target_pairs={{0,32},{1,225},{32,64},{33,1},{64,96},{65,33},{96,128},{97,65},{12... | collective-permute-start | bytes 1032200 | tf_op jit(solution)/shard_map/ppermute | solution.py:63
  36.0 22.5 %all-to-all-start.1 = ((bf16[8,96,256]{2,1,0:T(8,128)(2,1)}), bf16[8,96,256]{2,1,0:T(8,128)(2,1)S(1)}, u32[]{:S(2)}, u32[]{:S(2)}) async-start(bf16[8,96,256]{2,1,0:T(8,128)(2,1)} %bitcast.5), calls=%async_computation.1 | async-start | bytes 786432 | tf_op jit(solution)/shard_map/all_to_all | solution.py:176
  42.1 15.7 %collective-permute-start.19 = (bf16[96,1792]{1,0:T(8,128)(2,1)S(1)}, bf16[96,1792]{1,0:T(8,128)(2,1)S(1)}, u32[]{:S(2)}, u32[]{:S(2)}) collective-permute-start(bf16[96,1792]{1,0:T(8,128)(2,1)S(1)} %shard_map.52.refs_5_), channel_id=1, source_target_pairs={{0,32},{1,225},{32,64},{33,1},{64,96},{65,33},{96,128},{97,65},{12... | collective-permute-start | bytes 1032200 | tf_op jit(solution)/shard_map/ppermute | solution.py:63
  43.5 19.5 %collective-permute-start.22 = (bf16[96,1792]{1,0:T(8,128)(2,1)S(1)}, bf16[96,1792]{1,0:T(8,128)(2,1)S(1)}, u32[]{:S(2)}, u32[]{:S(2)}) collective-permute-start(bf16[96,1792]{1,0:T(8,128)(2,1)S(1)} %collective-permute-done.20.refs_2_), channel_id=1, source_target_pairs={{1,225},{33,1},{65,33},{97,65},{129,97},{161,129},{193,161},{225,1... | collective-permute-start | bytes 1032200 | tf_op jit(solution)/shard_map/ppermute | solution.py:63
  57.8 5.3 %collective-permute-start.21 = (bf16[96,1792]{1,0:T(8,128)(2,1)S(1)}, bf16[96,1792]{1,0:T(8,128)(2,1)S(1)}, u32[]{:S(2)}, u32[]{:S(2)}) collective-permute-start(bf16[96,1792]{1,0:T(8,128)(2,1)S(1)} %shard_map.55.refs_1_), channel_id=1, source_target_pairs={{0,32},{32,64},{64,96},{96,128},{128,160},{160,192},{192,224},{224... | collective-permute-start | bytes 1032200 | tf_op jit(solution)/shard_map/ppermute | solution.py:63
  58.5 4.5 %collective-permute-start.10 = (bf16[96,256]{1,0:T(8,128)(2,1)S(1)}, bf16[96,256]{1,0:T(8,128)(2,1)S(1)}, u32[]{:S(2)}, u32[]{:S(2)}) collective-permute-start(bf16[96,256]{1,0:T(8,128)(2,1)S(1)} %shard_map.54), channel_id=1, source_target_pairs={{0,16},{16,0},{1,17},{17,1},{2,18},{18,2},{3,19},{19,3},{4,20},{20... | collective-permute-start | bytes 147464 | tf_op jit(solution)/shard_map/ppermute | solution.py:18
  68.5 18.0 %all-to-all-start.2 = ((bf16[8,96,896]{2,1,0:T(8,128)(2,1)}), bf16[8,96,896]{2,1,0:T(8,128)(2,1)S(1)}, u32[]{:S(2)}, u32[]{:S(2)}) async-start(bf16[8,96,896]{2,1,0:T(8,128)(2,1)} %bitcast.37), calls=%async_computation.2 | async-start | bytes 2752512 | tf_op jit(solution)/shard_map/all_to_all | solution.py:176
  73.0 5.1 %collective-permute-start.11 = (bf16[192,256]{1,0:T(8,128)(2,1)S(1)}, bf16[192,256]{1,0:T(8,128)(2,1)S(1)}, u32[]{:S(2)}, u32[]{:S(2)}) collective-permute-start(bf16[192,256]{1,0:T(8,128)(2,1)S(1)} %pad_maximum_fusion), channel_id=1, source_target_pairs={{0,224},{32,0},{64,32},{96,64},{128,96},{160,128},{192,160},{224,1... | collective-permute-start | bytes 294920 | tf_op jit(solution)/shard_map/ppermute | solution.py:14
  73.1 5.8 %collective-permute-start.12 = (bf16[192,256]{1,0:T(8,128)(2,1)S(1)}, bf16[192,256]{1,0:T(8,128)(2,1)S(1)}, u32[]{:S(2)}, u32[]{:S(2)}) collective-permute-start(bf16[192,256]{1,0:T(8,128)(2,1)S(1)} %pad_maximum_fusion), channel_id=1, source_target_pairs={{0,192},{32,224},{64,0},{96,32},{128,64},{160,96},{192,128},{224,1... | collective-permute-start | bytes 294920 | tf_op jit(solution)/shard_map/ppermute | solution.py:14
  73.2 6.1 %collective-permute-start.14 = (bf16[192,256]{1,0:T(8,128)(2,1)S(1)}, bf16[192,256]{1,0:T(8,128)(2,1)S(1)}, u32[]{:S(2)}, u32[]{:S(2)}) collective-permute-start(bf16[192,256]{1,0:T(8,128)(2,1)S(1)} %pad_maximum_fusion), channel_id=1, source_target_pairs={{0,64},{32,96},{64,128},{96,160},{128,192},{160,224},{192,0},{224,... | collective-permute-start | bytes 294920 | tf_op jit(solution)/shard_map/ppermute | solution.py:14
  87.7 26.5 %all-to-all-start.3 = ((bf16[8,96,896]{2,1,0:T(8,128)(2,1)}), bf16[8,96,896]{2,1,0:T(8,128)(2,1)S(1)}, u32[]{:S(2)}, u32[]{:S(2)}) async-start(bf16[8,96,896]{2,1,0:T(8,128)(2,1)} %bitcast.18), calls=%async_computation.3 | async-start | bytes 2752512 | tf_op jit(solution)/shard_map/all_to_all | solution.py:176
  95.8 8.1 %collective-permute-start.13 = (bf16[192,256]{1,0:T(8,128)(2,1)S(1)}, bf16[192,256]{1,0:T(8,128)(2,1)S(1)}, u32[]{:S(2)}, u32[]{:S(2)}) collective-permute-start(bf16[192,256]{1,0:T(8,128)(2,1)S(1)} %collective-permute-done.12.refs_4_), channel_id=1, source_target_pairs={{0,224},{32,0},{64,32},{96,64},{128,96},{160,128},{192,160},{224,1... | collective-permute-start | bytes 294920 | tf_op jit(solution)/shard_map/ppermute | solution.py:14
  95.8 8.1 %collective-permute-start.15 = (bf16[192,256]{1,0:T(8,128)(2,1)S(1)}, bf16[192,256]{1,0:T(8,128)(2,1)S(1)}, u32[]{:S(2)}, u32[]{:S(2)}) collective-permute-start(bf16[192,256]{1,0:T(8,128)(2,1)S(1)} %collective-permute-done.14.refs_3_), channel_id=1, source_target_pairs={{0,32},{32,64},{64,96},{96,128},{128,160},{160,192},{192,224},{224... | collective-permute-start | bytes 294920 | tf_op jit(solution)/shard_map/ppermute | solution.py:14
  98.5 4.1 %collective-permute-start.17 = (bf16[192,128]{1,0:T(8,128)(2,1)S(1)}, bf16[192,128]{1,0:T(8,128)(2,1)S(1)}, u32[]{:S(2)}, u32[]{:S(2)}) collective-permute-start(bf16[192,128]{1,0:T(8,128)(2,1)S(1)} %slice.8), channel_id=1, source_target_pairs={{0,64},{32,96},{64,128},{96,160},{128,192},{160,224},{192,0},{224,... | collective-permute-start | bytes 147464 | tf_op jit(solution)/shard_map/ppermute | solution.py:14
  98.5 5.4 %collective-permute-start.18 = (bf16[192,128]{1,0:T(8,128)(2,1)S(1)}, bf16[192,128]{1,0:T(8,128)(2,1)S(1)}, u32[]{:S(2)}, u32[]{:S(2)}) collective-permute-start(bf16[192,128]{1,0:T(8,128)(2,1)S(1)} %slice.9), channel_id=1, source_target_pairs={{0,192},{32,224},{64,0},{96,32},{128,64},{160,96},{192,128},{224,1... | collective-permute-start | bytes 147464 | tf_op jit(solution)/shard_map/ppermute | solution.py:14
  (7 other events, 27.0 us)
